TPU v7x, 256 devices: a whole 4x4x8 slice. The times are simulated.
256 devices in a mesh: replica: 8 (over z_lo, x), fsdp: 32 (over y, z_hi, core).
Axes of the slice: x: 4, y: 4, z: 8 (z_hi: 4, z_lo: 2; z = z_hi * 2 + z_lo), core: 2. Of those that a mesh axis runs over, the one named last changes fastest.
Arguments:
- hidden_in: bfloat16 [8, 12288, 8192], P('replica', 'fsdp'), may hold values from -6 to 6
- value_weight: bfloat16 [8, 8192, 512], P('replica', 'fsdp'), may hold values from -0.0625 to 0.0625
- grad_out: bfloat16 [8, 12288, 512], P('replica', 'fsdp'), may hold values from -0.0546875 to 0.0546875
- local_fragment: float32 [8, 8388608], P('replica', 'fsdp'), may hold values from -6 to 6
- global_fragment: float32 [8388608], P('fsdp'), may hold values from -6 to 6
- momentum: float32 [8388608], P('fsdp'), may hold values from -3 to 3
- residual: float32 [8, 8388608], P('replica', 'fsdp'), may hold values from -3 to 3
Outputs:
- values: bfloat16 [8, 12288, 512], P('replica', 'fsdp')
- weight_grad: float32 [8, 8192, 512], P('replica', 'fsdp')
- mixed_fragment: float32 [8, 8388608], P('replica', 'fsdp')
- new_momentum: float32 [8388608], P('fsdp')
All inputs are finite; a program needn't handle non-finite values.
Results may differ from a plain program's by a relative error of at most 0.015.
Values may be sent and summed in bfloat16 or wider, within the bound.
No kernel may reach another device: no remote copies, remote signals or barrier semaphores. Data moves between devices by JAX's collectives and lax.ppermute only.
A program may use at most 128 MiB of HBM per device.

v0:
```python
import jax
import jax.numpy as jnp
from jax import lax
from jax.sharding import PartitionSpec as P

BLOCK = 128


outer_rate = 0.7
outer_momentum = 0.9
mix_weight = 0.5


def per_device(
    hidden_in, value_weight, grad_out, local_fragment, global_fragment, momentum, residual
):
    tokens = hidden_in[0]
    weight = value_weight[0]
    cotangent = grad_out[0]
    columns = tokens
    projected = jnp.dot(
        columns,
        lax.all_gather(weight, "fsdp", axis=0, tiled=True),
        preferred_element_type=jnp.float32,
    )
    values = projected.astype(jnp.bfloat16)[None]
    local_row = local_fragment[0]
    nudged = global_fragment - local_row + residual[0]
    blocks = nudged.reshape(-1, BLOCK)
    block_scale = lax.optimization_barrier(
        (jnp.max(jnp.abs(blocks), axis=1) + 1e-06).astype(jnp.bfloat16)
    )
    block_codes = lax.optimization_barrier(
        (blocks / block_scale.astype(jnp.float32)[:, None]).astype(jnp.bfloat16)
    )
    replicas = lax.axis_size("replica")
    decoded = block_codes.astype(jnp.float32) * block_scale.astype(jnp.float32)[:, None]
    summed_all = lax.psum(decoded.astype(jnp.bfloat16), "replica").astype(jnp.float32)
    average = (summed_all / replicas).reshape(-1)
    new_momentum = outer_momentum * momentum + average
    new_global = global_fragment - outer_rate * (average + outer_momentum * new_momentum)
    mixed_fragment = mix_weight * local_row + (1.0 - mix_weight) * new_global
    columns = tokens
    grad_rows = lax.psum_scatter(
        lax.dot_general(
            columns, cotangent, (((0,), (0,)), ((), ())), preferred_element_type=jnp.float32
        ),
        "fsdp",
        scatter_dimension=0,
        tiled=True,
    )
    return (values, grad_rows[None], mixed_fragment[None], new_momentum)


def solution(mesh):
    return jax.shard_map(
        per_device,
        mesh=mesh,
        in_specs=(
            P("replica", "fsdp", None),
            P("replica", "fsdp", None),
            P("replica", "fsdp", None),
            P("replica", "fsdp"),
            P("fsdp"),
            P("fsdp"),
            P("replica", "fsdp"),
        ),
        out_specs=(
            P("replica", "fsdp", None),
            P("replica", "fsdp", None),
            P("replica", "fsdp"),
            P("fsdp"),
        ),
        check_vma=False,
    )
```

profile of v0, /device:TPU:5, one launch (start us, length us, event | category | flops | bytes accessed | tf_op | source)
XLA Modules:
  0.0 276.0 jit_solution(1331536064113307561)
XLA Ops:
  8.0 0.0 copy-start
  8.0 0.0 all-reduce.2.cloned.1.call-start
  8.1 2.2 fusion.19
  10.3 2.2 fusion.20
  12.5 1.1 multiply_convert_fusion
  13.7 0.0 all-reduce.2.cloned.1.call-update
  13.7 0.0 all-gather.3.cloned.1.call-start
  13.8 0.5 all-gather.3.cloned.1.call-update
  14.3 0.0 reduce-scatter.2.cloned.1.call-start
  14.3 0.0 copy-done
  14.3 11.1 %fusion.2 = f32[8192,512]{1,0:T(8,128)} fusion(bf16[1,384,8192]{2,1,0:T(8,128)(2,1)} %param.7, bf16[1,384,512]{2,1,0:T(8,128)(2,1)S(1)} %copy-done), kind=kOutput, calls=%fused_computation.2 | convolution fusion | flops 3221225472 | bytes 23461888 | tf_op jit(solution)/shard_map/dot_general | solution.py:45
  25.4 0.0 copy-start.1
  25.4 0.0 copy-start.2
  25.4 0.0 copy-start.3
  25.4 0.0 reduce-scatter.2.cloned.1.call-update
  25.5 82.8 %all-reduce.2.cloned.1.call-done = bf16[2048,128]{1,0:T(8,128)(2,1)} async-done(((bf16[2048,128]{1,0:T(8,128)(2,1)}), bf16[2048,128]{1,0:T(8,128)(2,1)}) %all-reduce.2.cloned.1.call-update) | async-done | bytes 524304 | tf_op jit(solution)/shard_map/psum | solution.py:38
  108.3 0.0 copy-done.1
  108.3 0.0 copy-done.2
  108.3 0.0 copy-done.3
  108.3 2.7 fusion.18
  111.0 0.0 all-gather.3.cloned.1.call-done
  111.0 9.9 %fusion.10 = bf16[1,384,512]{2,1,0:T(8,128)(2,1)} fusion(bf16[1,8192,512]{2,1,0:T(8,128)(2,1)} %all-gather.3.cloned.1.call-done, bf16[1,384,8192]{2,1,0:T(8,128)(2,1)} %param.7), kind=kOutput, calls=%fused_computation.6 | convolution fusion | flops 3221422080 | bytes 15073280 | tf_op jit(solution)/shard_map/dot_general | solution.py:21
  120.8 147.7 %reduce-scatter.2.cloned.1.call-done = f32[256,512]{1,0:T(8,128)} async-done(((f32[8192,512]{1,0:T(8,128)}), f32[256,512]{1,0:T(8,128)}) %reduce-scatter.2.cloned.1.call-update) | async-done | bytes 524304 | tf_op jit(solution)/shard_map/reduce_scatter | solution.py:44
  (2 shorter events, 0.0 us)
Async XLA Ops:
  8.0 6.3 %copy-start = (bf16[1,384,512]{2,1,0:T(8,128)(2,1)S(1)}, bf16[1,384,512]{2,1,0:T(8,128)(2,1)}, u32[]{:S(2)}) copy-start(bf16[1,384,512]{2,1,0:T(8,128)(2,1)} %param.9) | copy-start | bytes 1179652
  8.0 100.2 %all-reduce.2.cloned.1.call-start = ((), (), s32[]{:S(2)}) async-start(), calls=%async_computation.2 | async-start | bytes 1048576 | tf_op jit(solution)/shard_map/psum | solution.py:38
  13.7 97.3 %all-gather.3.cloned.1.call-start = ((), (), s32[]{:S(2)}) async-start(), calls=%async_computation.3 | async-start | bytes 8650752 | tf_op jit(solution)/shard_map/all_gather | solution.py:23
  14.3 254.3 %reduce-scatter.2.cloned.1.call-start = ((), (), s32[]{:S(2)}) async-start(), calls=%async_computation.1 | async-start | bytes 17301504 | tf_op jit(solution)/shard_map/reduce_scatter | solution.py:44
  25.4 82.8 %copy-start.1 = (f32[1,262144]{1,0:T(1,128)S(1)}, f32[1,262144]{1,0:T(1,128)}, u32[]{:S(2)}) copy-start(f32[1,262144]{1,0:T(1,128)} %param.10) | copy-start | bytes 3145732
  25.4 82.8 %copy-start.2 = (f32[262144]{0:T(1024)S(1)}, f32[262144]{0:T(1024)}, u32[]{:S(2)}) copy-start(f32[262144]{0:T(1024)} %param.11) | copy-start | bytes 3145732
  25.4 82.8 %copy-start.3 = (f32[262144]{0:T(1024)S(1)}, f32[262144]{0:T(1024)}, u32[]{:S(2)}) copy-start(f32[262144]{0:T(1024)} %param.12) | copy-start | bytes 3145732
Sparse Core Ops, SparseCore 0:
  13.8 94.3 all-reduce.1
Sparse Core Ops, SparseCore 1:
  16.7 81.5 all-gather.2
  102.9 165.5 reduce-scatter.1
where the time goes:
time: 278 us; the launch traced here: 276 us
  waiting for transfers between devices  231 us (83%)
  matrix products  20.9 us (8%)
  between operations  15.5 us (6%)
  other arithmetic  8.29 us (3%)
    reduce_scatter x1, waiting for transfers between devices, per_device(): lax.psum_scatter(lax.dot_general(columns, cotangent, (((0,), (0,)), ((),...  148 us
    psum x1, waiting for transfers between devices, per_device(): lax.psum(decoded.astype(jnp.bfloat16), 'replica').astype(jnp.float32)  82.8 us
    dot_general x1, matrix products, per_device(): lax.dot_general(columns, cotangent, (((0,), (0,)), ((), ())), preferred_e...  11.1 us
    dot_general x1, matrix products, per_device(): jnp.dot(columns, lax.all_gather(weight, 'fsdp', axis=0, tiled=True), pref...  9.85 us
  transfers between devices with their start and end apart: 3, of which 2 were waited for; matrix products, arithmetic and copies ran while one was open for 9% of the time, Pallas kernels for 0%

commit v1 on v0

v1 whole, which is shorter than its diff:
```python
import functools

import jax
import jax.numpy as jnp
from jax import lax
from jax.experimental import pallas as pl
from jax.experimental.pallas import tpu as pltpu
from jax.sharding import Mesh, PartitionSpec as P

BLOCK = 128


outer_rate = 0.7
outer_momentum = 0.9
mix_weight = 0.5

RING = 4
ROWS = 256


def shift(v, axis, k):
    n = lax.axis_size(axis)
    return lax.ppermute(v, axis, [(i, (i + k) % n) for i in range(n)])


def params(mib=32):
    return pltpu.CompilerParams(vmem_limit_bytes=mib << 20)


def pick_kernel(_, h_ref, o_ref):
    o_ref[...] = h_ref[...]


def other_columns(tokens, core):
    t, d = tokens.shape
    n = d // (2 * ROWS)
    return pl.pallas_call(
        pick_kernel,
        grid_spec=pltpu.PrefetchScalarGridSpec(
            num_scalar_prefetch=1,
            grid=(n,),
            in_specs=[pl.BlockSpec((t, ROWS), lambda i, s: (0, 2 * i + 1 - s[0]))],
            out_specs=pl.BlockSpec((t, ROWS), lambda i, s: (0, i)),
        ),
        out_shape=jax.ShapeDtypeStruct((t, d // 2), tokens.dtype),
        compiler_params=params(),
        cost_estimate=pl.CostEstimate(flops=0, bytes_accessed=2 * t * d, transcendentals=0),
    )(core[None], tokens)


TN = (((0,), (0,)), ((), ()))


def grad_kernel(n, naccs, _, h_ref, hr_ref, g_ref, gp_ref, *refs):
    accs, outs = refs[: 2 * naccs], refs[2 * naccs :]
    i = pl.program_id(0)
    total = lax.dot_general(h_ref[...], g_ref[...], TN, preferred_element_type=jnp.float32)
    total += lax.dot_general(hr_ref[...], gp_ref[...], TN, preferred_element_type=jnp.float32)
    for half in range(2):

        @pl.when((i < n // 2) if half == 0 else (i >= n // 2))
        def _():
            s = total
            for a in range(naccs):
                s = s + accs[2 * a + half][0].astype(jnp.float32)
            outs[half][0] = s.astype(outs[half].dtype)


def grad_blocks(core, blocks, tokens, theirs, cot, cot_theirs, accs, dtype):
    t = tokens.shape[0]
    k = cot.shape[1]
    n = blocks.shape[0]
    h = n // 2
    first = lambda i, s: (jnp.minimum(i, h - 1), 0, 0)
    second = lambda i, s: (jnp.maximum(i - h, 0), 0, 0)
    unit = (1, ROWS, k)
    return pl.pallas_call(
        functools.partial(grad_kernel, n, len(accs)),
        grid_spec=pltpu.PrefetchScalarGridSpec(
            num_scalar_prefetch=1,
            grid=(n,),
            in_specs=[
                pl.BlockSpec((t, ROWS), lambda i, s: (0, 2 * s[i + 1] + s[0])),
                pl.BlockSpec((t, ROWS), lambda i, s: (0, s[i + 1])),
                pl.BlockSpec((t, k), lambda i, s: (0, 0)),
                pl.BlockSpec((t, k), lambda i, s: (0, 0)),
            ]
            + [pl.BlockSpec(unit, first), pl.BlockSpec(unit, second)] * len(accs),
            out_specs=[pl.BlockSpec(unit, first), pl.BlockSpec(unit, second)],
        ),
        out_shape=[jax.ShapeDtypeStruct((h, ROWS, k), dtype)] * 2,
        compiler_params=params(),
        cost_estimate=pl.CostEstimate(
            flops=4 * n * ROWS * t * k, bytes_accessed=n * ROWS * (4 * t + 4 * k), transcendentals=0
        ),
    )(
        jnp.concatenate([core[None], blocks]),
        tokens,
        theirs,
        cot,
        cot_theirs,
        *[a for pair in accs for a in pair],
    )


def values_kernel(n, has_acc, _, *refs):
    pieces, h, hr = refs[:n], refs[n : 2 * n], refs[2 * n : 3 * n]
    outs = refs[-2:]
    for j, blocks in enumerate((h, hr)):
        total = refs[3 * n + j][...] if has_acc else None
        for piece, block in zip(pieces, blocks):
            part = jnp.dot(block[...], piece[...], preferred_element_type=jnp.float32)
            total = part if total is None else total + part
        outs[j][...] = total


def values_part(core, pieces, tokens, theirs, acc):
    t = tokens.shape[0]
    k = pieces[0][0].shape[1]
    n = len(pieces)
    specs, ours, other = [], [], []
    for j, (w, _, half) in enumerate(pieces):
        r = w.shape[0]
        f = ROWS // r
        half = half or 0
        specs.append(pl.BlockSpec((r, k), lambda i, s: (0, 0)))
        ours.append(
            pl.BlockSpec((t, r), lambda i, s, j=j, f=f, half=half: (0, (2 * s[j + 1] + s[0]) * f + half))
        )
        other.append(pl.BlockSpec((t, r), lambda i, s, j=j, f=f, half=half: (0, s[j + 1] * f + half)))
    whole = pl.BlockSpec((t, k), lambda i, s: (0, 0))
    rows = sum(w.shape[0] for w, _, _ in pieces)
    acc = list(acc or ())
    return pl.pallas_call(
        functools.partial(values_kernel, n, bool(acc)),
        grid_spec=pltpu.PrefetchScalarGridSpec(
            num_scalar_prefetch=1,
            grid=(1,),
            in_specs=specs + ours + other + [whole] * len(acc),
            out_specs=[whole, whole],
        ),
        out_shape=[jax.ShapeDtypeStruct((t, k), jnp.float32)] * 2,
        compiler_params=params(48),
        cost_estimate=pl.CostEstimate(
            flops=4 * t * rows * k, bytes_accessed=4 * t * rows + 2 * rows * k, transcendentals=0
        ),
    )(
        jnp.stack([core] + [b for _, b, _ in pieces]),
        *[w for w, _, _ in pieces],
        *[tokens] * n,
        *[theirs] * n,
        *acc,
    )


def per_device(
    hidden_in, value_weight, grad_out, local_fragment, global_fragment, momentum, residual
):
    tokens = hidden_in[0]
    weight = value_weight[0]
    cot = grad_out[0]
    x, y, zh, core = (lax.axis_index(a) for a in ("x", "y", "zh", "core"))

    def block(dy, dz):
        return lax.rem(y + dy, RING) * RING + lax.rem(zh + dz, RING)

    cot_theirs = shift(cot, "core", 1)
    theirs = shift(other_columns(tokens, core), "core", 1)

    hw = ROWS // 2

    def spread(v, axis):
        h = v.shape[0] // 2
        prev, nxt = shift(v, axis, 1), shift(v, axis, -1)
        return prev, nxt, shift(prev[:h], axis, 1), shift(nxt[h:], axis, -1)

    z3, z1, z2a, z2b = spread(weight, "zh")
    groups = [
        (weight, [0]),
        (jnp.concatenate([z1, z3]), [1, 3]),
        (jnp.concatenate([z2a, z2b]), [2]),
    ]
    near, mid, far = [], [], []
    for v, zs in groups:
        prev, nxt, fa, fb = spread(v, "y")
        for j, dz in enumerate(zs):
            cut = slice(j * ROWS, (j + 1) * ROWS)
            near.append((v[cut], block(0, dz), None))
            mid.append((prev[cut], block(3, dz), None))
            mid.append((nxt[cut], block(1, dz), None))
        if len(zs) == 1:
            far += [(fa, block(2, zs[0]), 0), (fb, block(2, zs[0]), 1)]
        else:
            far += [(fa, block(2, zs[0]), None), (fb, block(2, zs[1]), None)]

    local_row = local_fragment[0]
    nudged = global_fragment - local_row + residual[0]
    blocks = nudged.reshape(-1, BLOCK)
    block_scale = lax.optimization_barrier(
        (jnp.max(jnp.abs(blocks), axis=1) + 1e-06).astype(jnp.bfloat16)
    )
    block_codes = lax.optimization_barrier(
        (blocks / block_scale.astype(jnp.float32)[:, None]).astype(jnp.bfloat16)
    )
    decoded = block_codes.astype(jnp.float32) * block_scale.astype(jnp.float32)[:, None]
    decoded = decoded.astype(jnp.bfloat16)
    part = decoded.shape[0] // RING

    def chunk(k):
        return lax.dynamic_slice_in_dim(decoded, lax.rem(x + k, RING) * part, part)

    parts = [chunk(0)] + [shift(chunk(k), "x", k) for k in (1, 2, 3)]
    over_x = sum(v.astype(jnp.float32) for v in parts).astype(jnp.bfloat16)
    both = over_x.astype(jnp.float32) + shift(over_x, "zl", 1).astype(jnp.float32)
    mine = both.astype(jnp.bfloat16)
    ordered = jnp.concatenate([mine] + [shift(mine, "x", -k) for k in (1, 2, 3)])
    ordered = jnp.concatenate([ordered, ordered])
    summed_all = lax.dynamic_slice_in_dim(
        ordered, lax.rem(RING - x, RING) * part, RING * part
    ).astype(jnp.float32)
    replicas = lax.axis_size("x") * lax.axis_size("zl")
    average = (summed_all / replicas).reshape(-1)
    new_momentum = outer_momentum * momentum + average
    new_global = global_fragment - outer_rate * (average + outer_momentum * new_momentum)
    mixed_fragment = mix_weight * local_row + (1.0 - mix_weight) * new_global

    def grads(where, accs, dtype):
        return grad_blocks(
            core, jnp.stack([block(*w) for w in where]), tokens, theirs, cot, cot_theirs, accs, dtype
        )

    bf = jnp.bfloat16
    far_a, far_b = grads([(2, 0), (2, 1), (2, 2), (2, 3)], [], bf)
    in_a, in_b = shift(far_a, "y", 1), shift(far_b, "y", -1)
    dir_b, dir_a = grads([(1, 2), (1, 3), (3, 0), (3, 1)], [], bf)
    got_b, got_a = shift(dir_b, "y", 1), shift(dir_a, "y", -1)
    mer_a, mer_b = grads([(1, 0), (1, 1), (3, 2), (3, 3)], [(in_a, in_b)], bf)
    sum_a, sum_b = shift(mer_a, "y", 1), shift(mer_b, "y", -1)
    s01, s23 = grads(
        [(0, 0), (0, 1), (0, 2), (0, 3)], [(got_a, got_b), (sum_a, sum_b)], jnp.float32
    )
    s0, s1, s2, s3 = s01[0], s01[1], s23[0], s23[1]
    in_a, in_b = shift(s2[:hw].astype(bf), "zh", 1), shift(s2[hw:].astype(bf), "zh", -1)
    got_b, got_a = shift(s1[hw:].astype(bf), "zh", 1), shift(s3[:hw].astype(bf), "zh", -1)
    f32 = jnp.float32
    sum_a = shift((s1[:hw] + in_a.astype(f32)).astype(bf), "zh", 1)
    sum_b = shift((s3[hw:] + in_b.astype(f32)).astype(bf), "zh", -1)
    top = s0[:hw] + got_a.astype(f32) + sum_a.astype(f32)
    bottom = s0[hw:] + got_b.astype(f32) + sum_b.astype(f32)
    grad_rows = jnp.concatenate([top, bottom])

    acc = values_part(core, near, tokens, theirs, None)
    acc = values_part(core, mid, tokens, theirs, acc)
    ours, other = values_part(core, far, tokens, theirs, acc)
    values = (ours + shift(other, "core", 1)).astype(bf)

    return (values[None], grad_rows[None], mixed_fragment[None], new_momentum)


def solution(mesh):
    whole = Mesh(mesh.devices.reshape(2, 4, 4, 4, 2), ("zl", "x", "y", "zh", "core"))
    replica, fsdp = ("zl", "x"), ("y", "zh", "core")
    return jax.shard_map(
        per_device,
        mesh=whole,
        in_specs=(
            P(replica, fsdp, None),
            P(replica, fsdp, None),
            P(replica, fsdp, None),
            P(replica, fsdp),
            P(fsdp),
            P(fsdp),
            P(replica, fsdp),
        ),
        out_specs=(
            P(replica, fsdp, None),
            P(replica, fsdp, None),
            P(replica, fsdp),
            P(fsdp),
        ),
        check_vma=False,
    )
```

time: 278 us -> 168 us (0.60)
  the two profiles are of different devices: /device:TPU:5 before, /device:TPU:6 now
where the time goes in v1:
time: 168 us
  starting transfers between devices  56.2 us (33%)
  waiting for transfers between devices  51.9 us (31%)
  Pallas kernels  32.9 us (20%)
  local copies, waits for them, and re-layouts  14.4 us (9%)
  other arithmetic  11.2 us (7%)
    ppermute x38, starting transfers between devices, shift(): return lax.ppermute(v, axis, [(i, (i + k) % n) for i in range(n)])  56.2 us
    ppermute x38, waiting for transfers between devices, shift(): return lax.ppermute(v, axis, [(i, (i + k) % n) for i in range(n)])  51.9 us
    pallas_call x4, Pallas kernels, grad_blocks(): pl.pallas_call(functools.partial(grad_kernel, n, len(accs)), grid_spec=pl...  15 us
    pallas_call x3, Pallas kernels, values_part(): pl.pallas_call(functools.partial(values_kernel, n, bool(acc)), grid_spec=...  11.8 us
    unnamed x48, local copies, waits for them, and re-layouts  7.52 us
    pallas_call x1, Pallas kernels, other_columns(): pl.pallas_call(pick_kernel, grid_spec=pltpu.PrefetchScalarGridSpec(num_sc...  6.09 us
  transfers between devices with their start and end apart: 38, of which 11 were waited for; matrix products, arithmetic and copies ran while one was open for 11% of the time, Pallas kernels for 16%

profile of v1, /device:TPU:6, one launch (start us, length us, event | category | flops | bytes accessed | tf_op | source)
XLA Modules:
  0.0 167.7 jit_solution(11049796114487829678)
XLA Ops:
  0.6 2.8 %copy-done = bf16[1,384,8192]{2,1,0:T(8,128)(2,1)S(1)} copy-done((bf16[1,384,8192]{2,1,0:T(8,128)(2,1)S(1)}, bf16[1,384,8192]{2,1,0:T(8,128)(2,1)}, u32[]{:S(2)}) %copy-start) | copy-done | bytes 6291480
  3.4 6.1 %shard_map.102 = bf16[384,4096]{1,0:T(8,128)(2,1)} custom-call(s32[1]{0:T(128)} %bitcast._, bf16[384,8192]{1,0:T(8,128)(2,1)S(1)} %bitcast.88), custom_call_target="tpu_custom_call" | custom-call | bytes 6291456 | tf_op jit(solution)/shard_map/pallas_call | solution.py:37
  9.9 3.0 %fusion.5 = bf16[2048,128]{1,0:T(8,128)(2,1)} fusion(f32[2048]{0:T(1024)S(1)} %convert_element_type.100, f32[262144]{0:T(1024)} %bitcast.108, f32[262144]{0:T(1024)} %param.11, f32[262144]{0:T(1024)} %bitcast.105), kind=kLoop, calls=%fused_computation.9 | loop fusion | flops 1048576 | bytes 3678208 | tf_op jit(solution)/shard_map/convert_element_type | solution.py:203
  16.7 2.8 %collective-permute-start.32 = (bf16[512,128]{1,0:T(8,128)(2,1)}, bf16[512,128]{1,0:T(8,128)(2,1)}, u32[]{:S(2)}, u32[]{:S(2)}) collective-permute-start(bf16[512,128]{1,0:T(8,128)(2,1)} %get-tuple-element.40), channel_id=1, source_target_pairs={{0,64},{32,96},{64,0},{96,32},{1,65},{33,97},{65,1},{97,33},{2,66}... | collective-permute-start | bytes 393224 | tf_op jit(solution)/shard_map/ppermute | solution.py:23
  19.9 6.3 %collective-permute-start.4 = (bf16[256,512]{1,0:T(8,128)(2,1)}, bf16[256,512]{1,0:T(8,128)(2,1)}, u32[]{:S(2)}, u32[]{:S(2)}) collective-permute-start(bf16[256,512]{1,0:T(8,128)(2,1)} %bitcast.100), channel_id=1, source_target_pairs={{0,6},{2,0},{4,2},{6,4},{1,7},{3,1},{5,3},{7,5},{8,14},{10,8},{12,... | collective-permute-start | bytes 786440 | tf_op jit(solution)/shard_map/ppermute | solution.py:23
  26.3 3.2 %collective-permute-start.5 = (bf16[256,512]{1,0:T(8,128)(2,1)}, bf16[256,512]{1,0:T(8,128)(2,1)}, u32[]{:S(2)}, u32[]{:S(2)}) collective-permute-start(bf16[256,512]{1,0:T(8,128)(2,1)} %bitcast.101), channel_id=1, source_target_pairs={{0,2},{2,4},{4,6},{6,0},{1,3},{3,5},{5,7},{7,1},{8,10},{10,12},{12... | collective-permute-start | bytes 786440 | tf_op jit(solution)/shard_map/ppermute | solution.py:23
  37.0 8.5 %collective-permute-done.5.refs_2_ = bf16[256,512]{1,0:T(8,128)(2,1)} collective-permute-done((bf16[256,512]{1,0:T(8,128)(2,1)}, bf16[256,512]{1,0:T(8,128)(2,1)}, u32[]{:S(2)}, u32[]{:S(2)}) %collective-permute-start.5) | collective-permute-done | bytes 262176 | tf_op jit(solution)/shard_map/ppermute | solution.py:23
  45.6 3.0 %collective-permute-start.2 = (bf16[256,512]{1,0:T(8,128)(2,1)}, bf16[256,512]{1,0:T(8,128)(2,1)S(1)}, u32[]{:S(2)}, u32[]{:S(2)}) collective-permute-start(bf16[256,512]{1,0:T(8,128)(2,1)} %bitcast.103), channel_id=1, source_target_pairs={{0,24},{8,0},{16,8},{24,16},{1,25},{9,1},{17,9},{25,17},{2,26},{10... | collective-permute-start | bytes 786440 | tf_op jit(solution)/shard_map/ppermute | solution.py:23
  50.8 3.9 %collective-permute-start.11 = (bf16[128,512]{1,0:T(8,128)(2,1)S(1)}, bf16[128,512]{1,0:T(8,128)(2,1)S(1)}, u32[]{:S(2)}, u32[]{:S(2)}) collective-permute-start(bf16[128,512]{1,0:T(8,128)(2,1)S(1)} %slice.115), channel_id=1, source_target_pairs={{0,6},{2,0},{4,2},{6,4},{1,7},{3,1},{5,3},{7,5},{8,14},{10,8},{12,... | collective-permute-start | bytes 393224 | tf_op jit(solution)/shard_map/ppermute | solution.py:23
  59.0 3.3 %collective-permute-start.37 = (bf16[512,128]{1,0:T(8,128)(2,1)S(1)}, bf16[512,128]{1,0:T(8,128)(2,1)S(1)}, u32[]{:S(2)}, u32[]{:S(2)}) collective-permute-start(bf16[512,128]{1,0:T(8,128)(2,1)S(1)} %get-tuple-element.35), channel_id=1, source_target_pairs={{0,32},{32,64},{64,96},{96,0},{1,33},{33,65},{65,97},{97,1},{2,34}... | collective-permute-start | bytes 393224 | tf_op jit(solution)/shard_map/ppermute | solution.py:23
  62.3 6.4 %collective-permute-done.35 = bf16[512,128]{1,0:T(8,128)(2,1)S(1)} collective-permute-done((bf16[512,128]{1,0:T(8,128)(2,1)S(1)}, bf16[512,128]{1,0:T(8,128)(2,1)S(1)}, u32[]{:S(2)}, u32[]{:S(2)}) %collective-permute-start.35) | collective-permute-done | bytes 131104 | tf_op jit(solution)/shard_map/ppermute | solution.py:23
  68.8 3.3 %collective-permute-start.8 = (bf16[512,512]{1,0:T(8,128)(2,1)S(1)}, bf16[512,512]{1,0:T(8,128)(2,1)S(1)}, u32[]{:S(2)}, u32[]{:S(2)}) collective-permute-start(bf16[512,512]{1,0:T(8,128)(2,1)S(1)} %constant_dynamic-update-slice_fusion), channel_id=1, source_target_pairs={{0,24},{8,0},{16,8},{24,16},{1,25},{9,1},{17,9},{25,17},{2,26},{10... | collective-permute-start | bytes 1572872 | tf_op jit(solution)/shard_map/ppermute | solution.py:23
  72.3 3.3 %collective-permute-start.14 = (bf16[256,512]{1,0:T(8,128)(2,1)S(1)}, bf16[256,512]{1,0:T(8,128)(2,1)S(1)}, u32[]{:S(2)}, u32[]{:S(2)}) collective-permute-start(bf16[256,512]{1,0:T(8,128)(2,1)S(1)} %constant_dynamic-update-slice_fusion.2.refs_3_), channel_id=1, source_target_pairs={{0,24},{8,0},{16,8},{24,16},{1,25},{9,1},{17,9},{25,17},{2,26},{10... | collective-permute-start | bytes 786440 | tf_op jit(solution)/shard_map/ppermute | solution.py:23
  75.6 2.8 %copy-done.1 = bf16[1,384,8192]{2,1,0:T(8,128)(2,1)S(1)} copy-done((bf16[1,384,8192]{2,1,0:T(8,128)(2,1)S(1)}, bf16[1,384,8192]{2,1,0:T(8,128)(2,1)}, u32[]{:S(2)}) %copy-start.1) | copy-done | bytes 6291480
  78.4 2.8 %shard_map.107 = (bf16[2,256,512]{2,1,0:T(8,128)(2,1)S(1)}, bf16[2,256,512]{2,1,0:T(8,128)(2,1)S(1)}) custom-call(s32[5]{0:T(128)S(1)} %copy-done.8, bf16[384,8192]{1,0:T(8,128)(2,1)S(1)} %bitcast.89, ...), custom_call_target="tpu_custom_call" | custom-call | flops 805306368 | bytes 3670016 | tf_op jit(solution)/shard_map/pallas_call | solution.py:77
  81.3 9.1 %collective-permute-done.12.refs_6_ = bf16[256,512]{1,0:T(8,128)(2,1)S(1)} collective-permute-done((bf16[256,512]{1,0:T(8,128)(2,1)S(1)}, bf16[256,512]{1,0:T(8,128)(2,1)S(1)}, u32[]{:S(2)}, u32[]{:S(2)}) %collective-permute-start.12) | collective-permute-done | bytes 262176 | tf_op jit(solution)/shard_map/ppermute | solution.py:23
  94.8 6.8 %collective-permute-done.21.refs_0_ = bf16[2,256,512]{2,1,0:T(8,128)(2,1)S(1)} collective-permute-done((bf16[2,256,512]{2,1,0:T(8,128)(2,1)S(1)}, bf16[2,256,512]{2,1,0:T(8,128)(2,1)S(1)}, u32[]{:S(2)}, u32[]{:S(2)}) %collective-permute-start.21) | collective-permute-done | bytes 524320 | tf_op jit(solution)/shard_map/ppermute | solution.py:23
  101.6 2.9 %collective-permute-done.22.refs_1_ = bf16[2,256,512]{2,1,0:T(8,128)(2,1)S(1)} collective-permute-done((bf16[2,256,512]{2,1,0:T(8,128)(2,1)S(1)}, bf16[2,256,512]{2,1,0:T(8,128)(2,1)S(1)}, u32[]{:S(2)}, u32[]{:S(2)}) %collective-permute-start.22) | collective-permute-done | bytes 524320 | tf_op jit(solution)/shard_map/ppermute | solution.py:23
  104.8 3.8 %shard_map.106 = (bf16[2,256,512]{2,1,0:T(8,128)(2,1)}, bf16[2,256,512]{2,1,0:T(8,128)(2,1)}) custom-call(s32[5]{0:T(128)S(1)} %concatenate.29._, bf16[384,8192]{1,0:T(8,128)(2,1)S(1)} %bitcast.90, ...), custom_call_target="tpu_custom_call" | custom-call | flops 805306368 | bytes 3670016 | tf_op jit(solution)/shard_map/pallas_call | solution.py:77
  108.6 3.8 %shard_map.108 = (bf16[2,256,512]{2,1,0:T(8,128)(2,1)}, bf16[2,256,512]{2,1,0:T(8,128)(2,1)}) custom-call(s32[5]{0:T(128)S(1)} %concatenate.30._, bf16[384,8192]{1,0:T(8,128)(2,1)S(1)} %bitcast.91, ...), custom_call_target="tpu_custom_call" | custom-call | flops 805306368 | bytes 3670016 | tf_op jit(solution)/shard_map/pallas_call | solution.py:77
  119.5 2.8 %shard_map.103 = (f32[384,512]{1,0:T(8,128)S(1)}, f32[384,512]{1,0:T(8,128)S(1)}) custom-call(s32[5]{0:T(128)S(1)} %stack.99._, bf16[256,512]{1,0:T(8,128)(2,1)S(1)} %bitcast.104, bf16[256,512]{1,0:T(8,128)(2,1)} %collective-permute-done.4.refs_1_, bf16[256,512]{1,0:T(8,128)(2,1)} %collective-permute-done.5.refs_2_, ...), custom_call_target="tpu_custom_call" | custom-call | flops 805306368 | bytes 2621440 | tf_op jit(solution)/shard_map/pallas_call | solution.py:134
  122.4 4.4 %shard_map.104 = (f32[384,512]{1,0:T(8,128)S(1)}, f32[384,512]{1,0:T(8,128)S(1)}) custom-call(s32[9]{0:T(128)S(1)} %copy-done.9, bf16[256,512]{1,0:T(8,128)(2,1)} %collective-permute-done.refs_0_, bf16[256,512]{1,0:T(8,128)(2,1)S(1)} %collective-permute-done.2.refs_1_, bf16[256,512]{1,0:T(8,128)(2,1)S(1)} %get-tuple-element.45.refs_2_, ...), custom_call_target="tpu_custom_call" | custom-call | flops 1610612736 | bytes 5242880 | tf_op jit(solution)/shard_map/pallas_call | solution.py:134
  126.8 4.6 %shard_map.105 = (f32[384,512]{1,0:T(8,128)S(1)}, f32[384,512]{1,0:T(8,128)}) custom-call(s32[7]{0:T(128)S(1)} %copy-done.10, bf16[128,512]{1,0:T(8,128)(2,1)S(1)} %collective-permute-done.1.refs_0_, bf16[128,512]{1,0:T(8,128)(2,1)S(1)} %collective-permute-done.3.refs_1_, bf16[256,512]{1,0:T(8,128)(2,1)S(1)} %collective-permute-done.7.refs_2_, ...), custom_call_target="tpu_custom_call" | custom-call | flops 805306368 | bytes 2621440 | tf_op jit(solution)/shard_map/pallas_call | solution.py:134
  133.0 4.0 %collective-permute-done.23.refs_2_ = bf16[2,256,512]{2,1,0:T(8,128)(2,1)} collective-permute-done((bf16[2,256,512]{2,1,0:T(8,128)(2,1)}, bf16[2,256,512]{2,1,0:T(8,128)(2,1)}, u32[]{:S(2)}, u32[]{:S(2)}) %collective-permute-start.23) | collective-permute-done | bytes 524320 | tf_op jit(solution)/shard_map/ppermute | solution.py:23
  137.0 3.3 %collective-permute-done.24.refs_3_ = bf16[2,256,512]{2,1,0:T(8,128)(2,1)} collective-permute-done((bf16[2,256,512]{2,1,0:T(8,128)(2,1)}, bf16[2,256,512]{2,1,0:T(8,128)(2,1)}, u32[]{:S(2)}, u32[]{:S(2)}) %collective-permute-start.24) | collective-permute-done | bytes 524320 | tf_op jit(solution)/shard_map/ppermute | solution.py:23
  140.3 4.6 %shard_map.109 = (f32[2,256,512]{2,1,0:T(8,128)S(1)}, f32[2,256,512]{2,1,0:T(8,128)S(1)}) custom-call(s32[5]{0:T(128)S(1)} %concatenate.28._, bf16[384,8192]{1,0:T(8,128)(2,1)S(1)} %bitcast.94, bf16[384,4096]{1,0:T(8,128)(2,1)S(1)} %copy-done.3, bf16[384,512]{1,0:T(8,128)(2,1)S(1)} %bitcast.99, bf16[384,512]{1,0:T(8,128)(2,1)S(1)} %copy-done.6, ...), custom_call_target="tpu_custom_call" | custom-call | flops 805306368 | bytes 3670016 | tf_op jit(solution)/shard_map/pallas_call | solution.py:77
  145.9 3.4 %collective-permute-start.25 = (bf16[128,512]{1,0:T(8,128)(2,1)S(1)}, bf16[128,512]{1,0:T(8,128)(2,1)S(1)}, u32[]{:S(2)}, u32[]{:S(2)}) collective-permute-start(bf16[128,512]{1,0:T(8,128)(2,1)S(1)} %get-tuple-element.41), channel_id=1, source_target_pairs={{0,6},{2,0},{4,2},{6,4},{1,7},{3,1},{5,3},{7,5},{8,14},{10,8},{12,... | collective-permute-start | bytes 393224 | tf_op jit(solution)/shard_map/ppermute | solution.py:23
  150.1 2.2 %collective-permute-start.28 = (bf16[128,512]{1,0:T(8,128)(2,1)S(1)}, bf16[128,512]{1,0:T(8,128)(2,1)S(1)}, u32[]{:S(2)}, u32[]{:S(2)}) collective-permute-start(bf16[128,512]{1,0:T(8,128)(2,1)S(1)} %fusion.11), channel_id=1, source_target_pairs={{0,2},{2,4},{4,6},{6,0},{1,3},{3,5},{5,7},{7,1},{8,10},{10,12},{12... | collective-permute-start | bytes 393224 | tf_op jit(solution)/shard_map/ppermute | solution.py:23
  152.3 4.0 %collective-permute-done.26 = bf16[128,512]{1,0:T(8,128)(2,1)S(1)} collective-permute-done((bf16[128,512]{1,0:T(8,128)(2,1)S(1)}, bf16[128,512]{1,0:T(8,128)(2,1)S(1)}, u32[]{:S(2)}, u32[]{:S(2)}) %collective-permute-start.26) | collective-permute-done | bytes 131104 | tf_op jit(solution)/shard_map/ppermute | solution.py:23
  157.5 3.2 %collective-permute-start.30 = (bf16[128,512]{1,0:T(8,128)(2,1)S(1)}, bf16[128,512]{1,0:T(8,128)(2,1)S(1)}, u32[]{:S(2)}, u32[]{:S(2)}) collective-permute-start(bf16[128,512]{1,0:T(8,128)(2,1)S(1)} %fusion.7), channel_id=1, source_target_pairs={{0,6},{2,0},{4,2},{6,4},{1,7},{3,1},{5,3},{7,5},{8,14},{10,8},{12,... | collective-permute-start | bytes 393224 | tf_op jit(solution)/shard_map/ppermute | solution.py:23
  161.5 3.1 %collective-permute-done.27 = bf16[128,512]{1,0:T(8,128)(2,1)S(1)} collective-permute-done((bf16[128,512]{1,0:T(8,128)(2,1)S(1)}, bf16[128,512]{1,0:T(8,128)(2,1)S(1)}, u32[]{:S(2)}, u32[]{:S(2)}) %collective-permute-start.27) | collective-permute-done | bytes 131104 | tf_op jit(solution)/shard_map/ppermute | solution.py:23
  164.6 2.2 %collective-permute-done.30 = bf16[128,512]{1,0:T(8,128)(2,1)S(1)} collective-permute-done((bf16[128,512]{1,0:T(8,128)(2,1)S(1)}, bf16[128,512]{1,0:T(8,128)(2,1)S(1)}, u32[]{:S(2)}, u32[]{:S(2)}) %collective-permute-start.30) | collective-permute-done | bytes 131104 | tf_op jit(solution)/shard_map/ppermute | solution.py:23
  (136 shorter events, 36.9 us)
Async XLA Ops:
  9.5 66.1 %collective-permute-start.16 = (bf16[384,4096]{1,0:T(8,128)(2,1)}, bf16[384,4096]{1,0:T(8,128)(2,1)S(1)}, u32[]{:S(2)}, u32[]{:S(2)}) collective-permute-start(bf16[384,4096]{1,0:T(8,128)(2,1)} %shard_map.102), channel_id=1, source_target_pairs={{0,1},{1,0},{2,3},{3,2},{4,5},{5,4},{6,7},{7,6},{8,9},{9,8},{10,11... | collective-permute-start | bytes 9437192 | tf_op jit(solution)/shard_map/ppermute | solution.py:23
  15.9 10.3 %collective-permute-start.33 = (bf16[512,128]{1,0:T(8,128)(2,1)}, bf16[512,128]{1,0:T(8,128)(2,1)}, u32[]{:S(2)}, u32[]{:S(2)}) collective-permute-start(bf16[512,128]{1,0:T(8,128)(2,1)} %get-tuple-element.39), channel_id=1, source_target_pairs={{0,96},{32,0},{64,32},{96,64},{1,97},{33,1},{65,33},{97,65},{2,98}... | collective-permute-start | bytes 393224 | tf_op jit(solution)/shard_map/ppermute | solution.py:23
  16.7 12.7 %collective-permute-start.32 = (bf16[512,128]{1,0:T(8,128)(2,1)}, bf16[512,128]{1,0:T(8,128)(2,1)}, u32[]{:S(2)}, u32[]{:S(2)}) collective-permute-start(bf16[512,128]{1,0:T(8,128)(2,1)} %get-tuple-element.40), channel_id=1, source_target_pairs={{0,64},{32,96},{64,0},{96,32},{1,65},{33,97},{65,1},{97,33},{2,66}... | collective-permute-start | bytes 393224 | tf_op jit(solution)/shard_map/ppermute | solution.py:23
  19.9 29.5 %collective-permute-start.4 = (bf16[256,512]{1,0:T(8,128)(2,1)}, bf16[256,512]{1,0:T(8,128)(2,1)}, u32[]{:S(2)}, u32[]{:S(2)}) collective-permute-start(bf16[256,512]{1,0:T(8,128)(2,1)} %bitcast.100), channel_id=1, source_target_pairs={{0,6},{2,0},{4,2},{6,4},{1,7},{3,1},{5,3},{7,5},{8,14},{10,8},{12,... | collective-permute-start | bytes 786440 | tf_op jit(solution)/shard_map/ppermute | solution.py:23
  26.3 19.3 %collective-permute-start.5 = (bf16[256,512]{1,0:T(8,128)(2,1)}, bf16[256,512]{1,0:T(8,128)(2,1)}, u32[]{:S(2)}, u32[]{:S(2)}) collective-permute-start(bf16[256,512]{1,0:T(8,128)(2,1)} %bitcast.101), channel_id=1, source_target_pairs={{0,2},{2,4},{4,6},{6,0},{1,3},{3,5},{5,7},{7,1},{8,10},{10,12},{12... | collective-permute-start | bytes 786440 | tf_op jit(solution)/shard_map/ppermute | solution.py:23
  31.2 19.6 %collective-permute-start.34 = (bf16[512,128]{1,0:T(8,128)(2,1)}, bf16[512,128]{1,0:T(8,128)(2,1)}, u32[]{:S(2)}, u32[]{:S(2)}) collective-permute-start(bf16[512,128]{1,0:T(8,128)(2,1)} %add_convert_fusion.2), channel_id=1, source_target_pairs={{0,128},{128,0},{1,129},{129,1},{2,130},{130,2},{3,131},{131,3},{4... | collective-permute-start | bytes 393224 | tf_op jit(solution)/shard_map/ppermute | solution.py:23
  33.2 24.5 %collective-permute-start = (bf16[256,512]{1,0:T(8,128)(2,1)}, bf16[256,512]{1,0:T(8,128)(2,1)}, u32[]{:S(2)}, u32[]{:S(2)}) collective-permute-start(bf16[256,512]{1,0:T(8,128)(2,1)} %bitcast.102), channel_id=1, source_target_pairs={{0,8},{8,16},{16,24},{24,0},{1,9},{9,17},{17,25},{25,1},{2,10},{10... | collective-permute-start | bytes 786440 | tf_op jit(solution)/shard_map/ppermute | solution.py:23
  45.6 13.2 %collective-permute-start.2 = (bf16[256,512]{1,0:T(8,128)(2,1)}, bf16[256,512]{1,0:T(8,128)(2,1)S(1)}, u32[]{:S(2)}, u32[]{:S(2)}) collective-permute-start(bf16[256,512]{1,0:T(8,128)(2,1)} %bitcast.103), channel_id=1, source_target_pairs={{0,24},{8,0},{16,8},{24,16},{1,25},{9,1},{17,9},{25,17},{2,26},{10... | collective-permute-start | bytes 786440 | tf_op jit(solution)/shard_map/ppermute | solution.py:23
  57.7 14.6 %collective-permute-start.18 = (bf16[384,512]{1,0:T(8,128)(2,1)S(1)}, bf16[384,512]{1,0:T(8,128)(2,1)S(1)}, u32[]{:S(2)}, u32[]{:S(2)}) collective-permute-start(bf16[384,512]{1,0:T(8,128)(2,1)S(1)} %bitcast.95), channel_id=1, source_target_pairs={{0,1},{1,0},{2,3},{3,2},{4,5},{5,4},{6,7},{7,6},{8,9},{9,8},{10,11... | collective-permute-start | bytes 1179656 | tf_op jit(solution)/shard_map/ppermute | solution.py:23
  58.7 10.0 %collective-permute-start.35 = (bf16[512,128]{1,0:T(8,128)(2,1)S(1)}, bf16[512,128]{1,0:T(8,128)(2,1)S(1)}, u32[]{:S(2)}, u32[]{:S(2)}) collective-permute-start(bf16[512,128]{1,0:T(8,128)(2,1)S(1)} %get-tuple-element.35), channel_id=1, source_target_pairs={{0,96},{32,0},{64,32},{96,64},{1,97},{33,1},{65,33},{97,65},{2,98}... | collective-permute-start | bytes 393224 | tf_op jit(solution)/shard_map/ppermute | solution.py:23
  58.8 9.9 %collective-permute-start.36 = (bf16[512,128]{1,0:T(8,128)(2,1)S(1)}, bf16[512,128]{1,0:T(8,128)(2,1)S(1)}, u32[]{:S(2)}, u32[]{:S(2)}) collective-permute-start(bf16[512,128]{1,0:T(8,128)(2,1)S(1)} %get-tuple-element.35), channel_id=1, source_target_pairs={{0,64},{32,96},{64,0},{96,32},{1,65},{33,97},{65,1},{97,33},{2,66}... | collective-permute-start | bytes 393224 | tf_op jit(solution)/shard_map/ppermute | solution.py:23
  59.0 13.1 %collective-permute-start.37 = (bf16[512,128]{1,0:T(8,128)(2,1)S(1)}, bf16[512,128]{1,0:T(8,128)(2,1)S(1)}, u32[]{:S(2)}, u32[]{:S(2)}) collective-permute-start(bf16[512,128]{1,0:T(8,128)(2,1)S(1)} %get-tuple-element.35), channel_id=1, source_target_pairs={{0,32},{32,64},{64,96},{96,0},{1,33},{33,65},{65,97},{97,1},{2,34}... | collective-permute-start | bytes 393224 | tf_op jit(solution)/shard_map/ppermute | solution.py:23
  68.7 23.8 %collective-permute-start.6 = (bf16[512,512]{1,0:T(8,128)(2,1)S(1)}, bf16[512,512]{1,0:T(8,128)(2,1)S(1)}, u32[]{:S(2)}, u32[]{:S(2)}) collective-permute-start(bf16[512,512]{1,0:T(8,128)(2,1)S(1)} %constant_dynamic-update-slice_fusion), channel_id=1, source_target_pairs={{0,8},{8,16},{16,24},{24,0},{1,9},{9,17},{17,25},{25,1},{2,10},{10... | collective-permute-start | bytes 1572872 | tf_op jit(solution)/shard_map/ppermute | solution.py:23
  68.8 25.1 %collective-permute-start.8 = (bf16[512,512]{1,0:T(8,128)(2,1)S(1)}, bf16[512,512]{1,0:T(8,128)(2,1)S(1)}, u32[]{:S(2)}, u32[]{:S(2)}) collective-permute-start(bf16[512,512]{1,0:T(8,128)(2,1)S(1)} %constant_dynamic-update-slice_fusion), channel_id=1, source_target_pairs={{0,24},{8,0},{16,8},{24,16},{1,25},{9,1},{17,9},{25,17},{2,26},{10... | collective-permute-start | bytes 1572872 | tf_op jit(solution)/shard_map/ppermute | solution.py:23
  72.1 18.3 %collective-permute-start.12 = (bf16[256,512]{1,0:T(8,128)(2,1)S(1)}, bf16[256,512]{1,0:T(8,128)(2,1)S(1)}, u32[]{:S(2)}, u32[]{:S(2)}) collective-permute-start(bf16[256,512]{1,0:T(8,128)(2,1)S(1)} %constant_dynamic-update-slice_fusion.2.refs_3_), channel_id=1, source_target_pairs={{0,8},{8,16},{16,24},{24,0},{1,9},{9,17},{17,25},{25,1},{2,10},{10... | collective-permute-start | bytes 786440 | tf_op jit(solution)/shard_map/ppermute | solution.py:23
  72.3 18.1 %collective-permute-start.14 = (bf16[256,512]{1,0:T(8,128)(2,1)S(1)}, bf16[256,512]{1,0:T(8,128)(2,1)S(1)}, u32[]{:S(2)}, u32[]{:S(2)}) collective-permute-start(bf16[256,512]{1,0:T(8,128)(2,1)S(1)} %constant_dynamic-update-slice_fusion.2.refs_3_), channel_id=1, source_target_pairs={{0,24},{8,0},{16,8},{24,16},{1,25},{9,1},{17,9},{25,17},{2,26},{10... | collective-permute-start | bytes 786440 | tf_op jit(solution)/shard_map/ppermute | solution.py:23
  81.2 20.4 %collective-permute-start.21 = (bf16[2,256,512]{2,1,0:T(8,128)(2,1)S(1)}, bf16[2,256,512]{2,1,0:T(8,128)(2,1)S(1)}, u32[]{:S(2)}, u32[]{:S(2)}) collective-permute-start(bf16[2,256,512]{2,1,0:T(8,128)(2,1)S(1)} %get-tuple-element.26), channel_id=1, source_target_pairs={{0,8},{8,16},{16,24},{24,0},{1,9},{9,17},{17,25},{25,1},{2,10},{10... | collective-permute-start | bytes 1572872 | tf_op jit(solution)/shard_map/ppermute | solution.py:23
  90.4 14.1 %collective-permute-start.22 = (bf16[2,256,512]{2,1,0:T(8,128)(2,1)S(1)}, bf16[2,256,512]{2,1,0:T(8,128)(2,1)S(1)}, u32[]{:S(2)}, u32[]{:S(2)}) collective-permute-start(bf16[2,256,512]{2,1,0:T(8,128)(2,1)S(1)} %get-tuple-element.27), channel_id=1, source_target_pairs={{0,24},{8,0},{16,8},{24,16},{1,25},{9,1},{17,9},{25,17},{2,26},{10... | collective-permute-start | bytes 1572872 | tf_op jit(solution)/shard_map/ppermute | solution.py:23
  90.4 22.0 %collective-permute-start.1 = (bf16[128,512]{1,0:T(8,128)(2,1)S(1)}, bf16[128,512]{1,0:T(8,128)(2,1)S(1)}, u32[]{:S(2)}, u32[]{:S(2)}) collective-permute-start(bf16[128,512]{1,0:T(8,128)(2,1)S(1)} %slice.110), channel_id=1, source_target_pairs={{0,8},{8,16},{16,24},{24,0},{1,9},{9,17},{17,25},{25,1},{2,10},{10... | collective-permute-start | bytes 393224 | tf_op jit(solution)/shard_map/ppermute | solution.py:23
  92.5 20.0 %collective-permute-start.3 = (bf16[128,512]{1,0:T(8,128)(2,1)S(1)}, bf16[128,512]{1,0:T(8,128)(2,1)S(1)}, u32[]{:S(2)}, u32[]{:S(2)}) collective-permute-start(bf16[128,512]{1,0:T(8,128)(2,1)S(1)} %slice.111), channel_id=1, source_target_pairs={{0,24},{8,0},{16,8},{24,16},{1,25},{9,1},{17,9},{25,17},{2,26},{10... | collective-permute-start | bytes 393224 | tf_op jit(solution)/shard_map/ppermute | solution.py:23
  93.9 22.7 %collective-permute-start.7 = (bf16[256,512]{1,0:T(8,128)(2,1)S(1)}, bf16[256,512]{1,0:T(8,128)(2,1)S(1)}, u32[]{:S(2)}, u32[]{:S(2)}) collective-permute-start(bf16[256,512]{1,0:T(8,128)(2,1)S(1)} %get-tuple-element.45.refs_2_), channel_id=1, source_target_pairs={{0,8},{8,16},{16,24},{24,0},{1,9},{9,17},{17,25},{25,1},{2,10},{10... | collective-permute-start | bytes 786440 | tf_op jit(solution)/shard_map/ppermute | solution.py:23
  101.6 12.7 %collective-permute-start.13 = (bf16[128,512]{1,0:T(8,128)(2,1)S(1)}, bf16[128,512]{1,0:T(8,128)(2,1)S(1)}, u32[]{:S(2)}, u32[]{:S(2)}) collective-permute-start(bf16[128,512]{1,0:T(8,128)(2,1)S(1)} %slice.116), channel_id=1, source_target_pairs={{0,8},{8,16},{16,24},{24,0},{1,9},{9,17},{17,25},{25,1},{2,10},{10... | collective-permute-start | bytes 393224 | tf_op jit(solution)/shard_map/ppermute | solution.py:23
  104.5 10.1 %collective-permute-start.15 = (bf16[128,512]{1,0:T(8,128)(2,1)S(1)}, bf16[128,512]{1,0:T(8,128)(2,1)S(1)}, u32[]{:S(2)}, u32[]{:S(2)}) collective-permute-start(bf16[128,512]{1,0:T(8,128)(2,1)S(1)} %slice.117), channel_id=1, source_target_pairs={{0,24},{8,0},{16,8},{24,16},{1,25},{9,1},{17,9},{25,17},{2,26},{10... | collective-permute-start | bytes 393224 | tf_op jit(solution)/shard_map/ppermute | solution.py:23
  112.5 14.3 %collective-permute-start.9 = (bf16[256,512]{1,0:T(8,128)(2,1)S(1)}, bf16[256,512]{1,0:T(8,128)(2,1)S(1)}, u32[]{:S(2)}, u32[]{:S(2)}) collective-permute-start(bf16[256,512]{1,0:T(8,128)(2,1)S(1)} %get-tuple-element.47.refs_5_), channel_id=1, source_target_pairs={{0,24},{8,0},{16,8},{24,16},{1,25},{9,1},{17,9},{25,17},{2,26},{10... | collective-permute-start | bytes 786440 | tf_op jit(solution)/shard_map/ppermute | solution.py:23
  112.5 20.5 %collective-permute-start.19 = (bf16[2,256,512]{2,1,0:T(8,128)(2,1)}, bf16[2,256,512]{2,1,0:T(8,128)(2,1)S(1)}, u32[]{:S(2)}, u32[]{:S(2)}) collective-permute-start(bf16[2,256,512]{2,1,0:T(8,128)(2,1)} %get-tuple-element.24), channel_id=1, source_target_pairs={{0,24},{8,0},{16,8},{24,16},{1,25},{9,1},{17,9},{25,17},{2,26},{10... | collective-permute-start | bytes 1572872 | tf_op jit(solution)/shard_map/ppermute | solution.py:23
  114.3 18.6 %collective-permute-start.20 = (bf16[2,256,512]{2,1,0:T(8,128)(2,1)}, bf16[2,256,512]{2,1,0:T(8,128)(2,1)}, u32[]{:S(2)}, u32[]{:S(2)}) collective-permute-start(bf16[2,256,512]{2,1,0:T(8,128)(2,1)} %get-tuple-element.25), channel_id=1, source_target_pairs={{0,8},{8,16},{16,24},{24,0},{1,9},{9,17},{17,25},{25,1},{2,10},{10... | collective-permute-start | bytes 1572872 | tf_op jit(solution)/shard_map/ppermute | solution.py:23
  114.6 22.4 %collective-permute-start.23 = (bf16[2,256,512]{2,1,0:T(8,128)(2,1)}, bf16[2,256,512]{2,1,0:T(8,128)(2,1)}, u32[]{:S(2)}, u32[]{:S(2)}) collective-permute-start(bf16[2,256,512]{2,1,0:T(8,128)(2,1)} %get-tuple-element.28), channel_id=1, source_target_pairs={{0,8},{8,16},{16,24},{24,0},{1,9},{9,17},{17,25},{25,1},{2,10},{10... | collective-permute-start | bytes 1572872 | tf_op jit(solution)/shard_map/ppermute | solution.py:23
  116.6 23.7 %collective-permute-start.24 = (bf16[2,256,512]{2,1,0:T(8,128)(2,1)}, bf16[2,256,512]{2,1,0:T(8,128)(2,1)}, u32[]{:S(2)}, u32[]{:S(2)}) collective-permute-start(bf16[2,256,512]{2,1,0:T(8,128)(2,1)} %get-tuple-element.29), channel_id=1, source_target_pairs={{0,24},{8,0},{16,8},{24,16},{1,25},{9,1},{17,9},{25,17},{2,26},{10... | collective-permute-start | bytes 1572872 | tf_op jit(solution)/shard_map/ppermute | solution.py:23
  131.4 29.2 %collective-permute-start.17 = (f32[384,512]{1,0:T(8,128)}, f32[384,512]{1,0:T(8,128)S(1)}, u32[]{:S(2)}, u32[]{:S(2)}) collective-permute-start(f32[384,512]{1,0:T(8,128)} %get-tuple-element.23), channel_id=1, source_target_pairs={{0,1},{1,0},{2,3},{3,2},{4,5},{5,4},{6,7},{7,6},{8,9},{9,8},{10,11... | collective-permute-start | bytes 2359304 | tf_op jit(solution)/shard_map/ppermute | solution.py:23
  145.0 11.3 %collective-permute-start.26 = (bf16[128,512]{1,0:T(8,128)(2,1)S(1)}, bf16[128,512]{1,0:T(8,128)(2,1)S(1)}, u32[]{:S(2)}, u32[]{:S(2)}) collective-permute-start(bf16[128,512]{1,0:T(8,128)(2,1)S(1)} %get-tuple-element.43), channel_id=1, source_target_pairs={{0,2},{2,4},{4,6},{6,0},{1,3},{3,5},{5,7},{7,1},{8,10},{10,12},{12... | collective-permute-start | bytes 393224 | tf_op jit(solution)/shard_map/ppermute | solution.py:23
  145.9 15.7 %collective-permute-start.25 = (bf16[128,512]{1,0:T(8,128)(2,1)S(1)}, bf16[128,512]{1,0:T(8,128)(2,1)S(1)}, u32[]{:S(2)}, u32[]{:S(2)}) collective-permute-start(bf16[128,512]{1,0:T(8,128)(2,1)S(1)} %get-tuple-element.41), channel_id=1, source_target_pairs={{0,6},{2,0},{4,2},{6,4},{1,7},{3,1},{5,3},{7,5},{8,14},{10,8},{12,... | collective-permute-start | bytes 393224 | tf_op jit(solution)/shard_map/ppermute | solution.py:23
  150.1 11.4 %collective-permute-start.28 = (bf16[128,512]{1,0:T(8,128)(2,1)S(1)}, bf16[128,512]{1,0:T(8,128)(2,1)S(1)}, u32[]{:S(2)}, u32[]{:S(2)}) collective-permute-start(bf16[128,512]{1,0:T(8,128)(2,1)S(1)} %fusion.11), channel_id=1, source_target_pairs={{0,2},{2,4},{4,6},{6,0},{1,3},{3,5},{5,7},{7,1},{8,10},{10,12},{12... | collective-permute-start | bytes 393224 | tf_op jit(solution)/shard_map/ppermute | solution.py:23
  (26 other events, 334.5 us)

commit v2 on v0

v2 whole, which is shorter than its diff:
```python
import functools

import jax
import jax.numpy as jnp
from jax import lax
from jax.experimental import pallas as pl
from jax.experimental.pallas import tpu as pltpu
from jax.sharding import Mesh, PartitionSpec as P

BLOCK = 128


outer_rate = 0.7
outer_momentum = 0.9
mix_weight = 0.5

RING = 4
ROWS = 256


def shift(v, axis, k):
    n = lax.axis_size(axis)
    return lax.ppermute(v, axis, [(i, (i + k) % n) for i in range(n)])


def params(mib=24):
    return pltpu.CompilerParams(vmem_limit_bytes=mib << 20)


FREE = pl.CostEstimate(flops=1, bytes_accessed=1, transcendentals=0)
TN = (((0,), (0,)), ((), ()))
PAIR = 2 * ROWS

FAR = [(2, 0), (2, 1), (2, 2), (2, 3)]
NEXT = [(1, 2), (1, 3), (3, 0), (3, 1)]
LAST = [(1, 0), (1, 1), (3, 2), (3, 3), (0, 0), (0, 1), (0, 2), (0, 3)]


def after(v, *others):
    return lax.optimization_barrier((v, *others))[0]


def pick_kernel(n, s_ref, a_ref, b_ref, *refs):
    (*cots, mine, send), core = refs, s_ref[0]
    i = pl.program_id(0)

    def pair():
        for j, v in enumerate((a_ref, b_ref)):
            cut = slice(j * ROWS, (j + 1) * ROWS)
            left, right = v[:, :ROWS], v[:, ROWS:]
            mine[:, cut] = jnp.where(core == 0, left, right)
            send[:, cut] = jnp.where(core == 0, right, left)

    if not cots:
        pair()
        return
    pl.when(i < n)(pair)

    @pl.when(i == n)
    def _():
        send[...] = cots[0][...]


def pick(tokens, core, blocks, cot=None):
    t = tokens.shape[0]
    n = len(blocks) // 2
    cots = [] if cot is None else [cot]
    steps = n + len(cots)
    return pl.pallas_call(
        functools.partial(pick_kernel, n),
        grid_spec=pltpu.PrefetchScalarGridSpec(
            num_scalar_prefetch=1,
            grid=(steps,),
            in_specs=[
                pl.BlockSpec((t, PAIR), lambda i, s, j=j: (0, s[2 * jnp.minimum(i, n - 1) + j + 1]))
                for j in range(2)
            ]
            + [pl.BlockSpec((t, PAIR), lambda i, s: (0, 0))] * len(cots),
            out_specs=[
                pl.BlockSpec((t, PAIR), lambda i, s: (0, jnp.minimum(i, n - 1))),
                pl.BlockSpec((t, PAIR), lambda i, s: (0, i)),
            ],
        ),
        out_shape=[
            jax.ShapeDtypeStruct((t, n * PAIR), tokens.dtype),
            jax.ShapeDtypeStruct((t, steps * PAIR), tokens.dtype),
        ],
        compiler_params=params(),
        cost_estimate=FREE,
    )(jnp.stack([core] + blocks), tokens, tokens, *cots)


def stack_kernel(*refs):
    out = refs[-1]
    r = refs[0].shape[0]
    for i, v in enumerate(refs[:-1]):
        out[i * r : (i + 1) * r] = v[...]


def stack_rows(*arrays):
    r, k = arrays[0].shape
    n = len(arrays)
    return pl.pallas_call(
        stack_kernel,
        out_shape=jax.ShapeDtypeStruct((n * r, k), arrays[0].dtype),
        compiler_params=params(),
        cost_estimate=FREE,
    )(*arrays)


def grad_kernel(h_ref, hr_ref, g_ref, gp_ref, *outs):
    total = lax.dot_general(h_ref[...], g_ref[...], TN, preferred_element_type=jnp.float32)
    total += lax.dot_general(hr_ref[...], gp_ref[...], TN, preferred_element_type=jnp.float32)
    for step, out in enumerate(outs):

        @pl.when(pl.program_id(0) == step)
        def _():
            out[...] = total.astype(out.dtype)


def grad_rows_of(mine, theirs, first, cot, with_cot, dtypes):
    t, k = cot.shape
    column = pl.BlockSpec((t, PAIR), lambda i: (0, i + first))
    last = with_cot.shape[1] // k - 1
    return pl.pallas_call(
        grad_kernel,
        grid=(len(dtypes),),
        in_specs=[
            column,
            column,
            pl.BlockSpec((t, k), lambda i: (0, 0)),
            pl.BlockSpec((t, k), lambda i: (0, last)),
        ],
        out_specs=[pl.BlockSpec((PAIR, k), lambda i: (0, 0))] * len(dtypes),
        out_shape=[jax.ShapeDtypeStruct((PAIR, k), d) for d in dtypes],
        compiler_params=params(),
        cost_estimate=FREE,
    )(mine, theirs, cot, with_cot)


def sums_kernel(own_01, own_23, a, b, c, d, s0, s1, s2, s3):
    f32 = jnp.float32
    for j, out in enumerate((s0, s1, s2, s3)):
        own, more = ((own_01, (a, b)), (own_23, (c, d)))[j // 2]
        cut = slice((j % 2) * ROWS, (j % 2 + 1) * ROWS)
        out[...] = (own[cut] + more[0][cut].astype(f32) + more[1][cut].astype(f32)).astype(out.dtype)


def sums_along_y(own_01, own_23, *received):
    k = own_01.shape[1]
    dtypes = [jnp.float32] + [jnp.bfloat16] * 3
    return pl.pallas_call(
        sums_kernel,
        out_shape=[jax.ShapeDtypeStruct((ROWS, k), d) for d in dtypes],
        compiler_params=params(),
        cost_estimate=FREE,
    )(own_01, own_23, *received)


def values_kernel(cuts, has_acc, *refs):
    m, n = len(cuts), sum(len(c) for c in cuts)
    pieces, h, hr = refs[:m], refs[m : m + n], refs[m + n : m + 2 * n]
    outs = refs[-2:]
    for j, blocks in enumerate((h, hr)):
        total = refs[m + 2 * n + j][...] if has_acc else None
        b = 0
        for piece, cut in zip(pieces, cuts):
            for start in cut:
                part = jnp.dot(
                    blocks[b][...],
                    piece[start : start + PAIR],
                    preferred_element_type=jnp.float32,
                )
                total = part if total is None else total + part
                b += 1
        outs[j][...] = total


def values_part(pieces, acc):
    cuts = [[start for start, _, _ in parts] for _, parts in pieces]
    use = [(source, pair) for _, parts in pieces for _, source, pair in parts]
    t = use[0][0][0].shape[0]
    k = pieces[0][0].shape[1]
    acc = list(acc or ())
    whole = pl.BlockSpec((t, k), lambda i: (0, 0))
    columns = [pl.BlockSpec((t, PAIR), lambda i, p=p: (0, p)) for _, p in use]
    return pl.pallas_call(
        functools.partial(values_kernel, cuts, bool(acc)),
        grid=(1,),
        in_specs=[pl.BlockSpec(w.shape, lambda i: (0, 0)) for w, _ in pieces]
        + columns
        + columns
        + [whole] * len(acc),
        out_specs=[whole, whole],
        out_shape=[jax.ShapeDtypeStruct((t, k), jnp.float32)] * 2,
        compiler_params=params(),
        cost_estimate=FREE,
    )(
        *[w for w, _ in pieces],
        *[source[0] for source, _ in use],
        *[source[1] for source, _ in use],
        *acc,
    )


def encode_kernel(_, l_ref, g_ref, r_ref, *outs):
    nudged = (g_ref[...] - l_ref[...]) + r_ref[...]
    top = jnp.max(jnp.abs(nudged), axis=1, keepdims=True) + 1e-06
    scale = top.astype(jnp.bfloat16).astype(jnp.float32)
    codes = (nudged / scale).astype(jnp.bfloat16).astype(jnp.float32)
    decoded = (codes * scale).astype(jnp.bfloat16)
    for k, out in enumerate(outs):

        @pl.when(pl.program_id(0) == k)
        def _():
            out[...] = decoded


def encode(x, local_row, global_row, residual_row):
    n = local_row.shape[0] // RING
    part = pl.BlockSpec((n, BLOCK), lambda i, s: (lax.rem(s[0] + i, RING), 0))
    return pl.pallas_call(
        encode_kernel,
        grid_spec=pltpu.PrefetchScalarGridSpec(
            num_scalar_prefetch=1,
            grid=(RING,),
            in_specs=[part] * 3,
            out_specs=[pl.BlockSpec((n, BLOCK), lambda i, s: (0, 0))] * RING,
        ),
        out_shape=[jax.ShapeDtypeStruct((n, BLOCK), jnp.bfloat16)] * RING,
        compiler_params=params(),
        cost_estimate=FREE,
    )(x[None], local_row, global_row, residual_row)


def outer_kernel(replicas, _, l_ref, g_ref, m_ref, *refs):
    sums, (mixed_ref, momentum_ref) = refs[:-2], refs[-2:]
    for k, chunk in enumerate(sums):

        @pl.when(pl.program_id(0) == k)
        def _():
            average = chunk[...].astype(jnp.float32) / replicas
            new_momentum = outer_momentum * m_ref[...] + average
            new_global = g_ref[...] - outer_rate * (average + outer_momentum * new_momentum)
            mixed_ref[...] = mix_weight * l_ref[...] + (1.0 - mix_weight) * new_global
            momentum_ref[...] = new_momentum


def outer_step(x, replicas, local_row, global_row, momentum_row, sums):
    n = local_row.shape[0] // RING
    part = pl.BlockSpec((n, BLOCK), lambda i, s: (lax.rem(s[0] + i, RING), 0))
    return pl.pallas_call(
        functools.partial(outer_kernel, replicas),
        grid_spec=pltpu.PrefetchScalarGridSpec(
            num_scalar_prefetch=1,
            grid=(RING,),
            in_specs=[part] * 3 + [pl.BlockSpec((n, BLOCK), lambda i, s: (0, 0))] * RING,
            out_specs=[part, part],
        ),
        out_shape=[jax.ShapeDtypeStruct(local_row.shape, jnp.float32)] * 2,
        compiler_params=params(),
        cost_estimate=FREE,
    )(x[None], local_row, global_row, momentum_row, *sums)


def per_device(
    hidden_in, value_weight, grad_out, local_fragment, global_fragment, momentum, residual
):
    tokens = hidden_in[0]
    weight = value_weight[0]
    cot = grad_out[0]
    bf, f32 = jnp.bfloat16, jnp.float32
    x, y, zh, core = (lax.axis_index(a) for a in ("x", "y", "zh", "core"))

    def blocks(where):
        return [lax.rem(y + dy, RING) * RING + lax.rem(zh + dz, RING) for dy, dz in where]

    w_1, w_3 = shift(weight, "zh", -1), shift(weight, "zh", -3)

    mine, send = pick(tokens, core, blocks(FAR + NEXT + LAST), cot)
    local_row, global_row, momentum_row, residual_row = (
        v.reshape(-1, BLOCK) for v in (local_fragment, global_fragment, momentum, residual)
    )
    chunks = encode(x, local_row, global_row, residual_row)
    mine, send, w_1, w_3, *chunks = lax.optimization_barrier((mine, send, w_1, w_3, *chunks))
    theirs = shift(send, "core", 1)
    parts = [chunks[0]] + [shift(chunks[k], "x", k) for k in (1, 2, 3)]

    w_2 = shift(after(weight, w_1), "zh", 2)
    w_01 = stack_rows(weight, w_1)
    prev_01, next_01 = shift(w_01, "y", 1), shift(w_01, "y", -1)

    def grads(first, dtypes, *others):
        return grad_rows_of(mine, after(theirs, *others), first, cot, theirs, dtypes)

    far_a, far_b = grads(0, [bf, bf], w_01)
    in_a, in_b = shift(far_a, "y", 1), shift(far_b, "y", -1)
    parts = after(tuple(parts), far_a)
    dir_b, dir_a = grads(2, [bf, bf], *parts)
    over_x = sum(v.astype(f32) for v in after(parts, dir_b)).astype(bf)
    from_zl = shift(over_x, "zl", 1)
    got_b, got_a = shift(dir_b, "y", 1), shift(dir_a, "y", -1)

    in_a, in_b, from_zl = lax.optimization_barrier((in_a, in_b, from_zl, dir_b))[:3]
    own_a, own_b, own_01, own_23 = grads(4, [f32] * 4, in_a, in_b, from_zl)
    prev_01, next_01 = after((prev_01, next_01), own_a)
    far_01 = shift(prev_01, "y", 1)
    in_a, in_b, next_01 = lax.optimization_barrier((in_a, in_b, next_01))
    mer_a = (own_a + in_a.astype(f32)).astype(bf)
    mer_b = (own_b + in_b.astype(f32)).astype(bf)
    sum_a, sum_b = shift(mer_a, "y", 1), shift(mer_b, "y", -1)

    from_zl, over_x = after((from_zl, over_x), mer_a, mer_b)
    total = (over_x.astype(f32) + from_zl.astype(f32)).astype(bf)
    totals = [total] + [shift(total, "x", -k) for k in (1, 2, 3)]
    replicas = lax.axis_size("x") * lax.axis_size("zl")
    mixed, new_momentum = outer_step(x, replicas, local_row, global_row, momentum_row, totals)

    w_23 = stack_rows(*after((w_2, w_3), mixed))
    received = after((got_a, sum_a, got_b, sum_b), w_23, mixed)
    s0, s1, s2, s3 = sums_along_y(own_01, own_23, *received)
    g1, g2, g3 = (shift(v, "zh", k) for v, k in ((s1, 1), (s2, 2), (s3, 3)))
    w_23 = after(w_23, s1)
    prev_23, next_23 = shift(w_23, "y", 1), shift(w_23, "y", -1)

    cols = (mine, theirs)
    acc = values_part(
        [
            (after(w_01, s1), [(0, cols, 6)]),
            (w_23, [(0, cols, 7)]),
            (prev_01, [(0, cols, 3)]),
            (next_01, [(0, cols, 4)]),
            (far_01, [(0, cols, 0)]),
        ],
        None,
    )
    prev_23, next_23 = after((prev_23, next_23), acc[0], g1, g3)
    far_23 = shift(next_23, "y", -1)
    acc = values_part([(prev_23, [(0, cols, 5)]), (next_23, [(0, cols, 2)])], acc)
    far_23, g1, g2, g3 = lax.optimization_barrier((far_23, g1, g2, g3))
    ours, other = values_part([(far_23, [(0, cols, 1)])], acc)
    back = shift(other, "core", 1)
    grad_rows = s0 + g1.astype(f32) + g2.astype(f32) + g3.astype(f32)
    values = (ours + back).astype(bf)

    return (values[None], grad_rows[None], mixed.reshape(1, -1), new_momentum.reshape(-1))


def solution(mesh):
    whole = Mesh(mesh.devices.reshape(2, 4, 4, 4, 2), ("zl", "x", "y", "zh", "core"))
    replica, fsdp = ("zl", "x"), ("y", "zh", "core")
    return jax.shard_map(
        per_device,
        mesh=whole,
        in_specs=(
            P(replica, fsdp, None),
            P(replica, fsdp, None),
            P(replica, fsdp, None),
            P(replica, fsdp),
            P(fsdp),
            P(fsdp),
            P(replica, fsdp),
        ),
        out_specs=(
            P(replica, fsdp, None),
            P(replica, fsdp, None),
            P(replica, fsdp),
            P(fsdp),
        ),
        check_vma=False,
    )
```

time: 278 us -> 132 us (0.47)
  waiting for transfers between devices: 231 us -> 60.7 us
  starting transfers between devices: 0.12 us -> 37.9 us
  matrix products: 20.9 us -> 0 us
  Pallas kernels: 0 us -> 18.2 us
  between operations: 15.5 us -> 0.86 us
  local copies, waits for them, and re-layouts: 0.02 us -> 10.3 us
  other arithmetic: 8.29 us -> 2.24 us
    reduce_scatter x1 -> x0, waiting for transfers between devices: 148 us -> none  [per_device(): lax.psum_scatter(lax.dot_general(columns, cotangent, (((0,), (0,)), ((),...]
    psum x1 -> x0, waiting for transfers between devices: 82.8 us -> none  [per_device(): lax.psum(decoded.astype(jnp.bfloat16), 'replica').astype(jnp.float32)]
    ppermute x0 -> x27, waiting for transfers between devices: none -> 60.7 us  [shift(): return lax.ppermute(v, axis, [(i, (i + k) % n) for i in range(n)])]
    ppermute x0 -> x27, starting transfers between devices: none -> 37.9 us  [shift(): return lax.ppermute(v, axis, [(i, (i + k) % n) for i in range(n)])]
    dot_general x2 -> x0, matrix products: 20.9 us -> none  [the longest x1 11.1 us: per_device(): lax.dot_general(columns, cotangent, (((0,), (0,)), ((), ())), preferred_e...]
    pallas_call x0 -> x12, Pallas kernels: none -> 18.2 us  [the longest x3 7.03 us: grad_rows_of(): pl.pallas_call(grad_kernel, grid=(len(dtypes),), in_specs=[column, column...]
    unnamed x8 -> x22, local copies, waits for them, and re-layouts: 0.02 us -> 10.2 us
    convert_element_type x4, other arithmetic: 3.35 us -> 0.47 us  [the longest x1 0.2 us: per_device(): mer_b = (own_b + in_b.astype(f32)).astype(bf)]
  transfers between devices with their start and end apart: 3 -> 27, of which waited for: 2 -> 11; matrix products, arithmetic and copies ran while one was open for 9% -> 1% of each run, Pallas kernels for 0% -> 14%
where the time goes in v2:
time: 132 us; the launch traced here: 130 us
  waiting for transfers between devices  60.7 us (46%)
  starting transfers between devices  37.9 us (29%)
  Pallas kernels  18.2 us (14%)
  local copies, waits for them, and re-layouts  10.3 us (8%)
  other arithmetic  2.24 us (2%)
    ppermute x27, waiting for transfers between devices, shift(): return lax.ppermute(v, axis, [(i, (i + k) % n) for i in range(n)])  60.7 us
    ppermute x27, starting transfers between devices, shift(): return lax.ppermute(v, axis, [(i, (i + k) % n) for i in range(n)])  37.9 us
    unnamed x22, local copies, waits for them, and re-layouts  10.2 us
    pallas_call x3, Pallas kernels, grad_rows_of(): pl.pallas_call(grad_kernel, grid=(len(dtypes),), in_specs=[column, column...  7.03 us
    pallas_call x3, Pallas kernels, values_part(): pl.pallas_call(functools.partial(values_kernel, cuts, bool(acc)), grid=(1...  3.72 us
  transfers between devices with their start and end apart: 27, of which 11 were waited for; matrix products, arithmetic and copies ran while one was open for 1% of the time, Pallas kernels for 14%

profile of v2, /device:TPU:5, one launch (start us, length us, event | category | flops | bytes accessed | tf_op | source)
XLA Modules:
  0.0 130.2 jit_solution(2368061455145394632)
XLA Ops:
  0.6 6.1 %collective-permute-start = (bf16[256,512]{1,0:T(8,128)(2,1)}, bf16[256,512]{1,0:T(8,128)(2,1)}, u32[]{:S(2)}, u32[]{:S(2)}) collective-permute-start(bf16[256,512]{1,0:T(8,128)(2,1)} %bitcast.43), channel_id=1, source_target_pairs={{0,6},{2,0},{4,2},{6,4},{1,7},{3,1},{5,3},{7,5},{8,14},{10,8},{12,... | collective-permute-start | bytes 786440 | tf_op jit(solution)/shard_map/ppermute | solution.py:23
  6.8 2.8 %copy-done = bf16[1,384,8192]{2,1,0:T(8,128)(2,1)S(1)} copy-done((bf16[1,384,8192]{2,1,0:T(8,128)(2,1)S(1)}, bf16[1,384,8192]{2,1,0:T(8,128)(2,1)}, u32[]{:S(2)}) %copy-start) | copy-done | bytes 6291480
  10.6 2.4 %shard_map.102 = (bf16[384,4096]{1,0:T(8,128)(2,1)S(1)}, bf16[384,4608]{1,0:T(8,128)(2,1)S(1)}) custom-call(s32[17]{0:T(128)S(1)} %stack.71.s_ref, bf16[384,8192]{1,0:T(8,128)(2,1)S(1)} %bitcast.31, bf16[384,8192]{1,0:T(8,128)(2,1)S(1)} %bitcast.32, bf16[384,512]{1,0:T(8,128)(2,1)S(1)} %bitcast.33), custom_call_target="tpu_custom_call" | custom-call | flops 1 | bytes 1 | tf_op jit(solution)/shard_map/pallas_call | solution.py:69
  13.1 1.7 %copy-done.10 = bf16[384,4608]{1,0:T(8,128)(2,1)} copy-done((bf16[384,4608]{1,0:T(8,128)(2,1)}, bf16[384,4608]{1,0:T(8,128)(2,1)S(1)}, u32[]{:S(2)}) %copy-start.10) | copy-done | bytes 3538968
  14.8 1.3 copy-done.3
  19.3 3.7 %collective-permute-start.3 = (bf16[384,4608]{1,0:T(8,128)(2,1)}, bf16[384,4608]{1,0:T(8,128)(2,1)S(1)}, u32[]{:S(2)}, u32[]{:S(2)}) collective-permute-start(bf16[384,4608]{1,0:T(8,128)(2,1)} %copy-done.10), channel_id=1, source_target_pairs={{0,1},{1,0},{2,3},{3,2},{4,5},{5,4},{6,7},{7,6},{8,9},{9,8},{10,11... | collective-permute-start | bytes 10616840 | tf_op jit(solution)/shard_map/ppermute | solution.py:23
  26.4 2.7 %collective-permute-done.3.hr_ref.gp_ref.refs_10_.refs_11_.refs_12_.refs_13_.refs_14_.refs_4_.refs_5_.refs_2_ = bf16[384,4608]{1,0:T(8,128)(2,1)S(1)} collective-permute-done((bf16[384,4608]{1,0:T(8,128)(2,1)}, bf16[384,4608]{1,0:T(8,128)(2,1)S(1)}, u32[]{:S(2)}, u32[]{:S(2)}) %collective-permute-start.3) | collective-permute-done | bytes 3538976 | tf_op jit(solution)/shard_map/ppermute | solution.py:23
  29.1 1.8 %shard_map.105 = (bf16[512,512]{1,0:T(8,128)(2,1)S(1)}, bf16[512,512]{1,0:T(8,128)(2,1)S(1)}) custom-call(bf16[384,4096]{1,0:T(8,128)(2,1)S(1)} %get-tuple-element.83.h_ref.refs_5_.refs_6_.refs_7_.refs_8_.refs_9_.refs_2_.refs_3_.refs_1_, ...), custom_call_target="tpu_custom_call" | custom-call | flops 1 | bytes 1 | tf_op jit(solution)/shard_map/pallas_call | solution.py:125
  30.9 1.4 %collective-permute-start.4 = (bf16[512,512]{1,0:T(8,128)(2,1)S(1)}, bf16[512,512]{1,0:T(8,128)(2,1)S(1)}, u32[]{:S(2)}, u32[]{:S(2)}) collective-permute-start(bf16[512,512]{1,0:T(8,128)(2,1)S(1)} %get-tuple-element.86), channel_id=1, source_target_pairs={{0,8},{8,16},{16,24},{24,0},{1,9},{9,17},{17,25},{25,1},{2,10},{10... | collective-permute-start | bytes 1572872 | tf_op jit(solution)/shard_map/ppermute | solution.py:23
  32.2 1.5 %collective-permute-start.5 = (bf16[512,512]{1,0:T(8,128)(2,1)S(1)}, bf16[512,512]{1,0:T(8,128)(2,1)S(1)}, u32[]{:S(2)}, u32[]{:S(2)}) collective-permute-start(bf16[512,512]{1,0:T(8,128)(2,1)S(1)} %get-tuple-element.87), channel_id=1, source_target_pairs={{0,24},{8,0},{16,8},{24,16},{1,25},{9,1},{17,9},{25,17},{2,26},{10... | collective-permute-start | bytes 1572872 | tf_op jit(solution)/shard_map/ppermute | solution.py:23
  33.8 2.7 %collective-permute-start.11 = (bf16[512,512]{1,0:T(8,128)(2,1)S(1)}, bf16[512,512]{1,0:T(8,128)(2,1)S(1)}, u32[]{:S(2)}, u32[]{:S(2)}) collective-permute-start(bf16[512,512]{1,0:T(8,128)(2,1)S(1)} %shard_map.104.refs_0_), channel_id=1, source_target_pairs={{0,24},{8,0},{16,8},{24,16},{1,25},{9,1},{17,9},{25,17},{2,26},{10... | collective-permute-start | bytes 1572872 | tf_op jit(solution)/shard_map/ppermute | solution.py:23
  36.7 3.9 %collective-permute-done.8 = bf16[512,128]{1,0:T(8,128)(2,1)S(1)} collective-permute-done((bf16[512,128]{1,0:T(8,128)(2,1)S(1)}, bf16[512,128]{1,0:T(8,128)(2,1)S(1)}, u32[]{:S(2)}, u32[]{:S(2)}) %collective-permute-start.8) | collective-permute-done | bytes 131104 | tf_op jit(solution)/shard_map/ppermute | solution.py:23
  40.6 1.8 %shard_map.106 = (bf16[512,512]{1,0:T(8,128)(2,1)S(1)}, bf16[512,512]{1,0:T(8,128)(2,1)S(1)}) custom-call(bf16[384,4096]{1,0:T(8,128)(2,1)S(1)} %get-tuple-element.83.h_ref.refs_5_.refs_6_.refs_7_.refs_8_.refs_9_.refs_2_.refs_3_.refs_1_, ...), custom_call_target="tpu_custom_call" | custom-call | flops 1 | bytes 1 | tf_op jit(solution)/shard_map/pallas_call | solution.py:125
  43.6 3.0 %collective-permute-done.9 = bf16[512,128]{1,0:T(8,128)(2,1)S(1)} collective-permute-done((bf16[512,128]{1,0:T(8,128)(2,1)S(1)}, bf16[512,128]{1,0:T(8,128)(2,1)S(1)}, u32[]{:S(2)}, u32[]{:S(2)}) %collective-permute-start.9) | collective-permute-done | bytes 131104 | tf_op jit(solution)/shard_map/ppermute | solution.py:23
  46.6 3.5 %shard_map.107 = (f32[512,512]{1,0:T(8,128)S(1)}, f32[512,512]{1,0:T(8,128)S(1)}, f32[512,512]{1,0:T(8,128)S(1)}, f32[512,512]{1,0:T(8,128)S(1)}) custom-call(bf16[384,4096]{1,0:T(8,128)(2,1)S(1)} %get-tuple-element.83.h_ref.refs_5_.refs_6_.refs_7_.refs_8_.refs_9_.refs_2_.refs_3_.refs_1_, ...), custom_call_target="tpu_custom_call" | custom-call | flops 1 | bytes 1 | tf_op jit(solution)/shard_map/pallas_call | solution.py:125
  50.2 6.5 %collective-permute-done.10.refs_2_ = bf16[512,512]{1,0:T(8,128)(2,1)S(1)} collective-permute-done((bf16[512,512]{1,0:T(8,128)(2,1)S(1)}, bf16[512,512]{1,0:T(8,128)(2,1)S(1)}, u32[]{:S(2)}, u32[]{:S(2)}) %collective-permute-start.10) | collective-permute-done | bytes 524320 | tf_op jit(solution)/shard_map/ppermute | solution.py:23
  57.4 2.5 %collective-permute-start.13 = (bf16[512,128]{1,0:T(8,128)(2,1)S(1)}, bf16[512,128]{1,0:T(8,128)(2,1)S(1)}, u32[]{:S(2)}, u32[]{:S(2)}) collective-permute-start(bf16[512,128]{1,0:T(8,128)(2,1)S(1)} %add_convert_fusion.3.refs_0_), channel_id=1, source_target_pairs={{0,64},{32,96},{64,0},{96,32},{1,65},{33,97},{65,1},{97,33},{2,66}... | collective-permute-start | bytes 393224 | tf_op jit(solution)/shard_map/ppermute | solution.py:23
  60.8 1.8 %collective-permute-start.15 = (bf16[512,512]{1,0:T(8,128)(2,1)S(1)}, bf16[512,512]{1,0:T(8,128)(2,1)S(1)}, u32[]{:S(2)}, u32[]{:S(2)}) collective-permute-start(bf16[512,512]{1,0:T(8,128)(2,1)S(1)} %get-tuple-element.118), channel_id=1, source_target_pairs={{0,24},{8,0},{16,8},{24,16},{1,25},{9,1},{17,9},{25,17},{2,26},{10... | collective-permute-start | bytes 1572872 | tf_op jit(solution)/shard_map/ppermute | solution.py:23
  62.5 1.3 %collective-permute-start.18 = (bf16[512,512]{1,0:T(8,128)(2,1)S(1)}, bf16[512,512]{1,0:T(8,128)(2,1)S(1)}, u32[]{:S(2)}, u32[]{:S(2)}) collective-permute-start(bf16[512,512]{1,0:T(8,128)(2,1)S(1)} %add_convert_fusion), channel_id=1, source_target_pairs={{0,24},{8,0},{16,8},{24,16},{1,25},{9,1},{17,9},{25,17},{2,26},{10... | collective-permute-start | bytes 1572872 | tf_op jit(solution)/shard_map/ppermute | solution.py:23
  64.0 1.4 %collective-permute-start.14 = (bf16[512,128]{1,0:T(8,128)(2,1)S(1)}, bf16[512,128]{1,0:T(8,128)(2,1)S(1)}, u32[]{:S(2)}, u32[]{:S(2)}) collective-permute-start(bf16[512,128]{1,0:T(8,128)(2,1)S(1)} %add_convert_fusion.3.refs_0_), channel_id=1, source_target_pairs={{0,32},{32,64},{64,96},{96,0},{1,33},{33,65},{65,97},{97,1},{2,34}... | collective-permute-start | bytes 393224 | tf_op jit(solution)/shard_map/ppermute | solution.py:23
  65.4 2.7 %collective-permute-done.14.refs_3_ = bf16[512,128]{1,0:T(8,128)(2,1)S(1)} collective-permute-done((bf16[512,128]{1,0:T(8,128)(2,1)S(1)}, bf16[512,128]{1,0:T(8,128)(2,1)S(1)}, u32[]{:S(2)}, u32[]{:S(2)}) %collective-permute-start.14) | collective-permute-done | bytes 131104 | tf_op jit(solution)/shard_map/ppermute | solution.py:23
  69.0 2.0 %shard_map.108 = (f32[2048,128]{1,0:T(8,128)}, f32[2048,128]{1,0:T(8,128)}) custom-call(s32[1]{0:T(128)} %bitcast.20._, f32[2048,128]{1,0:T(8,128)S(1)} %bitcast.38, f32[2048,128]{1,0:T(8,128)S(1)} %bitcast.40, f32[2048,128]{1,0:T(8,128)S(1)} %bitcast.42, bf16[512,128]{1,0:T(8,128)(2,1)S(1)} %add_convert_fusion.3.refs_0_, ...), custom_call_target="tpu_custom_call" | custom-call | flops 1 | bytes 1 | tf_op jit(solution)/shard_map/pallas_call | solution.py:252
  71.0 13.4 %collective-permute-done.2.refs_0_ = bf16[256,512]{1,0:T(8,128)(2,1)S(1)} collective-permute-done((bf16[256,512]{1,0:T(8,128)(2,1)S(1)}, bf16[256,512]{1,0:T(8,128)(2,1)S(1)}, u32[]{:S(2)}, u32[]{:S(2)}) %collective-permute-start.2) | collective-permute-done | bytes 262176 | tf_op jit(solution)/shard_map/ppermute | solution.py:23
  85.8 2.8 %collective-permute-start.20 = (bf16[512,512]{1,0:T(8,128)(2,1)S(1)}, bf16[512,512]{1,0:T(8,128)(2,1)S(1)}, u32[]{:S(2)}, u32[]{:S(2)}) collective-permute-start(bf16[512,512]{1,0:T(8,128)(2,1)S(1)} %shard_map.109.refs_1_), channel_id=1, source_target_pairs={{0,24},{8,0},{16,8},{24,16},{1,25},{9,1},{17,9},{25,17},{2,26},{10... | collective-permute-start | bytes 1572872 | tf_op jit(solution)/shard_map/ppermute | solution.py:23
  88.6 3.6 %collective-permute-start.23 = (bf16[256,512]{1,0:T(8,128)(2,1)S(1)}, bf16[256,512]{1,0:T(8,128)(2,1)S(1)}, u32[]{:S(2)}, u32[]{:S(2)}) collective-permute-start(bf16[256,512]{1,0:T(8,128)(2,1)S(1)} %get-tuple-element.129), channel_id=1, source_target_pairs={{0,6},{2,0},{4,2},{6,4},{1,7},{3,1},{5,3},{7,5},{8,14},{10,8},{12,... | collective-permute-start | bytes 786440 | tf_op jit(solution)/shard_map/ppermute | solution.py:23
  92.1 4.9 %collective-permute-done.21.refs_4_ = bf16[512,512]{1,0:T(8,128)(2,1)S(1)} collective-permute-done((bf16[512,512]{1,0:T(8,128)(2,1)S(1)}, bf16[512,512]{1,0:T(8,128)(2,1)S(1)}, u32[]{:S(2)}, u32[]{:S(2)}) %collective-permute-start.21) | collective-permute-done | bytes 524320 | tf_op jit(solution)/shard_map/ppermute | solution.py:23
  97.0 2.2 %shard_map.111 = (f32[384,512]{1,0:T(8,128)S(1)}, f32[384,512]{1,0:T(8,128)S(1)}) custom-call(bf16[512,512]{1,0:T(8,128)(2,1)S(1)} %shard_map.104.refs_0_, bf16[512,512]{1,0:T(8,128)(2,1)S(1)} %shard_map.109.refs_1_, bf16[512,512]{1,0:T(8,128)(2,1)S(1)} %collective-permute-done.10.refs_2_, bf16[512,512]{1,0:T(8,128)(2,1)S(1)} %collective-permute-done.11.refs_3_, ...), custom_call_target="tpu_custom_call" | custom-call | flops 1 | bytes 1 | tf_op jit(solution)/shard_map/pallas_call | solution.py:187
  99.2 3.5 %collective-permute-done.22 = bf16[256,512]{1,0:T(8,128)(2,1)S(1)} collective-permute-done((bf16[256,512]{1,0:T(8,128)(2,1)S(1)}, bf16[256,512]{1,0:T(8,128)(2,1)S(1)}, u32[]{:S(2)}, u32[]{:S(2)}) %collective-permute-start.22) | collective-permute-done | bytes 262176 | tf_op jit(solution)/shard_map/ppermute | solution.py:23
  102.7 5.5 %collective-permute-done.19.refs_0_ = bf16[512,512]{1,0:T(8,128)(2,1)S(1)} collective-permute-done((bf16[512,512]{1,0:T(8,128)(2,1)S(1)}, bf16[512,512]{1,0:T(8,128)(2,1)S(1)}, u32[]{:S(2)}, u32[]{:S(2)}) %collective-permute-start.19) | collective-permute-done | bytes 524320 | tf_op jit(solution)/shard_map/ppermute | solution.py:23
  108.2 1.4 %collective-permute-start.24 = (bf16[512,512]{1,0:T(8,128)(2,1)S(1)}, bf16[512,512]{1,0:T(8,128)(2,1)S(1)}, u32[]{:S(2)}, u32[]{:S(2)}) collective-permute-start(bf16[512,512]{1,0:T(8,128)(2,1)S(1)} %collective-permute-done.20.refs_1_), channel_id=1, source_target_pairs={{0,24},{8,0},{16,8},{24,16},{1,25},{9,1},{17,9},{25,17},{2,26},{10... | collective-permute-start | bytes 1572872 | tf_op jit(solution)/shard_map/ppermute | solution.py:23
  111.3 13.6 %collective-permute-done.25 = bf16[256,512]{1,0:T(8,128)(2,1)S(1)} collective-permute-done((bf16[256,512]{1,0:T(8,128)(2,1)S(1)}, bf16[256,512]{1,0:T(8,128)(2,1)S(1)}, u32[]{:S(2)}, u32[]{:S(2)}) %collective-permute-start.25) | collective-permute-done | bytes 262176 | tf_op jit(solution)/shard_map/ppermute | solution.py:23
  125.5 1.9 %collective-permute-start.26 = (f32[384,512]{1,0:T(8,128)S(1)}, f32[384,512]{1,0:T(8,128)S(1)}, u32[]{:S(2)}, u32[]{:S(2)}) collective-permute-start(f32[384,512]{1,0:T(8,128)S(1)} %get-tuple-element.138), channel_id=1, source_target_pairs={{0,1},{1,0},{2,3},{3,2},{4,5},{5,4},{6,7},{7,6},{8,9},{9,8},{10,11... | collective-permute-start | bytes 2359304 | tf_op jit(solution)/shard_map/ppermute | solution.py:23
  (63 shorter events, 18.3 us)
Async XLA Ops:
  0.6 18.7 %collective-permute-start = (bf16[256,512]{1,0:T(8,128)(2,1)}, bf16[256,512]{1,0:T(8,128)(2,1)}, u32[]{:S(2)}, u32[]{:S(2)}) collective-permute-start(bf16[256,512]{1,0:T(8,128)(2,1)} %bitcast.43), channel_id=1, source_target_pairs={{0,6},{2,0},{4,2},{6,4},{1,7},{3,1},{5,3},{7,5},{8,14},{10,8},{12,... | collective-permute-start | bytes 786440 | tf_op jit(solution)/shard_map/ppermute | solution.py:23
  6.7 12.6 %collective-permute-start.1 = (bf16[256,512]{1,0:T(8,128)(2,1)}, bf16[256,512]{1,0:T(8,128)(2,1)}, u32[]{:S(2)}, u32[]{:S(2)}) collective-permute-start(bf16[256,512]{1,0:T(8,128)(2,1)} %bitcast.44), channel_id=1, source_target_pairs={{0,2},{2,4},{4,6},{6,0},{1,3},{3,5},{5,7},{7,1},{8,10},{10,12},{12... | collective-permute-start | bytes 786440 | tf_op jit(solution)/shard_map/ppermute | solution.py:23
  6.8 2.8 %copy-start = (bf16[1,384,8192]{2,1,0:T(8,128)(2,1)S(1)}, bf16[1,384,8192]{2,1,0:T(8,128)(2,1)}, u32[]{:S(2)}) copy-start(bf16[1,384,8192]{2,1,0:T(8,128)(2,1)} %param.7) | copy-start | bytes 18874372
  14.8 14.3 %copy-start.2 = (bf16[1,384,512]{2,1,0:T(8,128)(2,1)S(1)}, bf16[1,384,512]{2,1,0:T(8,128)(2,1)}, u32[]{:S(2)}) copy-start(bf16[1,384,512]{2,1,0:T(8,128)(2,1)} %param.9) | copy-start | bytes 1179652
  19.3 9.8 %collective-permute-start.3 = (bf16[384,4608]{1,0:T(8,128)(2,1)}, bf16[384,4608]{1,0:T(8,128)(2,1)S(1)}, u32[]{:S(2)}, u32[]{:S(2)}) collective-permute-start(bf16[384,4608]{1,0:T(8,128)(2,1)} %copy-done.10), channel_id=1, source_target_pairs={{0,1},{1,0},{2,3},{3,2},{4,5},{5,4},{6,7},{7,6},{8,9},{9,8},{10,11... | collective-permute-start | bytes 10616840 | tf_op jit(solution)/shard_map/ppermute | solution.py:23
  23.0 10.7 %collective-permute-start.6 = (bf16[512,128]{1,0:T(8,128)(2,1)S(1)}, bf16[512,128]{1,0:T(8,128)(2,1)S(1)}, u32[]{:S(2)}, u32[]{:S(2)}) collective-permute-start(bf16[512,128]{1,0:T(8,128)(2,1)S(1)} %get-tuple-element.89), channel_id=1, source_target_pairs={{0,32},{32,64},{64,96},{96,0},{1,33},{33,65},{65,97},{97,1},{2,34}... | collective-permute-start | bytes 393224 | tf_op jit(solution)/shard_map/ppermute | solution.py:23
  24.0 12.5 %collective-permute-start.7 = (bf16[512,128]{1,0:T(8,128)(2,1)S(1)}, bf16[512,128]{1,0:T(8,128)(2,1)S(1)}, u32[]{:S(2)}, u32[]{:S(2)}) collective-permute-start(bf16[512,128]{1,0:T(8,128)(2,1)S(1)} %get-tuple-element.90), channel_id=1, source_target_pairs={{0,64},{32,96},{64,0},{96,32},{1,65},{33,97},{65,1},{97,33},{2,66}... | collective-permute-start | bytes 393224 | tf_op jit(solution)/shard_map/ppermute | solution.py:23
  30.9 15.8 %collective-permute-start.4 = (bf16[512,512]{1,0:T(8,128)(2,1)S(1)}, bf16[512,512]{1,0:T(8,128)(2,1)S(1)}, u32[]{:S(2)}, u32[]{:S(2)}) collective-permute-start(bf16[512,512]{1,0:T(8,128)(2,1)S(1)} %get-tuple-element.86), channel_id=1, source_target_pairs={{0,8},{8,16},{16,24},{24,0},{1,9},{9,17},{17,25},{25,1},{2,10},{10... | collective-permute-start | bytes 1572872 | tf_op jit(solution)/shard_map/ppermute | solution.py:23
  32.2 14.4 %collective-permute-start.5 = (bf16[512,512]{1,0:T(8,128)(2,1)S(1)}, bf16[512,512]{1,0:T(8,128)(2,1)S(1)}, u32[]{:S(2)}, u32[]{:S(2)}) collective-permute-start(bf16[512,512]{1,0:T(8,128)(2,1)S(1)} %get-tuple-element.87), channel_id=1, source_target_pairs={{0,24},{8,0},{16,8},{24,16},{1,25},{9,1},{17,9},{25,17},{2,26},{10... | collective-permute-start | bytes 1572872 | tf_op jit(solution)/shard_map/ppermute | solution.py:23
  33.8 22.9 %collective-permute-start.10 = (bf16[512,512]{1,0:T(8,128)(2,1)S(1)}, bf16[512,512]{1,0:T(8,128)(2,1)S(1)}, u32[]{:S(2)}, u32[]{:S(2)}) collective-permute-start(bf16[512,512]{1,0:T(8,128)(2,1)S(1)} %shard_map.104.refs_0_), channel_id=1, source_target_pairs={{0,8},{8,16},{16,24},{24,0},{1,9},{9,17},{17,25},{25,1},{2,10},{10... | collective-permute-start | bytes 1572872 | tf_op jit(solution)/shard_map/ppermute | solution.py:23
  33.8 22.9 %collective-permute-start.11 = (bf16[512,512]{1,0:T(8,128)(2,1)S(1)}, bf16[512,512]{1,0:T(8,128)(2,1)S(1)}, u32[]{:S(2)}, u32[]{:S(2)}) collective-permute-start(bf16[512,512]{1,0:T(8,128)(2,1)S(1)} %shard_map.104.refs_0_), channel_id=1, source_target_pairs={{0,24},{8,0},{16,8},{24,16},{1,25},{9,1},{17,9},{25,17},{2,26},{10... | collective-permute-start | bytes 1572872 | tf_op jit(solution)/shard_map/ppermute | solution.py:23
  36.5 4.1 %collective-permute-start.8 = (bf16[512,128]{1,0:T(8,128)(2,1)S(1)}, bf16[512,128]{1,0:T(8,128)(2,1)S(1)}, u32[]{:S(2)}, u32[]{:S(2)}) collective-permute-start(bf16[512,128]{1,0:T(8,128)(2,1)S(1)} %get-tuple-element.91), channel_id=1, source_target_pairs={{0,96},{32,0},{64,32},{96,64},{1,97},{33,1},{65,33},{97,65},{2,98}... | collective-permute-start | bytes 393224 | tf_op jit(solution)/shard_map/ppermute | solution.py:23
  42.4 4.2 %collective-permute-start.9 = (bf16[512,128]{1,0:T(8,128)(2,1)S(1)}, bf16[512,128]{1,0:T(8,128)(2,1)S(1)}, u32[]{:S(2)}, u32[]{:S(2)}) collective-permute-start(bf16[512,128]{1,0:T(8,128)(2,1)S(1)} %add_convert_fusion.4), channel_id=1, source_target_pairs={{0,128},{128,0},{1,129},{129,1},{2,130},{130,2},{3,131},{131,3},{4... | collective-permute-start | bytes 393224 | tf_op jit(solution)/shard_map/ppermute | solution.py:23
  50.2 18.0 %copy-start.9 = (bf16[1,256,512]{2,1,0:T(8,128)(2,1)S(1)}, bf16[1,256,512]{2,1,0:T(8,128)(2,1)}, u32[]{:S(2)}) copy-start(bf16[1,256,512]{2,1,0:T(8,128)(2,1)} %param.8) | copy-start | bytes 786436
  50.2 18.8 %copy-start.4 = (f32[1,262144]{1,0:T(1,128)S(1)}, f32[1,262144]{1,0:T(1,128)}, u32[]{:S(2)}) copy-start(f32[1,262144]{1,0:T(1,128)} %param.10) | copy-start | bytes 3145732
  50.2 18.8 %copy-start.7 = (f32[262144]{0:T(1024)S(1)}, f32[262144]{0:T(1024)}, u32[]{:S(2)}) copy-start(f32[262144]{0:T(1024)} %param.12) | copy-start | bytes 3145732
  57.1 6.8 %collective-permute-start.12 = (bf16[512,128]{1,0:T(8,128)(2,1)S(1)}, bf16[512,128]{1,0:T(8,128)(2,1)S(1)}, u32[]{:S(2)}, u32[]{:S(2)}) collective-permute-start(bf16[512,128]{1,0:T(8,128)(2,1)S(1)} %add_convert_fusion.3.refs_0_), channel_id=1, source_target_pairs={{0,96},{32,0},{64,32},{96,64},{1,97},{33,1},{65,33},{97,65},{2,98}... | collective-permute-start | bytes 393224 | tf_op jit(solution)/shard_map/ppermute | solution.py:23
  57.4 6.6 %collective-permute-start.13 = (bf16[512,128]{1,0:T(8,128)(2,1)S(1)}, bf16[512,128]{1,0:T(8,128)(2,1)S(1)}, u32[]{:S(2)}, u32[]{:S(2)}) collective-permute-start(bf16[512,128]{1,0:T(8,128)(2,1)S(1)} %add_convert_fusion.3.refs_0_), channel_id=1, source_target_pairs={{0,64},{32,96},{64,0},{96,32},{1,65},{33,97},{65,1},{97,33},{2,66}... | collective-permute-start | bytes 393224 | tf_op jit(solution)/shard_map/ppermute | solution.py:23
  59.9 25.5 %collective-permute-start.17 = (bf16[512,512]{1,0:T(8,128)(2,1)S(1)}, bf16[512,512]{1,0:T(8,128)(2,1)S(1)}, u32[]{:S(2)}, u32[]{:S(2)}) collective-permute-start(bf16[512,512]{1,0:T(8,128)(2,1)S(1)} %get-tuple-element.97), channel_id=1, source_target_pairs={{0,8},{8,16},{16,24},{24,0},{1,9},{9,17},{17,25},{25,1},{2,10},{10... | collective-permute-start | bytes 1572872 | tf_op jit(solution)/shard_map/ppermute | solution.py:23
  60.8 24.6 %collective-permute-start.15 = (bf16[512,512]{1,0:T(8,128)(2,1)S(1)}, bf16[512,512]{1,0:T(8,128)(2,1)S(1)}, u32[]{:S(2)}, u32[]{:S(2)}) collective-permute-start(bf16[512,512]{1,0:T(8,128)(2,1)S(1)} %get-tuple-element.118), channel_id=1, source_target_pairs={{0,24},{8,0},{16,8},{24,16},{1,25},{9,1},{17,9},{25,17},{2,26},{10... | collective-permute-start | bytes 1572872 | tf_op jit(solution)/shard_map/ppermute | solution.py:23
  62.5 22.8 %collective-permute-start.18 = (bf16[512,512]{1,0:T(8,128)(2,1)S(1)}, bf16[512,512]{1,0:T(8,128)(2,1)S(1)}, u32[]{:S(2)}, u32[]{:S(2)}) collective-permute-start(bf16[512,512]{1,0:T(8,128)(2,1)S(1)} %add_convert_fusion), channel_id=1, source_target_pairs={{0,24},{8,0},{16,8},{24,16},{1,25},{9,1},{17,9},{25,17},{2,26},{10... | collective-permute-start | bytes 1572872 | tf_op jit(solution)/shard_map/ppermute | solution.py:23
  63.9 21.5 %collective-permute-start.16 = (bf16[512,512]{1,0:T(8,128)(2,1)S(1)}, bf16[512,512]{1,0:T(8,128)(2,1)S(1)}, u32[]{:S(2)}, u32[]{:S(2)}) collective-permute-start(bf16[512,512]{1,0:T(8,128)(2,1)S(1)} %add_convert_fusion.1), channel_id=1, source_target_pairs={{0,8},{8,16},{16,24},{24,0},{1,9},{9,17},{17,25},{25,1},{2,10},{10... | collective-permute-start | bytes 1572872 | tf_op jit(solution)/shard_map/ppermute | solution.py:23
  64.0 4.1 %collective-permute-start.14 = (bf16[512,128]{1,0:T(8,128)(2,1)S(1)}, bf16[512,128]{1,0:T(8,128)(2,1)S(1)}, u32[]{:S(2)}, u32[]{:S(2)}) collective-permute-start(bf16[512,128]{1,0:T(8,128)(2,1)S(1)} %add_convert_fusion.3.refs_0_), channel_id=1, source_target_pairs={{0,32},{32,64},{64,96},{96,0},{1,33},{33,65},{65,97},{97,1},{2,34}... | collective-permute-start | bytes 393224 | tf_op jit(solution)/shard_map/ppermute | solution.py:23
  68.1 16.2 %collective-permute-start.2 = (bf16[256,512]{1,0:T(8,128)(2,1)S(1)}, bf16[256,512]{1,0:T(8,128)(2,1)S(1)}, u32[]{:S(2)}, u32[]{:S(2)}) collective-permute-start(bf16[256,512]{1,0:T(8,128)(2,1)S(1)} %bitcast.46), channel_id=1, source_target_pairs={{0,4},{2,6},{4,0},{6,2},{1,5},{3,7},{5,1},{7,3},{8,12},{10,14},{12... | collective-permute-start | bytes 786440 | tf_op jit(solution)/shard_map/ppermute | solution.py:23
  84.4 12.6 %collective-permute-start.21 = (bf16[512,512]{1,0:T(8,128)(2,1)S(1)}, bf16[512,512]{1,0:T(8,128)(2,1)S(1)}, u32[]{:S(2)}, u32[]{:S(2)}) collective-permute-start(bf16[512,512]{1,0:T(8,128)(2,1)S(1)} %collective-permute-done.10.refs_2_), channel_id=1, source_target_pairs={{0,8},{8,16},{16,24},{24,0},{1,9},{9,17},{17,25},{25,1},{2,10},{10... | collective-permute-start | bytes 1572872 | tf_op jit(solution)/shard_map/ppermute | solution.py:23
  85.7 22.5 %collective-permute-start.19 = (bf16[512,512]{1,0:T(8,128)(2,1)S(1)}, bf16[512,512]{1,0:T(8,128)(2,1)S(1)}, u32[]{:S(2)}, u32[]{:S(2)}) collective-permute-start(bf16[512,512]{1,0:T(8,128)(2,1)S(1)} %shard_map.109.refs_1_), channel_id=1, source_target_pairs={{0,8},{8,16},{16,24},{24,0},{1,9},{9,17},{17,25},{25,1},{2,10},{10... | collective-permute-start | bytes 1572872 | tf_op jit(solution)/shard_map/ppermute | solution.py:23
  85.8 22.4 %collective-permute-start.20 = (bf16[512,512]{1,0:T(8,128)(2,1)S(1)}, bf16[512,512]{1,0:T(8,128)(2,1)S(1)}, u32[]{:S(2)}, u32[]{:S(2)}) collective-permute-start(bf16[512,512]{1,0:T(8,128)(2,1)S(1)} %shard_map.109.refs_1_), channel_id=1, source_target_pairs={{0,24},{8,0},{16,8},{24,16},{1,25},{9,1},{17,9},{25,17},{2,26},{10... | collective-permute-start | bytes 1572872 | tf_op jit(solution)/shard_map/ppermute | solution.py:23
  88.6 14.2 %collective-permute-start.22 = (bf16[256,512]{1,0:T(8,128)(2,1)S(1)}, bf16[256,512]{1,0:T(8,128)(2,1)S(1)}, u32[]{:S(2)}, u32[]{:S(2)}) collective-permute-start(bf16[256,512]{1,0:T(8,128)(2,1)S(1)} %get-tuple-element.123), channel_id=1, source_target_pairs={{0,2},{2,4},{4,6},{6,0},{1,3},{3,5},{5,7},{7,1},{8,10},{10,12},{12... | collective-permute-start | bytes 786440 | tf_op jit(solution)/shard_map/ppermute | solution.py:23
  88.6 14.2 %collective-permute-start.23 = (bf16[256,512]{1,0:T(8,128)(2,1)S(1)}, bf16[256,512]{1,0:T(8,128)(2,1)S(1)}, u32[]{:S(2)}, u32[]{:S(2)}) collective-permute-start(bf16[256,512]{1,0:T(8,128)(2,1)S(1)} %get-tuple-element.129), channel_id=1, source_target_pairs={{0,6},{2,0},{4,2},{6,4},{1,7},{3,1},{5,3},{7,5},{8,14},{10,8},{12,... | collective-permute-start | bytes 786440 | tf_op jit(solution)/shard_map/ppermute | solution.py:23
  108.2 16.7 %collective-permute-start.24 = (bf16[512,512]{1,0:T(8,128)(2,1)S(1)}, bf16[512,512]{1,0:T(8,128)(2,1)S(1)}, u32[]{:S(2)}, u32[]{:S(2)}) collective-permute-start(bf16[512,512]{1,0:T(8,128)(2,1)S(1)} %collective-permute-done.20.refs_1_), channel_id=1, source_target_pairs={{0,24},{8,0},{16,8},{24,16},{1,25},{9,1},{17,9},{25,17},{2,26},{10... | collective-permute-start | bytes 1572872 | tf_op jit(solution)/shard_map/ppermute | solution.py:23
  109.6 15.3 %collective-permute-start.25 = (bf16[256,512]{1,0:T(8,128)(2,1)S(1)}, bf16[256,512]{1,0:T(8,128)(2,1)S(1)}, u32[]{:S(2)}, u32[]{:S(2)}) collective-permute-start(bf16[256,512]{1,0:T(8,128)(2,1)S(1)} %get-tuple-element.131), channel_id=1, source_target_pairs={{0,4},{2,6},{4,0},{6,2},{1,5},{3,7},{5,1},{7,3},{8,12},{10,14},{12... | collective-permute-start | bytes 786440 | tf_op jit(solution)/shard_map/ppermute | solution.py:23
  125.5 3.9 %collective-permute-start.26 = (f32[384,512]{1,0:T(8,128)S(1)}, f32[384,512]{1,0:T(8,128)S(1)}, u32[]{:S(2)}, u32[]{:S(2)}) collective-permute-start(f32[384,512]{1,0:T(8,128)S(1)} %get-tuple-element.138), channel_id=1, source_target_pairs={{0,1},{1,0},{2,3},{3,2},{4,5},{5,4},{6,7},{7,6},{8,9},{9,8},{10,11... | collective-permute-start | bytes 2359304 | tf_op jit(solution)/shard_map/ppermute | solution.py:23
  (6 other events, 7.4 us)

commit v3 on v2

--- a/solution.py
+++ b/solution.py
@@ -138,20 +138,27 @@
     )(mine, theirs, cot, with_cot)
 
 
-def sums_kernel(own_01, own_23, a, b, c, d, s0, s1, s2, s3):
+def sums_kernel(own_01, own_23, a, b, c, d, up, down, own_up, own_down, own):
     f32 = jnp.float32
-    for j, out in enumerate((s0, s1, s2, s3)):
-        own, more = ((own_01, (a, b)), (own_23, (c, d)))[j // 2]
-        cut = slice((j % 2) * ROWS, (j % 2 + 1) * ROWS)
-        out[...] = (own[cut] + more[0][cut].astype(f32) + more[1][cut].astype(f32)).astype(out.dtype)
+    h = ROWS // 2
+
+    def half(j):
+        mine, more = ((own_01, (a, b)), (own_23, (c, d)))[j // 4]
+        cut = slice((j % 4) * h, (j % 4 + 1) * h)
+        return mine[cut] + more[0][cut].astype(f32) + more[1][cut].astype(f32)
+
+    own[:h], own[h:] = half(0), half(1)
+    own_up[...], own_down[...] = half(2), half(7)
+    up[:h], up[h:] = half(4).astype(up.dtype), half(3).astype(up.dtype)
+    down[:h], down[h:] = half(5).astype(down.dtype), half(6).astype(down.dtype)
 
 
 def sums_along_y(own_01, own_23, *received):
     k = own_01.shape[1]
-    dtypes = [jnp.float32] + [jnp.bfloat16] * 3
+    shapes = [(ROWS, jnp.bfloat16)] * 2 + [(ROWS // 2, jnp.float32)] * 2 + [(ROWS, jnp.float32)]
     return pl.pallas_call(
         sums_kernel,
-        out_shape=[jax.ShapeDtypeStruct((ROWS, k), d) for d in dtypes],
+        out_shape=[jax.ShapeDtypeStruct((r, k), d) for r, d in shapes],
         compiler_params=params(),
         cost_estimate=FREE,
     )(own_01, own_23, *received)
@@ -305,7 +312,7 @@
     own_a, own_b, own_01, own_23 = grads(4, [f32] * 4, in_a, in_b, from_zl)
     prev_01, next_01 = after((prev_01, next_01), own_a)
     far_01 = shift(prev_01, "y", 1)
-    in_a, in_b, next_01 = lax.optimization_barrier((in_a, in_b, next_01))
+    in_a, in_b, got_a, got_b, w_2 = lax.optimization_barrier((in_a, in_b, got_a, got_b, w_2))
     mer_a = (own_a + in_a.astype(f32)).astype(bf)
     mer_b = (own_b + in_b.astype(f32)).astype(bf)
     sum_a, sum_b = shift(mer_a, "y", 1), shift(mer_b, "y", -1)
@@ -317,16 +324,16 @@
     mixed, new_momentum = outer_step(x, replicas, local_row, global_row, momentum_row, totals)
 
     w_23 = stack_rows(*after((w_2, w_3), mixed))
-    received = after((got_a, sum_a, got_b, sum_b), w_23, mixed)
-    s0, s1, s2, s3 = sums_along_y(own_01, own_23, *received)
-    g1, g2, g3 = (shift(v, "zh", k) for v, k in ((s1, 1), (s2, 2), (s3, 3)))
-    w_23 = after(w_23, s1)
+    far_01, *received = lax.optimization_barrier((far_01, got_a, sum_a, got_b, sum_b, w_23, mixed))[:5]
+    up, down, own_up, own_down, own = sums_along_y(own_01, own_23, *received)
+    from_below, from_above = shift(up, "zh", 1), shift(down, "zh", -1)
+    w_23 = after(w_23, up)
     prev_23, next_23 = shift(w_23, "y", 1), shift(w_23, "y", -1)
 
     cols = (mine, theirs)
     acc = values_part(
         [
-            (after(w_01, s1), [(0, cols, 6)]),
+            (after(w_01, up), [(0, cols, 6)]),
             (w_23, [(0, cols, 7)]),
             (prev_01, [(0, cols, 3)]),
             (next_01, [(0, cols, 4)]),
@@ -334,13 +341,18 @@
         ],
         None,
     )
-    prev_23, next_23 = after((prev_23, next_23), acc[0], g1, g3)
+    h = ROWS // 2
+    mer_up = (own_up + from_below[:h].astype(f32)).astype(bf)
+    mer_down = (own_down + from_above[:h].astype(f32)).astype(bf)
+    top, bottom = shift(mer_up, "zh", 1), shift(mer_down, "zh", -1)
+    prev_23, next_23 = after((prev_23, next_23), acc[0], mer_up, mer_down)
     far_23 = shift(next_23, "y", -1)
     acc = values_part([(prev_23, [(0, cols, 5)]), (next_23, [(0, cols, 2)])], acc)
-    far_23, g1, g2, g3 = lax.optimization_barrier((far_23, g1, g2, g3))
+    far_23, top, bottom = lax.optimization_barrier((far_23, top, bottom))
     ours, other = values_part([(far_23, [(0, cols, 1)])], acc)
     back = shift(other, "core", 1)
-    grad_rows = s0 + g1.astype(f32) + g2.astype(f32) + g3.astype(f32)
+    direct = jnp.concatenate([from_above[h:], from_below[h:]]).astype(f32)
+    grad_rows = own + direct + jnp.concatenate([top, bottom]).astype(f32)
     values = (ours + back).astype(bf)
 
     return (values[None], grad_rows[None], mixed.reshape(1, -1), new_momentum.reshape(-1))

time: 132 us -> 128 us (0.970); the launches traced: 130 us -> 128 us
  waiting for transfers between devices: 60.7 us -> 49.5 us
  starting transfers between devices: 37.9 us -> 47.7 us
    ppermute x27 -> x28, waiting for transfers between devices: 60.7 us -> 49.5 us  [shift(): return lax.ppermute(v, axis, [(i, (i + k) % n) for i in range(n)])]
    ppermute x27 -> x28, starting transfers between devices: 37.9 us -> 47.7 us  [shift(): return lax.ppermute(v, axis, [(i, (i + k) % n) for i in range(n)])]
    unnamed x22 -> x18, local copies, waits for them, and re-layouts: 10.2 us -> 9.26 us
  transfers between devices with their start and end apart: 27 -> 28, of which waited for: 11 -> 16; matrix products, arithmetic and copies ran while one was open for 1% -> 1% of each run, Pallas kernels for 14% -> 12%
where the time goes in v3:
time: 128 us
  waiting for transfers between devices  49.5 us (39%)
  starting transfers between devices  47.7 us (37%)
  Pallas kernels  18.3 us (14%)
  local copies, waits for them, and re-layouts  9.37 us (7%)
  other arithmetic  2.22 us (2%)
    ppermute x28, waiting for transfers between devices, shift(): return lax.ppermute(v, axis, [(i, (i + k) % n) for i in range(n)])  49.5 us
    ppermute x28, starting transfers between devices, shift(): return lax.ppermute(v, axis, [(i, (i + k) % n) for i in range(n)])  47.7 us
    unnamed x18, local copies, waits for them, and re-layouts  9.26 us
    pallas_call x3, Pallas kernels, grad_rows_of(): pl.pallas_call(grad_kernel, grid=(len(dtypes),), in_specs=[column, column...  7.03 us
    pallas_call x3, Pallas kernels, values_part(): pl.pallas_call(functools.partial(values_kernel, cuts, bool(acc)), grid=(1...  3.72 us
  transfers between devices with their start and end apart: 28, of which 16 were waited for; matrix products, arithmetic and copies ran while one was open for 1% of the time, Pallas kernels for 12%

profile of v3, /device:TPU:5, one launch (start us, length us, event | category | flops | bytes accessed | tf_op | source)
XLA Modules:
  0.0 128.0 jit_solution(5315472001385188625)
XLA Ops:
  0.6 3.1 %collective-permute-start.1 = (bf16[256,512]{1,0:T(8,128)(2,1)}, bf16[256,512]{1,0:T(8,128)(2,1)}, u32[]{:S(2)}, u32[]{:S(2)}) collective-permute-start(bf16[256,512]{1,0:T(8,128)(2,1)} %bitcast.19.refs_0_), channel_id=1, source_target_pairs={{0,2},{2,4},{4,6},{6,0},{1,3},{3,5},{5,7},{7,1},{8,10},{10,12},{12... | collective-permute-start | bytes 786440 | tf_op jit(solution)/shard_map/ppermute | solution.py:23
  3.7 3.1 %collective-permute-start = (bf16[256,512]{1,0:T(8,128)(2,1)}, bf16[256,512]{1,0:T(8,128)(2,1)}, u32[]{:S(2)}, u32[]{:S(2)}) collective-permute-start(bf16[256,512]{1,0:T(8,128)(2,1)} %bitcast.19.refs_0_), channel_id=1, source_target_pairs={{0,6},{2,0},{4,2},{6,4},{1,7},{3,1},{5,3},{7,5},{8,14},{10,8},{12,... | collective-permute-start | bytes 786440 | tf_op jit(solution)/shard_map/ppermute | solution.py:23
  6.9 2.8 %copy-done = bf16[1,384,8192]{2,1,0:T(8,128)(2,1)S(1)} copy-done((bf16[1,384,8192]{2,1,0:T(8,128)(2,1)S(1)}, bf16[1,384,8192]{2,1,0:T(8,128)(2,1)}, u32[]{:S(2)}) %copy-start) | copy-done | bytes 6291480
  10.7 2.4 %shard_map.102 = (bf16[384,4096]{1,0:T(8,128)(2,1)S(1)}, bf16[384,4608]{1,0:T(8,128)(2,1)S(1)}) custom-call(s32[17]{0:T(128)S(1)} %stack.71.s_ref, bf16[384,8192]{1,0:T(8,128)(2,1)S(1)} %bitcast.31, bf16[384,8192]{1,0:T(8,128)(2,1)S(1)} %bitcast.32, bf16[384,512]{1,0:T(8,128)(2,1)S(1)} %bitcast.33), custom_call_target="tpu_custom_call" | custom-call | flops 1 | bytes 1 | tf_op jit(solution)/shard_map/pallas_call | solution.py:69
  13.2 1.7 %copy-done.8 = bf16[384,4608]{1,0:T(8,128)(2,1)} copy-done((bf16[384,4608]{1,0:T(8,128)(2,1)}, bf16[384,4608]{1,0:T(8,128)(2,1)S(1)}, u32[]{:S(2)}) %copy-start.8) | copy-done | bytes 3538968
  22.2 5.0 %collective-permute-done.2.hr_ref.gp_ref.refs_10_.refs_11_.refs_12_.refs_13_.refs_14_.refs_4_.refs_5_.refs_2_ = bf16[384,4608]{1,0:T(8,128)(2,1)S(1)} collective-permute-done((bf16[384,4608]{1,0:T(8,128)(2,1)}, bf16[384,4608]{1,0:T(8,128)(2,1)S(1)}, u32[]{:S(2)}, u32[]{:S(2)}) %collective-permute-start.2) | collective-permute-done | bytes 3538976 | tf_op jit(solution)/shard_map/ppermute | solution.py:23
  27.2 1.8 %shard_map.105 = (bf16[512,512]{1,0:T(8,128)(2,1)S(1)}, bf16[512,512]{1,0:T(8,128)(2,1)S(1)}) custom-call(bf16[384,4096]{1,0:T(8,128)(2,1)S(1)} %get-tuple-element.83.h_ref.refs_5_.refs_6_.refs_7_.refs_8_.refs_9_.refs_2_.refs_3_.refs_1_, ...), custom_call_target="tpu_custom_call" | custom-call | flops 1 | bytes 1 | tf_op jit(solution)/shard_map/pallas_call | solution.py:125
  28.9 2.8 %collective-permute-start.4 = (bf16[512,512]{1,0:T(8,128)(2,1)S(1)}, bf16[512,512]{1,0:T(8,128)(2,1)S(1)}, u32[]{:S(2)}, u32[]{:S(2)}) collective-permute-start(bf16[512,512]{1,0:T(8,128)(2,1)S(1)} %get-tuple-element.88), channel_id=1, source_target_pairs={{0,24},{8,0},{16,8},{24,16},{1,25},{9,1},{17,9},{25,17},{2,26},{10... | collective-permute-start | bytes 1572872 | tf_op jit(solution)/shard_map/ppermute | solution.py:23
  34.1 2.1 %collective-permute-done.5 = bf16[512,128]{1,0:T(8,128)(2,1)S(1)} collective-permute-done((bf16[512,128]{1,0:T(8,128)(2,1)S(1)}, bf16[512,128]{1,0:T(8,128)(2,1)S(1)}, u32[]{:S(2)}, u32[]{:S(2)}) %collective-permute-start.5) | collective-permute-done | bytes 131104 | tf_op jit(solution)/shard_map/ppermute | solution.py:23
  36.1 2.8 %collective-permute-done.6 = bf16[512,128]{1,0:T(8,128)(2,1)S(1)} collective-permute-done((bf16[512,128]{1,0:T(8,128)(2,1)S(1)}, bf16[512,128]{1,0:T(8,128)(2,1)S(1)}, u32[]{:S(2)}, u32[]{:S(2)}) %collective-permute-start.6) | collective-permute-done | bytes 131104 | tf_op jit(solution)/shard_map/ppermute | solution.py:23
  39.0 1.6 %collective-permute-done.7 = bf16[512,128]{1,0:T(8,128)(2,1)S(1)} collective-permute-done((bf16[512,128]{1,0:T(8,128)(2,1)S(1)}, bf16[512,128]{1,0:T(8,128)(2,1)S(1)}, u32[]{:S(2)}, u32[]{:S(2)}) %collective-permute-start.7) | collective-permute-done | bytes 131104 | tf_op jit(solution)/shard_map/ppermute | solution.py:23
  40.5 1.8 %shard_map.106 = (bf16[512,512]{1,0:T(8,128)(2,1)S(1)}, bf16[512,512]{1,0:T(8,128)(2,1)S(1)}) custom-call(bf16[384,4096]{1,0:T(8,128)(2,1)S(1)} %get-tuple-element.83.h_ref.refs_5_.refs_6_.refs_7_.refs_8_.refs_9_.refs_2_.refs_3_.refs_1_, ...), custom_call_target="tpu_custom_call" | custom-call | flops 1 | bytes 1 | tf_op jit(solution)/shard_map/pallas_call | solution.py:125
  42.4 2.7 %collective-permute-start.9 = (bf16[512,512]{1,0:T(8,128)(2,1)S(1)}, bf16[512,512]{1,0:T(8,128)(2,1)S(1)}, u32[]{:S(2)}, u32[]{:S(2)}) collective-permute-start(bf16[512,512]{1,0:T(8,128)(2,1)S(1)} %get-tuple-element.105), channel_id=1, source_target_pairs={{0,24},{8,0},{16,8},{24,16},{1,25},{9,1},{17,9},{25,17},{2,26},{10... | collective-permute-start | bytes 1572872 | tf_op jit(solution)/shard_map/ppermute | solution.py:23
  45.3 4.1 %collective-permute-done.8 = bf16[512,128]{1,0:T(8,128)(2,1)S(1)} collective-permute-done((bf16[512,128]{1,0:T(8,128)(2,1)S(1)}, bf16[512,128]{1,0:T(8,128)(2,1)S(1)}, u32[]{:S(2)}, u32[]{:S(2)}) %collective-permute-start.8) | collective-permute-done | bytes 131104 | tf_op jit(solution)/shard_map/ppermute | solution.py:23
  49.3 4.0 %collective-permute-start.11 = (bf16[256,512]{1,0:T(8,128)(2,1)}, bf16[256,512]{1,0:T(8,128)(2,1)S(1)}, u32[]{:S(2)}, u32[]{:S(2)}) collective-permute-start(bf16[256,512]{1,0:T(8,128)(2,1)} %bitcast.19.refs_0_), channel_id=1, source_target_pairs={{0,4},{2,6},{4,0},{6,2},{1,5},{3,7},{5,1},{7,3},{8,12},{10,14},{12... | collective-permute-start | bytes 786440 | tf_op jit(solution)/shard_map/ppermute | solution.py:23
  54.8 3.5 %shard_map.107 = (f32[512,512]{1,0:T(8,128)S(1)}, f32[512,512]{1,0:T(8,128)S(1)}, f32[512,512]{1,0:T(8,128)S(1)}, f32[512,512]{1,0:T(8,128)S(1)}) custom-call(bf16[384,4096]{1,0:T(8,128)(2,1)S(1)} %get-tuple-element.83.h_ref.refs_5_.refs_6_.refs_7_.refs_8_.refs_9_.refs_2_.refs_3_.refs_1_, ...), custom_call_target="tpu_custom_call" | custom-call | flops 1 | bytes 1 | tf_op jit(solution)/shard_map/pallas_call | solution.py:125
  58.3 2.7 %collective-permute-done.11.refs_0_ = bf16[256,512]{1,0:T(8,128)(2,1)S(1)} collective-permute-done((bf16[256,512]{1,0:T(8,128)(2,1)}, bf16[256,512]{1,0:T(8,128)(2,1)S(1)}, u32[]{:S(2)}, u32[]{:S(2)}) %collective-permute-start.11) | collective-permute-done | bytes 262176 | tf_op jit(solution)/shard_map/ppermute | solution.py:23
  61.2 4.1 %collective-permute-done.16.refs_3_ = bf16[512,512]{1,0:T(8,128)(2,1)S(1)} collective-permute-done((bf16[512,512]{1,0:T(8,128)(2,1)S(1)}, bf16[512,512]{1,0:T(8,128)(2,1)S(1)}, u32[]{:S(2)}, u32[]{:S(2)}) %collective-permute-start.16) | collective-permute-done | bytes 524320 | tf_op jit(solution)/shard_map/ppermute | solution.py:23
  66.9 2.1 %collective-permute-start.19 = (bf16[512,512]{1,0:T(8,128)(2,1)S(1)}, bf16[512,512]{1,0:T(8,128)(2,1)S(1)}, u32[]{:S(2)}, u32[]{:S(2)}) collective-permute-start(bf16[512,512]{1,0:T(8,128)(2,1)S(1)} %add_convert_fusion), channel_id=1, source_target_pairs={{0,24},{8,0},{16,8},{24,16},{1,25},{9,1},{17,9},{25,17},{2,26},{10... | collective-permute-start | bytes 1572872 | tf_op jit(solution)/shard_map/ppermute | solution.py:23
  69.0 2.2 %collective-permute-start.14 = (bf16[512,128]{1,0:T(8,128)(2,1)S(1)}, bf16[512,128]{1,0:T(8,128)(2,1)S(1)}, u32[]{:S(2)}, u32[]{:S(2)}) collective-permute-start(bf16[512,128]{1,0:T(8,128)(2,1)S(1)} %add_convert_fusion.5.refs_0_), channel_id=1, source_target_pairs={{0,32},{32,64},{64,96},{96,0},{1,33},{33,65},{65,97},{97,1},{2,34}... | collective-permute-start | bytes 393224 | tf_op jit(solution)/shard_map/ppermute | solution.py:23
  73.2 1.5 %collective-permute-start.12 = (bf16[512,128]{1,0:T(8,128)(2,1)S(1)}, bf16[512,128]{1,0:T(8,128)(2,1)S(1)}, u32[]{:S(2)}, u32[]{:S(2)}) collective-permute-start(bf16[512,128]{1,0:T(8,128)(2,1)S(1)} %add_convert_fusion.5.refs_0_), channel_id=1, source_target_pairs={{0,96},{32,0},{64,32},{96,64},{1,97},{33,1},{65,33},{97,65},{2,98}... | collective-permute-start | bytes 393224 | tf_op jit(solution)/shard_map/ppermute | solution.py:23
  74.7 2.2 %collective-permute-done.13.refs_2_ = bf16[512,128]{1,0:T(8,128)(2,1)S(1)} collective-permute-done((bf16[512,128]{1,0:T(8,128)(2,1)S(1)}, bf16[512,128]{1,0:T(8,128)(2,1)S(1)}, u32[]{:S(2)}, u32[]{:S(2)}) %collective-permute-start.13) | collective-permute-done | bytes 131104 | tf_op jit(solution)/shard_map/ppermute | solution.py:23
  78.0 2.0 %shard_map.108 = (f32[2048,128]{1,0:T(8,128)}, f32[2048,128]{1,0:T(8,128)}) custom-call(s32[1]{0:T(128)} %bitcast.20._, f32[2048,128]{1,0:T(8,128)S(1)} %bitcast.38, f32[2048,128]{1,0:T(8,128)S(1)} %bitcast.40, f32[2048,128]{1,0:T(8,128)S(1)} %bitcast.42, bf16[512,128]{1,0:T(8,128)(2,1)S(1)} %add_convert_fusion.5.refs_0_, ...), custom_call_target="tpu_custom_call" | custom-call | flops 1 | bytes 1 | tf_op jit(solution)/shard_map/pallas_call | solution.py:259
  81.1 6.9 %collective-permute-done.18.b = bf16[512,512]{1,0:T(8,128)(2,1)S(1)} collective-permute-done((bf16[512,512]{1,0:T(8,128)(2,1)S(1)}, bf16[512,512]{1,0:T(8,128)(2,1)S(1)}, u32[]{:S(2)}, u32[]{:S(2)}) %collective-permute-start.18) | collective-permute-done | bytes 524320 | tf_op jit(solution)/shard_map/ppermute | solution.py:23
  88.3 1.7 %collective-permute-start.23 = (bf16[256,512]{1,0:T(8,128)(2,1)S(1)}, bf16[256,512]{1,0:T(8,128)(2,1)S(1)}, u32[]{:S(2)}, u32[]{:S(2)}) collective-permute-start(bf16[256,512]{1,0:T(8,128)(2,1)S(1)} %get-tuple-element.137), channel_id=1, source_target_pairs={{0,6},{2,0},{4,2},{6,4},{1,7},{3,1},{5,3},{7,5},{8,14},{10,8},{12,... | collective-permute-start | bytes 786440 | tf_op jit(solution)/shard_map/ppermute | solution.py:23
  89.9 2.1 %collective-permute-start.21 = (bf16[512,512]{1,0:T(8,128)(2,1)S(1)}, bf16[512,512]{1,0:T(8,128)(2,1)S(1)}, u32[]{:S(2)}, u32[]{:S(2)}) collective-permute-start(bf16[512,512]{1,0:T(8,128)(2,1)S(1)} %shard_map.109.refs_1_), channel_id=1, source_target_pairs={{0,24},{8,0},{16,8},{24,16},{1,25},{9,1},{17,9},{25,17},{2,26},{10... | collective-permute-start | bytes 1572872 | tf_op jit(solution)/shard_map/ppermute | solution.py:23
  92.0 4.3 %collective-permute-start.22 = (bf16[256,512]{1,0:T(8,128)(2,1)S(1)}, bf16[256,512]{1,0:T(8,128)(2,1)S(1)}, u32[]{:S(2)}, u32[]{:S(2)}) collective-permute-start(bf16[256,512]{1,0:T(8,128)(2,1)S(1)} %get-tuple-element.129), channel_id=1, source_target_pairs={{0,2},{2,4},{4,6},{6,0},{1,3},{3,5},{5,7},{7,1},{8,10},{10,12},{12... | collective-permute-start | bytes 786440 | tf_op jit(solution)/shard_map/ppermute | solution.py:23
  96.4 2.2 %shard_map.111 = (f32[384,512]{1,0:T(8,128)S(1)}, f32[384,512]{1,0:T(8,128)S(1)}) custom-call(bf16[512,512]{1,0:T(8,128)(2,1)S(1)} %shard_map.104.refs_0_, bf16[512,512]{1,0:T(8,128)(2,1)S(1)} %shard_map.109.refs_1_, bf16[512,512]{1,0:T(8,128)(2,1)S(1)} %collective-permute-done.15.refs_2_, bf16[512,512]{1,0:T(8,128)(2,1)S(1)} %collective-permute-done.16.refs_3_, ...), custom_call_target="tpu_custom_call" | custom-call | flops 1 | bytes 1 | tf_op jit(solution)/shard_map/pallas_call | solution.py:194
  98.5 8.0 %collective-permute-done.23 = bf16[256,512]{1,0:T(8,128)(2,1)S(1)} collective-permute-done((bf16[256,512]{1,0:T(8,128)(2,1)S(1)}, bf16[256,512]{1,0:T(8,128)(2,1)S(1)}, u32[]{:S(2)}, u32[]{:S(2)}) %collective-permute-start.23) | collective-permute-done | bytes 262176 | tf_op jit(solution)/shard_map/ppermute | solution.py:23
  106.8 4.0 %collective-permute-start.25 = (bf16[128,512]{1,0:T(8,128)(2,1)S(1)}, bf16[128,512]{1,0:T(8,128)(2,1)S(1)}, u32[]{:S(2)}, u32[]{:S(2)}) collective-permute-start(bf16[128,512]{1,0:T(8,128)(2,1)S(1)} %add_convert_fusion.4), channel_id=1, source_target_pairs={{0,2},{2,4},{4,6},{6,0},{1,3},{3,5},{5,7},{7,1},{8,10},{10,12},{12... | collective-permute-start | bytes 393224 | tf_op jit(solution)/shard_map/ppermute | solution.py:23
  113.3 4.2 %collective-permute-done.25 = bf16[128,512]{1,0:T(8,128)(2,1)S(1)} collective-permute-done((bf16[128,512]{1,0:T(8,128)(2,1)S(1)}, bf16[128,512]{1,0:T(8,128)(2,1)S(1)}, u32[]{:S(2)}, u32[]{:S(2)}) %collective-permute-start.25) | collective-permute-done | bytes 131104 | tf_op jit(solution)/shard_map/ppermute | solution.py:23
  118.1 7.1 %collective-permute-start.27 = (f32[384,512]{1,0:T(8,128)S(1)}, f32[384,512]{1,0:T(8,128)S(1)}, u32[]{:S(2)}, u32[]{:S(2)}) collective-permute-start(f32[384,512]{1,0:T(8,128)S(1)} %get-tuple-element.145), channel_id=1, source_target_pairs={{0,1},{1,0},{2,3},{3,2},{4,5},{5,4},{6,7},{7,6},{8,9},{9,8},{10,11... | collective-permute-start | bytes 2359304 | tf_op jit(solution)/shard_map/ppermute | solution.py:23
  (65 shorter events, 24.6 us)
Async XLA Ops:
  0.6 18.8 %collective-permute-start.1 = (bf16[256,512]{1,0:T(8,128)(2,1)}, bf16[256,512]{1,0:T(8,128)(2,1)}, u32[]{:S(2)}, u32[]{:S(2)}) collective-permute-start(bf16[256,512]{1,0:T(8,128)(2,1)} %bitcast.19.refs_0_), channel_id=1, source_target_pairs={{0,2},{2,4},{4,6},{6,0},{1,3},{3,5},{5,7},{7,1},{8,10},{10,12},{12... | collective-permute-start | bytes 786440 | tf_op jit(solution)/shard_map/ppermute | solution.py:23
  3.7 16.5 %collective-permute-start = (bf16[256,512]{1,0:T(8,128)(2,1)}, bf16[256,512]{1,0:T(8,128)(2,1)}, u32[]{:S(2)}, u32[]{:S(2)}) collective-permute-start(bf16[256,512]{1,0:T(8,128)(2,1)} %bitcast.19.refs_0_), channel_id=1, source_target_pairs={{0,6},{2,0},{4,2},{6,4},{1,7},{3,1},{5,3},{7,5},{8,14},{10,8},{12,... | collective-permute-start | bytes 786440 | tf_op jit(solution)/shard_map/ppermute | solution.py:23
  6.9 2.8 %copy-start = (bf16[1,384,8192]{2,1,0:T(8,128)(2,1)S(1)}, bf16[1,384,8192]{2,1,0:T(8,128)(2,1)}, u32[]{:S(2)}) copy-start(bf16[1,384,8192]{2,1,0:T(8,128)(2,1)} %param.7) | copy-start | bytes 18874372
  14.9 12.3 %copy-start.2 = (bf16[1,384,512]{2,1,0:T(8,128)(2,1)S(1)}, bf16[1,384,512]{2,1,0:T(8,128)(2,1)}, u32[]{:S(2)}) copy-start(bf16[1,384,512]{2,1,0:T(8,128)(2,1)} %param.9) | copy-start | bytes 1179652
  20.2 7.0 %collective-permute-start.2 = (bf16[384,4608]{1,0:T(8,128)(2,1)}, bf16[384,4608]{1,0:T(8,128)(2,1)S(1)}, u32[]{:S(2)}, u32[]{:S(2)}) collective-permute-start(bf16[384,4608]{1,0:T(8,128)(2,1)} %copy-done.8), channel_id=1, source_target_pairs={{0,1},{1,0},{2,3},{3,2},{4,5},{5,4},{6,7},{7,6},{8,9},{9,8},{10,11... | collective-permute-start | bytes 10616840 | tf_op jit(solution)/shard_map/ppermute | solution.py:23
  28.9 24.3 %collective-permute-start.4 = (bf16[512,512]{1,0:T(8,128)(2,1)S(1)}, bf16[512,512]{1,0:T(8,128)(2,1)S(1)}, u32[]{:S(2)}, u32[]{:S(2)}) collective-permute-start(bf16[512,512]{1,0:T(8,128)(2,1)S(1)} %get-tuple-element.88), channel_id=1, source_target_pairs={{0,24},{8,0},{16,8},{24,16},{1,25},{9,1},{17,9},{25,17},{2,26},{10... | collective-permute-start | bytes 1572872 | tf_op jit(solution)/shard_map/ppermute | solution.py:23
  31.8 22.7 %collective-permute-start.3 = (bf16[512,512]{1,0:T(8,128)(2,1)S(1)}, bf16[512,512]{1,0:T(8,128)(2,1)S(1)}, u32[]{:S(2)}, u32[]{:S(2)}) collective-permute-start(bf16[512,512]{1,0:T(8,128)(2,1)S(1)} %get-tuple-element.87), channel_id=1, source_target_pairs={{0,8},{8,16},{16,24},{24,0},{1,9},{9,17},{17,25},{25,1},{2,10},{10... | collective-permute-start | bytes 1572872 | tf_op jit(solution)/shard_map/ppermute | solution.py:23
  31.8 4.4 %collective-permute-start.5 = (bf16[512,128]{1,0:T(8,128)(2,1)S(1)}, bf16[512,128]{1,0:T(8,128)(2,1)S(1)}, u32[]{:S(2)}, u32[]{:S(2)}) collective-permute-start(bf16[512,128]{1,0:T(8,128)(2,1)S(1)} %get-tuple-element.90), channel_id=1, source_target_pairs={{0,32},{32,64},{64,96},{96,0},{1,33},{33,65},{65,97},{97,1},{2,34}... | collective-permute-start | bytes 393224 | tf_op jit(solution)/shard_map/ppermute | solution.py:23
  32.7 6.3 %collective-permute-start.6 = (bf16[512,128]{1,0:T(8,128)(2,1)S(1)}, bf16[512,128]{1,0:T(8,128)(2,1)S(1)}, u32[]{:S(2)}, u32[]{:S(2)}) collective-permute-start(bf16[512,128]{1,0:T(8,128)(2,1)S(1)} %get-tuple-element.91), channel_id=1, source_target_pairs={{0,64},{32,96},{64,0},{96,32},{1,65},{33,97},{65,1},{97,33},{2,66}... | collective-permute-start | bytes 393224 | tf_op jit(solution)/shard_map/ppermute | solution.py:23
  33.2 7.3 %collective-permute-start.7 = (bf16[512,128]{1,0:T(8,128)(2,1)S(1)}, bf16[512,128]{1,0:T(8,128)(2,1)S(1)}, u32[]{:S(2)}, u32[]{:S(2)}) collective-permute-start(bf16[512,128]{1,0:T(8,128)(2,1)S(1)} %get-tuple-element.92), channel_id=1, source_target_pairs={{0,96},{32,0},{64,32},{96,64},{1,97},{33,1},{65,33},{97,65},{2,98}... | collective-permute-start | bytes 393224 | tf_op jit(solution)/shard_map/ppermute | solution.py:23
  42.3 18.8 %collective-permute-start.10 = (bf16[512,512]{1,0:T(8,128)(2,1)S(1)}, bf16[512,512]{1,0:T(8,128)(2,1)S(1)}, u32[]{:S(2)}, u32[]{:S(2)}) collective-permute-start(bf16[512,512]{1,0:T(8,128)(2,1)S(1)} %get-tuple-element.98), channel_id=1, source_target_pairs={{0,8},{8,16},{16,24},{24,0},{1,9},{9,17},{17,25},{25,1},{2,10},{10... | collective-permute-start | bytes 1572872 | tf_op jit(solution)/shard_map/ppermute | solution.py:23
  42.4 18.7 %collective-permute-start.9 = (bf16[512,512]{1,0:T(8,128)(2,1)S(1)}, bf16[512,512]{1,0:T(8,128)(2,1)S(1)}, u32[]{:S(2)}, u32[]{:S(2)}) collective-permute-start(bf16[512,512]{1,0:T(8,128)(2,1)S(1)} %get-tuple-element.105), channel_id=1, source_target_pairs={{0,24},{8,0},{16,8},{24,16},{1,25},{9,1},{17,9},{25,17},{2,26},{10... | collective-permute-start | bytes 1572872 | tf_op jit(solution)/shard_map/ppermute | solution.py:23
  45.1 4.2 %collective-permute-start.8 = (bf16[512,128]{1,0:T(8,128)(2,1)S(1)}, bf16[512,128]{1,0:T(8,128)(2,1)S(1)}, u32[]{:S(2)}, u32[]{:S(2)}) collective-permute-start(bf16[512,128]{1,0:T(8,128)(2,1)S(1)} %add_convert_fusion.6), channel_id=1, source_target_pairs={{0,128},{128,0},{1,129},{129,1},{2,130},{130,2},{3,131},{131,3},{4... | collective-permute-start | bytes 393224 | tf_op jit(solution)/shard_map/ppermute | solution.py:23
  49.3 11.7 %collective-permute-start.11 = (bf16[256,512]{1,0:T(8,128)(2,1)}, bf16[256,512]{1,0:T(8,128)(2,1)S(1)}, u32[]{:S(2)}, u32[]{:S(2)}) collective-permute-start(bf16[256,512]{1,0:T(8,128)(2,1)} %bitcast.19.refs_0_), channel_id=1, source_target_pairs={{0,4},{2,6},{4,0},{6,2},{1,5},{3,7},{5,1},{7,3},{8,12},{10,14},{12... | collective-permute-start | bytes 786440 | tf_op jit(solution)/shard_map/ppermute | solution.py:23
  53.3 12.0 %collective-permute-start.16 = (bf16[512,512]{1,0:T(8,128)(2,1)S(1)}, bf16[512,512]{1,0:T(8,128)(2,1)S(1)}, u32[]{:S(2)}, u32[]{:S(2)}) collective-permute-start(bf16[512,512]{1,0:T(8,128)(2,1)S(1)} %shard_map.104.refs_0_), channel_id=1, source_target_pairs={{0,24},{8,0},{16,8},{24,16},{1,25},{9,1},{17,9},{25,17},{2,26},{10... | collective-permute-start | bytes 1572872 | tf_op jit(solution)/shard_map/ppermute | solution.py:23
  54.5 10.9 %collective-permute-start.15 = (bf16[512,512]{1,0:T(8,128)(2,1)S(1)}, bf16[512,512]{1,0:T(8,128)(2,1)S(1)}, u32[]{:S(2)}, u32[]{:S(2)}) collective-permute-start(bf16[512,512]{1,0:T(8,128)(2,1)S(1)} %shard_map.104.refs_0_), channel_id=1, source_target_pairs={{0,8},{8,16},{16,24},{24,0},{1,9},{9,17},{17,25},{25,1},{2,10},{10... | collective-permute-start | bytes 1572872 | tf_op jit(solution)/shard_map/ppermute | solution.py:23
  58.3 19.7 %copy-start.4 = (f32[1,262144]{1,0:T(1,128)S(1)}, f32[1,262144]{1,0:T(1,128)}, u32[]{:S(2)}) copy-start(f32[1,262144]{1,0:T(1,128)} %param.10) | copy-start | bytes 3145732
  58.3 19.7 %copy-start.7 = (f32[262144]{0:T(1024)S(1)}, f32[262144]{0:T(1024)}, u32[]{:S(2)}) copy-start(f32[262144]{0:T(1024)} %param.12) | copy-start | bytes 3145732
  65.3 15.7 %collective-permute-start.17 = (bf16[512,512]{1,0:T(8,128)(2,1)S(1)}, bf16[512,512]{1,0:T(8,128)(2,1)S(1)}, u32[]{:S(2)}, u32[]{:S(2)}) collective-permute-start(bf16[512,512]{1,0:T(8,128)(2,1)S(1)} %collective-permute-done.15.refs_2_), channel_id=1, source_target_pairs={{0,8},{8,16},{16,24},{24,0},{1,9},{9,17},{17,25},{25,1},{2,10},{10... | collective-permute-start | bytes 1572872 | tf_op jit(solution)/shard_map/ppermute | solution.py:23
  66.9 14.2 %collective-permute-start.19 = (bf16[512,512]{1,0:T(8,128)(2,1)S(1)}, bf16[512,512]{1,0:T(8,128)(2,1)S(1)}, u32[]{:S(2)}, u32[]{:S(2)}) collective-permute-start(bf16[512,512]{1,0:T(8,128)(2,1)S(1)} %add_convert_fusion), channel_id=1, source_target_pairs={{0,24},{8,0},{16,8},{24,16},{1,25},{9,1},{17,9},{25,17},{2,26},{10... | collective-permute-start | bytes 1572872 | tf_op jit(solution)/shard_map/ppermute | solution.py:23
  69.0 19.0 %collective-permute-start.18 = (bf16[512,512]{1,0:T(8,128)(2,1)S(1)}, bf16[512,512]{1,0:T(8,128)(2,1)S(1)}, u32[]{:S(2)}, u32[]{:S(2)}) collective-permute-start(bf16[512,512]{1,0:T(8,128)(2,1)S(1)} %add_convert_fusion.1), channel_id=1, source_target_pairs={{0,8},{8,16},{16,24},{24,0},{1,9},{9,17},{17,25},{25,1},{2,10},{10... | collective-permute-start | bytes 1572872 | tf_op jit(solution)/shard_map/ppermute | solution.py:23
  69.0 4.2 %collective-permute-start.14 = (bf16[512,128]{1,0:T(8,128)(2,1)S(1)}, bf16[512,128]{1,0:T(8,128)(2,1)S(1)}, u32[]{:S(2)}, u32[]{:S(2)}) collective-permute-start(bf16[512,128]{1,0:T(8,128)(2,1)S(1)} %add_convert_fusion.5.refs_0_), channel_id=1, source_target_pairs={{0,32},{32,64},{64,96},{96,0},{1,33},{33,65},{65,97},{97,1},{2,34}... | collective-permute-start | bytes 393224 | tf_op jit(solution)/shard_map/ppermute | solution.py:23
  71.3 5.6 %collective-permute-start.13 = (bf16[512,128]{1,0:T(8,128)(2,1)S(1)}, bf16[512,128]{1,0:T(8,128)(2,1)S(1)}, u32[]{:S(2)}, u32[]{:S(2)}) collective-permute-start(bf16[512,128]{1,0:T(8,128)(2,1)S(1)} %add_convert_fusion.5.refs_0_), channel_id=1, source_target_pairs={{0,64},{32,96},{64,0},{96,32},{1,65},{33,97},{65,1},{97,33},{2,66}... | collective-permute-start | bytes 393224 | tf_op jit(solution)/shard_map/ppermute | solution.py:23
  73.2 4.8 %collective-permute-start.12 = (bf16[512,128]{1,0:T(8,128)(2,1)S(1)}, bf16[512,128]{1,0:T(8,128)(2,1)S(1)}, u32[]{:S(2)}, u32[]{:S(2)}) collective-permute-start(bf16[512,128]{1,0:T(8,128)(2,1)S(1)} %add_convert_fusion.5.refs_0_), channel_id=1, source_target_pairs={{0,96},{32,0},{64,32},{96,64},{1,97},{33,1},{65,33},{97,65},{2,98}... | collective-permute-start | bytes 393224 | tf_op jit(solution)/shard_map/ppermute | solution.py:23
  88.3 18.3 %collective-permute-start.23 = (bf16[256,512]{1,0:T(8,128)(2,1)S(1)}, bf16[256,512]{1,0:T(8,128)(2,1)S(1)}, u32[]{:S(2)}, u32[]{:S(2)}) collective-permute-start(bf16[256,512]{1,0:T(8,128)(2,1)S(1)} %get-tuple-element.137), channel_id=1, source_target_pairs={{0,6},{2,0},{4,2},{6,4},{1,7},{3,1},{5,3},{7,5},{8,14},{10,8},{12,... | collective-permute-start | bytes 786440 | tf_op jit(solution)/shard_map/ppermute | solution.py:23
  89.9 16.7 %collective-permute-start.21 = (bf16[512,512]{1,0:T(8,128)(2,1)S(1)}, bf16[512,512]{1,0:T(8,128)(2,1)S(1)}, u32[]{:S(2)}, u32[]{:S(2)}) collective-permute-start(bf16[512,512]{1,0:T(8,128)(2,1)S(1)} %shard_map.109.refs_1_), channel_id=1, source_target_pairs={{0,24},{8,0},{16,8},{24,16},{1,25},{9,1},{17,9},{25,17},{2,26},{10... | collective-permute-start | bytes 1572872 | tf_op jit(solution)/shard_map/ppermute | solution.py:23
  92.0 14.6 %collective-permute-start.20 = (bf16[512,512]{1,0:T(8,128)(2,1)S(1)}, bf16[512,512]{1,0:T(8,128)(2,1)S(1)}, u32[]{:S(2)}, u32[]{:S(2)}) collective-permute-start(bf16[512,512]{1,0:T(8,128)(2,1)S(1)} %shard_map.109.refs_1_), channel_id=1, source_target_pairs={{0,8},{8,16},{16,24},{24,0},{1,9},{9,17},{17,25},{25,1},{2,10},{10... | collective-permute-start | bytes 1572872 | tf_op jit(solution)/shard_map/ppermute | solution.py:23
  92.0 14.6 %collective-permute-start.22 = (bf16[256,512]{1,0:T(8,128)(2,1)S(1)}, bf16[256,512]{1,0:T(8,128)(2,1)S(1)}, u32[]{:S(2)}, u32[]{:S(2)}) collective-permute-start(bf16[256,512]{1,0:T(8,128)(2,1)S(1)} %get-tuple-element.129), channel_id=1, source_target_pairs={{0,2},{2,4},{4,6},{6,0},{1,3},{3,5},{5,7},{7,1},{8,10},{10,12},{12... | collective-permute-start | bytes 786440 | tf_op jit(solution)/shard_map/ppermute | solution.py:23
  106.6 10.9 %collective-permute-start.24 = (bf16[512,512]{1,0:T(8,128)(2,1)S(1)}, bf16[512,512]{1,0:T(8,128)(2,1)S(1)}, u32[]{:S(2)}, u32[]{:S(2)}) collective-permute-start(bf16[512,512]{1,0:T(8,128)(2,1)S(1)} %collective-permute-done.21.refs_1_), channel_id=1, source_target_pairs={{0,24},{8,0},{16,8},{24,16},{1,25},{9,1},{17,9},{25,17},{2,26},{10... | collective-permute-start | bytes 1572872 | tf_op jit(solution)/shard_map/ppermute | solution.py:23
  106.7 6.6 %collective-permute-start.26 = (bf16[128,512]{1,0:T(8,128)(2,1)S(1)}, bf16[128,512]{1,0:T(8,128)(2,1)S(1)}, u32[]{:S(2)}, u32[]{:S(2)}) collective-permute-start(bf16[128,512]{1,0:T(8,128)(2,1)S(1)} %add_convert_fusion.3), channel_id=1, source_target_pairs={{0,6},{2,0},{4,2},{6,4},{1,7},{3,1},{5,3},{7,5},{8,14},{10,8},{12,... | collective-permute-start | bytes 393224 | tf_op jit(solution)/shard_map/ppermute | solution.py:23
  106.8 10.7 %collective-permute-start.25 = (bf16[128,512]{1,0:T(8,128)(2,1)S(1)}, bf16[128,512]{1,0:T(8,128)(2,1)S(1)}, u32[]{:S(2)}, u32[]{:S(2)}) collective-permute-start(bf16[128,512]{1,0:T(8,128)(2,1)S(1)} %add_convert_fusion.4), channel_id=1, source_target_pairs={{0,2},{2,4},{4,6},{6,0},{1,3},{3,5},{5,7},{7,1},{8,10},{10,12},{12... | collective-permute-start | bytes 393224 | tf_op jit(solution)/shard_map/ppermute | solution.py:23
  118.1 9.0 %collective-permute-start.27 = (f32[384,512]{1,0:T(8,128)S(1)}, f32[384,512]{1,0:T(8,128)S(1)}, u32[]{:S(2)}, u32[]{:S(2)}) collective-permute-start(f32[384,512]{1,0:T(8,128)S(1)} %get-tuple-element.145), channel_id=1, source_target_pairs={{0,1},{1,0},{2,3},{3,2},{4,5},{5,4},{6,7},{7,6},{8,9},{9,8},{10,11... | collective-permute-start | bytes 2359304 | tf_op jit(solution)/shard_map/ppermute | solution.py:23
  (5 other events, 6.5 us)

commit v4 on v3

--- a/solution.py
+++ b/solution.py
@@ -21,6 +21,10 @@
 def shift(v, axis, k):
     n = lax.axis_size(axis)
     return lax.ppermute(v, axis, [(i, (i + k) % n) for i in range(n)])
+
+
+def swap_x(v, bits):
+    return lax.ppermute(v, "x", [(i, i ^ bits) for i in range(RING)])
 
 
 def params(mib=24):
@@ -210,34 +214,37 @@
     )
 
 
-def encode_kernel(_, l_ref, g_ref, r_ref, *outs):
+def encode_kernel(_, l_ref, g_ref, r_ref, keep, send):
     nudged = (g_ref[...] - l_ref[...]) + r_ref[...]
     top = jnp.max(jnp.abs(nudged), axis=1, keepdims=True) + 1e-06
     scale = top.astype(jnp.bfloat16).astype(jnp.float32)
     codes = (nudged / scale).astype(jnp.bfloat16).astype(jnp.float32)
     decoded = (codes * scale).astype(jnp.bfloat16)
-    for k, out in enumerate(outs):
-
-        @pl.when(pl.program_id(0) == k)
+    for half, out in enumerate((keep, send)):
+
+        @pl.when(pl.program_id(0) // 2 == half)
         def _():
             out[...] = decoded
 
 
-def encode(x, local_row, global_row, residual_row):
+def encode(order, local_row, global_row, residual_row):
     n = local_row.shape[0] // RING
-    part = pl.BlockSpec((n, BLOCK), lambda i, s: (lax.rem(s[0] + i, RING), 0))
+    part = pl.BlockSpec((n, BLOCK), lambda i, s: (s[i], 0))
     return pl.pallas_call(
         encode_kernel,
         grid_spec=pltpu.PrefetchScalarGridSpec(
             num_scalar_prefetch=1,
             grid=(RING,),
             in_specs=[part] * 3,
-            out_specs=[pl.BlockSpec((n, BLOCK), lambda i, s: (0, 0))] * RING,
+            out_specs=[
+                pl.BlockSpec((n, BLOCK), lambda i, s: (jnp.minimum(i, 1), 0)),
+                pl.BlockSpec((n, BLOCK), lambda i, s: (jnp.maximum(i - 2, 0), 0)),
+            ],
         ),
-        out_shape=[jax.ShapeDtypeStruct((n, BLOCK), jnp.bfloat16)] * RING,
-        compiler_params=params(),
-        cost_estimate=FREE,
-    )(x[None], local_row, global_row, residual_row)
+        out_shape=[jax.ShapeDtypeStruct((2 * n, BLOCK), jnp.bfloat16)] * 2,
+        compiler_params=params(),
+        cost_estimate=FREE,
+    )(order, local_row, global_row, residual_row)
 
 
 def outer_kernel(replicas, _, l_ref, g_ref, m_ref, *refs):
@@ -253,21 +260,23 @@
             momentum_ref[...] = new_momentum
 
 
-def outer_step(x, replicas, local_row, global_row, momentum_row, sums):
+def outer_step(order, replicas, local_row, global_row, momentum_row, sums):
     n = local_row.shape[0] // RING
-    part = pl.BlockSpec((n, BLOCK), lambda i, s: (lax.rem(s[0] + i, RING), 0))
+    part = pl.BlockSpec((n, BLOCK), lambda i, s: (s[i], 0))
+    first, second, pair = sums
     return pl.pallas_call(
         functools.partial(outer_kernel, replicas),
         grid_spec=pltpu.PrefetchScalarGridSpec(
             num_scalar_prefetch=1,
             grid=(RING,),
-            in_specs=[part] * 3 + [pl.BlockSpec((n, BLOCK), lambda i, s: (0, 0))] * RING,
+            in_specs=[part] * 3
+            + [pl.BlockSpec((n, BLOCK), lambda i, s, b=b: (b, 0)) for b in (0, 0, 0, 1)],
             out_specs=[part, part],
         ),
         out_shape=[jax.ShapeDtypeStruct(local_row.shape, jnp.float32)] * 2,
         compiler_params=params(),
         cost_estimate=FREE,
-    )(x[None], local_row, global_row, momentum_row, *sums)
+    )(order, local_row, global_row, momentum_row, first, second, pair, pair)
 
 
 def per_device(
@@ -288,10 +297,12 @@
     local_row, global_row, momentum_row, residual_row = (
         v.reshape(-1, BLOCK) for v in (local_fragment, global_fragment, momentum, residual)
     )
-    chunks = encode(x, local_row, global_row, residual_row)
+    order = jnp.stack([x, x ^ 3, x ^ 1, x ^ 2])
+    chunks = encode(order, local_row, global_row, residual_row)
     mine, send, w_1, w_3, *chunks = lax.optimization_barrier((mine, send, w_1, w_3, *chunks))
     theirs = shift(send, "core", 1)
-    parts = [chunks[0]] + [shift(chunks[k], "x", k) for k in (1, 2, 3)]
+    keep, to_pair = chunks
+    from_pair = swap_x(to_pair, 1)
 
     w_2 = shift(after(weight, w_1), "zh", 2)
     w_01 = stack_rows(weight, w_1)
@@ -302,26 +313,33 @@
 
     far_a, far_b = grads(0, [bf, bf], w_01)
     in_a, in_b = shift(far_a, "y", 1), shift(far_b, "y", -1)
-    parts = after(tuple(parts), far_a)
-    dir_b, dir_a = grads(2, [bf, bf], *parts)
-    over_x = sum(v.astype(f32) for v in after(parts, dir_b)).astype(bf)
+    from_pair, prev_01, next_01 = after((from_pair, prev_01, next_01), far_a)
+    dir_b, dir_a = grads(2, [bf, bf], from_pair, prev_01, next_01)
+    keep, from_pair = after((keep, from_pair), dir_b)
+    two = keep.astype(f32) + from_pair.astype(f32)
+    n = two.shape[0] // 2
+    from_other = swap_x(two[n:].astype(bf), 3)
+    got_b, got_a = shift(dir_b, "y", 1), shift(dir_a, "y", -1)
+
+    in_a, in_b, from_other = lax.optimization_barrier((in_a, in_b, from_other, dir_b))[:3]
+    own_a, own_b, own_01, own_23 = grads(4, [f32] * 4, in_a, in_b, from_other)
+    over_x = (two[:n] + after(from_other, own_a).astype(f32)).astype(bf)
     from_zl = shift(over_x, "zl", 1)
-    got_b, got_a = shift(dir_b, "y", 1), shift(dir_a, "y", -1)
-
-    in_a, in_b, from_zl = lax.optimization_barrier((in_a, in_b, from_zl, dir_b))[:3]
-    own_a, own_b, own_01, own_23 = grads(4, [f32] * 4, in_a, in_b, from_zl)
     prev_01, next_01 = after((prev_01, next_01), own_a)
     far_01 = shift(prev_01, "y", 1)
-    in_a, in_b, got_a, got_b, w_2 = lax.optimization_barrier((in_a, in_b, got_a, got_b, w_2))
+    in_a, in_b, got_a, got_b, w_2, from_zl = lax.optimization_barrier(
+        (in_a, in_b, got_a, got_b, w_2, from_zl)
+    )
     mer_a = (own_a + in_a.astype(f32)).astype(bf)
     mer_b = (own_b + in_b.astype(f32)).astype(bf)
     sum_a, sum_b = shift(mer_a, "y", 1), shift(mer_b, "y", -1)
 
     from_zl, over_x = after((from_zl, over_x), mer_a, mer_b)
     total = (over_x.astype(f32) + from_zl.astype(f32)).astype(bf)
-    totals = [total] + [shift(total, "x", -k) for k in (1, 2, 3)]
+    other_total = swap_x(total, 3)
+    totals = total, other_total, swap_x(jnp.concatenate([total, other_total]), 1)
     replicas = lax.axis_size("x") * lax.axis_size("zl")
-    mixed, new_momentum = outer_step(x, replicas, local_row, global_row, momentum_row, totals)
+    mixed, new_momentum = outer_step(order, replicas, local_row, global_row, momentum_row, totals)
 
     w_23 = stack_rows(*after((w_2, w_3), mixed))
     far_01, *received = lax.optimization_barrier((far_01, got_a, sum_a, got_b, sum_b, w_23, mixed))[:5]

time: 128 us -> 121 us (0.945); the launches traced: 128 us -> 119 us
  waiting for transfers between devices: 49.5 us -> 41.5 us
  starting transfers between devices: 47.7 us -> 45.5 us
    ppermute x28 -> x22, waiting for transfers between devices: 49.5 us -> 28.9 us  [shift(): return lax.ppermute(v, axis, [(i, (i + k) % n) for i in range(n)])]
    ppermute x0 -> x4, waiting for transfers between devices: none -> 12.6 us  [swap_x(): return lax.ppermute(v, 'x', [(i, i ^ bits) for i in range(RING)])]
    ppermute x28 -> x22, starting transfers between devices: 47.7 us -> 40.4 us  [shift(): return lax.ppermute(v, axis, [(i, (i + k) % n) for i in range(n)])]
    ppermute x0 -> x4, starting transfers between devices: none -> 5.12 us  [swap_x(): return lax.ppermute(v, 'x', [(i, i ^ bits) for i in range(RING)])]
  transfers between devices with their start and end apart: 28 -> 26, of which waited for: 16 -> 15; matrix products, arithmetic and copies ran while one was open for 1% -> 1% of each run, Pallas kernels for 12% -> 16%
where the time goes in v4:
time: 121 us; the launch traced here: 119 us
  starting transfers between devices  45.5 us (38%)
  waiting for transfers between devices  41.5 us (34%)
  Pallas kernels  19.5 us (16%)
  local copies, waits for them, and re-layouts  9.36 us (8%)
  other arithmetic  2.34 us (2%)
    ppermute x22, starting transfers between devices, shift(): return lax.ppermute(v, axis, [(i, (i + k) % n) for i in range(n)])  40.4 us
    ppermute x22, waiting for transfers between devices, shift(): return lax.ppermute(v, axis, [(i, (i + k) % n) for i in range(n)])  28.9 us
    ppermute x4, waiting for transfers between devices, swap_x(): return lax.ppermute(v, 'x', [(i, i ^ bits) for i in range(RING)])  12.6 us
    unnamed x18, local copies, waits for them, and re-layouts  9.24 us
    pallas_call x3, Pallas kernels, grad_rows_of(): pl.pallas_call(grad_kernel, grid=(len(dtypes),), in_specs=[column, column...  7.04 us
    ppermute x4, starting transfers between devices, swap_x(): return lax.ppermute(v, 'x', [(i, i ^ bits) for i in range(RING)])  5.12 us
    pallas_call x3, Pallas kernels, values_part(): pl.pallas_call(functools.partial(values_kernel, cuts, bool(acc)), grid=(1...  3.74 us
    pallas_call x1, Pallas kernels, outer_step(): pl.pallas_call(functools.partial(outer_kernel, replicas), grid_spec=pltpu...  2.56 us
  transfers between devices with their start and end apart: 26, of which 15 were waited for; matrix products, arithmetic and copies ran while one was open for 1% of the time, Pallas kernels for 16%

profile of v4, /device:TPU:5, one launch (start us, length us, event | category | flops | bytes accessed | tf_op | source)
XLA Modules:
  0.0 119.1 jit_solution(6431696649986625096)
XLA Ops:
  0.6 3.1 %collective-permute-start.1 = (bf16[256,512]{1,0:T(8,128)(2,1)}, bf16[256,512]{1,0:T(8,128)(2,1)}, u32[]{:S(2)}, u32[]{:S(2)}) collective-permute-start(bf16[256,512]{1,0:T(8,128)(2,1)} %bitcast.19.refs_0_), channel_id=1, source_target_pairs={{0,2},{2,4},{4,6},{6,0},{1,3},{3,5},{5,7},{7,1},{8,10},{10,12},{12... | collective-permute-start | bytes 786440 | tf_op jit(solution)/shard_map/ppermute | solution.py:23
  3.7 3.1 %collective-permute-start = (bf16[256,512]{1,0:T(8,128)(2,1)}, bf16[256,512]{1,0:T(8,128)(2,1)}, u32[]{:S(2)}, u32[]{:S(2)}) collective-permute-start(bf16[256,512]{1,0:T(8,128)(2,1)} %bitcast.19.refs_0_), channel_id=1, source_target_pairs={{0,6},{2,0},{4,2},{6,4},{1,7},{3,1},{5,3},{7,5},{8,14},{10,8},{12,... | collective-permute-start | bytes 786440 | tf_op jit(solution)/shard_map/ppermute | solution.py:23
  6.9 2.8 %copy-done = bf16[1,384,8192]{2,1,0:T(8,128)(2,1)S(1)} copy-done((bf16[1,384,8192]{2,1,0:T(8,128)(2,1)S(1)}, bf16[1,384,8192]{2,1,0:T(8,128)(2,1)}, u32[]{:S(2)}) %copy-start) | copy-done | bytes 6291480
  10.7 2.4 %shard_map.102 = (bf16[384,4096]{1,0:T(8,128)(2,1)S(1)}, bf16[384,4608]{1,0:T(8,128)(2,1)S(1)}) custom-call(s32[17]{0:T(128)S(1)} %stack.86.s_ref, bf16[384,8192]{1,0:T(8,128)(2,1)S(1)} %bitcast.34, bf16[384,8192]{1,0:T(8,128)(2,1)S(1)} %bitcast.35, bf16[384,512]{1,0:T(8,128)(2,1)S(1)} %bitcast.36), custom_call_target="tpu_custom_call" | custom-call | flops 1 | bytes 1 | tf_op jit(solution)/shard_map/pallas_call | solution.py:73
  13.2 1.7 %copy-done.8 = bf16[384,4608]{1,0:T(8,128)(2,1)} copy-done((bf16[384,4608]{1,0:T(8,128)(2,1)}, bf16[384,4608]{1,0:T(8,128)(2,1)S(1)}, u32[]{:S(2)}) %copy-start.8) | copy-done | bytes 3538968
  22.2 2.8 %collective-permute-start.7 = (bf16[512,512]{1,0:T(8,128)(2,1)S(1)}, bf16[512,512]{1,0:T(8,128)(2,1)S(1)}, u32[]{:S(2)}, u32[]{:S(2)}) collective-permute-start(bf16[512,512]{1,0:T(8,128)(2,1)S(1)} %shard_map.104.refs_0_), channel_id=1, source_target_pairs={{0,24},{8,0},{16,8},{24,16},{1,25},{9,1},{17,9},{25,17},{2,26},{10... | collective-permute-start | bytes 1572872 | tf_op jit(solution)/shard_map/ppermute | solution.py:23
  27.2 1.8 %shard_map.105 = (bf16[512,512]{1,0:T(8,128)(2,1)S(1)}, bf16[512,512]{1,0:T(8,128)(2,1)S(1)}) custom-call(bf16[384,4096]{1,0:T(8,128)(2,1)S(1)} %get-tuple-element.76.h_ref.refs_5_.refs_6_.refs_7_.refs_8_.refs_9_.refs_2_.refs_3_.refs_1_, ...), custom_call_target="tpu_custom_call" | custom-call | flops 1 | bytes 1 | tf_op jit(solution)/shard_map/pallas_call | solution.py:129
  28.9 2.8 %collective-permute-start.4 = (bf16[512,512]{1,0:T(8,128)(2,1)S(1)}, bf16[512,512]{1,0:T(8,128)(2,1)S(1)}, u32[]{:S(2)}, u32[]{:S(2)}) collective-permute-start(bf16[512,512]{1,0:T(8,128)(2,1)S(1)} %get-tuple-element.81), channel_id=1, source_target_pairs={{0,24},{8,0},{16,8},{24,16},{1,25},{9,1},{17,9},{25,17},{2,26},{10... | collective-permute-start | bytes 1572872 | tf_op jit(solution)/shard_map/ppermute | solution.py:23
  32.6 3.7 %collective-permute-done.7.refs_3_ = bf16[512,512]{1,0:T(8,128)(2,1)S(1)} collective-permute-done((bf16[512,512]{1,0:T(8,128)(2,1)S(1)}, bf16[512,512]{1,0:T(8,128)(2,1)S(1)}, u32[]{:S(2)}, u32[]{:S(2)}) %collective-permute-start.7) | collective-permute-done | bytes 524320 | tf_op jit(solution)/shard_map/ppermute | solution.py:23
  36.4 3.1 %collective-permute-done.6.refs_2_ = bf16[512,512]{1,0:T(8,128)(2,1)S(1)} collective-permute-done((bf16[512,512]{1,0:T(8,128)(2,1)S(1)}, bf16[512,512]{1,0:T(8,128)(2,1)S(1)}, u32[]{:S(2)}, u32[]{:S(2)}) %collective-permute-start.6) | collective-permute-done | bytes 524320 | tf_op jit(solution)/shard_map/ppermute | solution.py:23
  39.4 1.8 %shard_map.106 = (bf16[512,512]{1,0:T(8,128)(2,1)S(1)}, bf16[512,512]{1,0:T(8,128)(2,1)S(1)}) custom-call(bf16[384,4096]{1,0:T(8,128)(2,1)S(1)} %get-tuple-element.76.h_ref.refs_5_.refs_6_.refs_7_.refs_8_.refs_9_.refs_2_.refs_3_.refs_1_, ...), custom_call_target="tpu_custom_call" | custom-call | flops 1 | bytes 1 | tf_op jit(solution)/shard_map/pallas_call | solution.py:129
  41.3 2.7 %collective-permute-start.9 = (bf16[512,512]{1,0:T(8,128)(2,1)S(1)}, bf16[512,512]{1,0:T(8,128)(2,1)S(1)}, u32[]{:S(2)}, u32[]{:S(2)}) collective-permute-start(bf16[512,512]{1,0:T(8,128)(2,1)S(1)} %get-tuple-element.93), channel_id=1, source_target_pairs={{0,24},{8,0},{16,8},{24,16},{1,25},{9,1},{17,9},{25,17},{2,26},{10... | collective-permute-start | bytes 1572872 | tf_op jit(solution)/shard_map/ppermute | solution.py:23
  44.4 3.9 %collective-permute-done.8 = bf16[512,128]{1,0:T(8,128)(2,1)S(1)} collective-permute-done((bf16[512,128]{1,0:T(8,128)(2,1)S(1)}, bf16[512,128]{1,0:T(8,128)(2,1)S(1)}, u32[]{:S(2)}, u32[]{:S(2)}) %collective-permute-start.8) | collective-permute-done | bytes 131104 | tf_op jit(solution)/shard_map/ppermute | solution.py:27
  48.2 4.6 %collective-permute-start.11 = (bf16[256,512]{1,0:T(8,128)(2,1)}, bf16[256,512]{1,0:T(8,128)(2,1)S(1)}, u32[]{:S(2)}, u32[]{:S(2)}) collective-permute-start(bf16[256,512]{1,0:T(8,128)(2,1)} %bitcast.19.refs_0_), channel_id=1, source_target_pairs={{0,4},{2,6},{4,0},{6,2},{1,5},{3,7},{5,1},{7,3},{8,12},{10,14},{12... | collective-permute-start | bytes 786440 | tf_op jit(solution)/shard_map/ppermute | solution.py:23
  52.9 3.5 %shard_map.107 = (f32[512,512]{1,0:T(8,128)S(1)}, f32[512,512]{1,0:T(8,128)S(1)}, f32[512,512]{1,0:T(8,128)S(1)}, f32[512,512]{1,0:T(8,128)S(1)}) custom-call(bf16[384,4096]{1,0:T(8,128)(2,1)S(1)} %get-tuple-element.76.h_ref.refs_5_.refs_6_.refs_7_.refs_8_.refs_9_.refs_2_.refs_3_.refs_1_, ...), custom_call_target="tpu_custom_call" | custom-call | flops 1 | bytes 1 | tf_op jit(solution)/shard_map/pallas_call | solution.py:129
  57.3 3.2 %collective-permute-done.11.refs_0_ = bf16[256,512]{1,0:T(8,128)(2,1)S(1)} collective-permute-done((bf16[256,512]{1,0:T(8,128)(2,1)}, bf16[256,512]{1,0:T(8,128)(2,1)S(1)}, u32[]{:S(2)}, u32[]{:S(2)}) %collective-permute-start.11) | collective-permute-done | bytes 262176 | tf_op jit(solution)/shard_map/ppermute | solution.py:23
  60.5 1.4 %collective-permute-done.10.c = bf16[512,512]{1,0:T(8,128)(2,1)S(1)} collective-permute-done((bf16[512,512]{1,0:T(8,128)(2,1)S(1)}, bf16[512,512]{1,0:T(8,128)(2,1)S(1)}, u32[]{:S(2)}, u32[]{:S(2)}) %collective-permute-start.10) | collective-permute-done | bytes 524320 | tf_op jit(solution)/shard_map/ppermute | solution.py:23
  61.9 3.8 %collective-permute-done.12 = bf16[512,128]{1,0:T(8,128)(2,1)S(1)} collective-permute-done((bf16[512,128]{1,0:T(8,128)(2,1)S(1)}, bf16[512,128]{1,0:T(8,128)(2,1)S(1)}, u32[]{:S(2)}, u32[]{:S(2)}) %collective-permute-start.12) | collective-permute-done | bytes 131104 | tf_op jit(solution)/shard_map/ppermute | solution.py:23
  66.1 2.7 %collective-permute-start.17 = (bf16[512,512]{1,0:T(8,128)(2,1)S(1)}, bf16[512,512]{1,0:T(8,128)(2,1)S(1)}, u32[]{:S(2)}, u32[]{:S(2)}) collective-permute-start(bf16[512,512]{1,0:T(8,128)(2,1)S(1)} %add_convert_fusion), channel_id=1, source_target_pairs={{0,24},{8,0},{16,8},{24,16},{1,25},{9,1},{17,9},{25,17},{2,26},{10... | collective-permute-start | bytes 1572872 | tf_op jit(solution)/shard_map/ppermute | solution.py:23
  69.3 3.9 %collective-permute-done.13.refs_1_ = bf16[512,128]{1,0:T(8,128)(2,1)S(1)} collective-permute-done((bf16[512,128]{1,0:T(8,128)(2,1)S(1)}, bf16[512,128]{1,0:T(8,128)(2,1)S(1)}, u32[]{:S(2)}, u32[]{:S(2)}) %collective-permute-start.13) | collective-permute-done | bytes 131104 | tf_op jit(solution)/shard_map/ppermute | solution.py:27
  73.1 3.5 %collective-permute-start.14 = (bf16[1024,128]{1,0:T(8,128)(2,1)S(1)}, bf16[1024,128]{1,0:T(8,128)(2,1)S(1)}, u32[]{:S(2)}, u32[]{:S(2)}) collective-permute-start(bf16[1024,128]{1,0:T(8,128)(2,1)S(1)} %pad_maximum_fusion), channel_id=1, source_target_pairs={{0,32},{32,0},{64,96},{96,64},{1,33},{33,1},{65,97},{97,65},{2,34}... | collective-permute-start | bytes 786440 | tf_op jit(solution)/shard_map/ppermute | solution.py:27
  76.7 4.1 %collective-permute-done.14.refs_2_.refs_3_ = bf16[1024,128]{1,0:T(8,128)(2,1)S(1)} collective-permute-done((bf16[1024,128]{1,0:T(8,128)(2,1)S(1)}, bf16[1024,128]{1,0:T(8,128)(2,1)S(1)}, u32[]{:S(2)}, u32[]{:S(2)}) %collective-permute-start.14) | collective-permute-done | bytes 262176 | tf_op jit(solution)/shard_map/ppermute | solution.py:27
  80.7 2.6 %shard_map.108 = (f32[2048,128]{1,0:T(8,128)}, f32[2048,128]{1,0:T(8,128)}) custom-call(s32[4]{0:T(128)S(1)} %pad_add_fusion._, f32[2048,128]{1,0:T(8,128)S(1)} %bitcast.41, f32[2048,128]{1,0:T(8,128)S(1)} %bitcast.43, f32[2048,128]{1,0:T(8,128)S(1)} %bitcast.45, bf16[512,128]{1,0:T(8,128)(2,1)S(1)} %add_convert_fusion.5.refs_0_, ...), custom_call_target="tpu_custom_call" | custom-call | flops 1 | bytes 1 | tf_op jit(solution)/shard_map/pallas_call | solution.py:267
  85.9 1.5 %collective-permute-start.18 = (bf16[512,512]{1,0:T(8,128)(2,1)S(1)}, bf16[512,512]{1,0:T(8,128)(2,1)S(1)}, u32[]{:S(2)}, u32[]{:S(2)}) collective-permute-start(bf16[512,512]{1,0:T(8,128)(2,1)S(1)} %shard_map.109.refs_1_), channel_id=1, source_target_pairs={{0,8},{8,16},{16,24},{24,0},{1,9},{9,17},{17,25},{25,1},{2,10},{10... | collective-permute-start | bytes 1572872 | tf_op jit(solution)/shard_map/ppermute | solution.py:23
  87.4 2.4 %collective-permute-start.20 = (bf16[256,512]{1,0:T(8,128)(2,1)S(1)}, bf16[256,512]{1,0:T(8,128)(2,1)S(1)}, u32[]{:S(2)}, u32[]{:S(2)}) collective-permute-start(bf16[256,512]{1,0:T(8,128)(2,1)S(1)} %get-tuple-element.119), channel_id=1, source_target_pairs={{0,2},{2,4},{4,6},{6,0},{1,3},{3,5},{5,7},{7,1},{8,10},{10,12},{12... | collective-permute-start | bytes 786440 | tf_op jit(solution)/shard_map/ppermute | solution.py:23
  89.8 2.2 %shard_map.111 = (f32[384,512]{1,0:T(8,128)S(1)}, f32[384,512]{1,0:T(8,128)S(1)}) custom-call(bf16[512,512]{1,0:T(8,128)(2,1)S(1)} %shard_map.104.refs_0_, bf16[512,512]{1,0:T(8,128)(2,1)S(1)} %shard_map.109.refs_1_, bf16[512,512]{1,0:T(8,128)(2,1)S(1)} %collective-permute-done.6.refs_2_, bf16[512,512]{1,0:T(8,128)(2,1)S(1)} %collective-permute-done.7.refs_3_, ...), custom_call_target="tpu_custom_call" | custom-call | flops 1 | bytes 1 | tf_op jit(solution)/shard_map/pallas_call | solution.py:198
  92.0 5.4 %collective-permute-done.21 = bf16[256,512]{1,0:T(8,128)(2,1)S(1)} collective-permute-done((bf16[256,512]{1,0:T(8,128)(2,1)S(1)}, bf16[256,512]{1,0:T(8,128)(2,1)S(1)}, u32[]{:S(2)}, u32[]{:S(2)}) %collective-permute-start.21) | collective-permute-done | bytes 262176 | tf_op jit(solution)/shard_map/ppermute | solution.py:23
  97.6 3.6 %collective-permute-start.24 = (bf16[128,512]{1,0:T(8,128)(2,1)S(1)}, bf16[128,512]{1,0:T(8,128)(2,1)S(1)}, u32[]{:S(2)}, u32[]{:S(2)}) collective-permute-start(bf16[128,512]{1,0:T(8,128)(2,1)S(1)} %add_convert_fusion.3), channel_id=1, source_target_pairs={{0,6},{2,0},{4,2},{6,4},{1,7},{3,1},{5,3},{7,5},{8,14},{10,8},{12,... | collective-permute-start | bytes 393224 | tf_op jit(solution)/shard_map/ppermute | solution.py:23
  101.2 2.3 %collective-permute-start.23 = (bf16[128,512]{1,0:T(8,128)(2,1)S(1)}, bf16[128,512]{1,0:T(8,128)(2,1)S(1)}, u32[]{:S(2)}, u32[]{:S(2)}) collective-permute-start(bf16[128,512]{1,0:T(8,128)(2,1)S(1)} %add_convert_fusion.4), channel_id=1, source_target_pairs={{0,2},{2,4},{4,6},{6,0},{1,3},{3,5},{5,7},{7,1},{8,10},{10,12},{12... | collective-permute-start | bytes 393224 | tf_op jit(solution)/shard_map/ppermute | solution.py:23
  104.4 1.8 %collective-permute-done.24 = bf16[128,512]{1,0:T(8,128)(2,1)S(1)} collective-permute-done((bf16[128,512]{1,0:T(8,128)(2,1)S(1)}, bf16[128,512]{1,0:T(8,128)(2,1)S(1)}, u32[]{:S(2)}, u32[]{:S(2)}) %collective-permute-start.24) | collective-permute-done | bytes 131104 | tf_op jit(solution)/shard_map/ppermute | solution.py:23
  106.2 4.1 %collective-permute-done.23 = bf16[128,512]{1,0:T(8,128)(2,1)S(1)} collective-permute-done((bf16[128,512]{1,0:T(8,128)(2,1)S(1)}, bf16[128,512]{1,0:T(8,128)(2,1)S(1)}, u32[]{:S(2)}, u32[]{:S(2)}) %collective-permute-start.23) | collective-permute-done | bytes 131104 | tf_op jit(solution)/shard_map/ppermute | solution.py:23
  110.9 5.4 %collective-permute-start.25 = (f32[384,512]{1,0:T(8,128)S(1)}, f32[384,512]{1,0:T(8,128)S(1)}, u32[]{:S(2)}, u32[]{:S(2)}) collective-permute-start(f32[384,512]{1,0:T(8,128)S(1)} %get-tuple-element.135), channel_id=1, source_target_pairs={{0,1},{1,0},{2,3},{3,2},{4,5},{5,4},{6,7},{7,6},{8,9},{9,8},{10,11... | collective-permute-start | bytes 2359304 | tf_op jit(solution)/shard_map/ppermute | solution.py:23
  (65 shorter events, 20.6 us)
Async XLA Ops:
  0.6 19.4 %collective-permute-start.1 = (bf16[256,512]{1,0:T(8,128)(2,1)}, bf16[256,512]{1,0:T(8,128)(2,1)}, u32[]{:S(2)}, u32[]{:S(2)}) collective-permute-start(bf16[256,512]{1,0:T(8,128)(2,1)} %bitcast.19.refs_0_), channel_id=1, source_target_pairs={{0,2},{2,4},{4,6},{6,0},{1,3},{3,5},{5,7},{7,1},{8,10},{10,12},{12... | collective-permute-start | bytes 786440 | tf_op jit(solution)/shard_map/ppermute | solution.py:23
  3.7 16.5 %collective-permute-start = (bf16[256,512]{1,0:T(8,128)(2,1)}, bf16[256,512]{1,0:T(8,128)(2,1)}, u32[]{:S(2)}, u32[]{:S(2)}) collective-permute-start(bf16[256,512]{1,0:T(8,128)(2,1)} %bitcast.19.refs_0_), channel_id=1, source_target_pairs={{0,6},{2,0},{4,2},{6,4},{1,7},{3,1},{5,3},{7,5},{8,14},{10,8},{12,... | collective-permute-start | bytes 786440 | tf_op jit(solution)/shard_map/ppermute | solution.py:23
  6.9 2.8 %copy-start = (bf16[1,384,8192]{2,1,0:T(8,128)(2,1)S(1)}, bf16[1,384,8192]{2,1,0:T(8,128)(2,1)}, u32[]{:S(2)}) copy-start(bf16[1,384,8192]{2,1,0:T(8,128)(2,1)} %param.7) | copy-start | bytes 18874372
  13.1 1.7 %copy-start.8 = (bf16[384,4608]{1,0:T(8,128)(2,1)}, bf16[384,4608]{1,0:T(8,128)(2,1)S(1)}, u32[]{:S(2)}) copy-start(bf16[384,4608]{1,0:T(8,128)(2,1)S(1)} %get-tuple-element.77) | copy-start | bytes 10616836
  14.9 12.3 %copy-start.2 = (bf16[1,384,512]{2,1,0:T(8,128)(2,1)S(1)}, bf16[1,384,512]{2,1,0:T(8,128)(2,1)}, u32[]{:S(2)}) copy-start(bf16[1,384,512]{2,1,0:T(8,128)(2,1)} %param.9) | copy-start | bytes 1179652
  15.0 1.3 %copy-start.3 = (f32[1,262144]{1,0:T(1,128)S(1)}, f32[1,262144]{1,0:T(1,128)}, u32[]{:S(2)}) copy-start(f32[1,262144]{1,0:T(1,128)} %param.10) | copy-start | bytes 3145732
  20.2 7.0 %collective-permute-start.2 = (bf16[384,4608]{1,0:T(8,128)(2,1)}, bf16[384,4608]{1,0:T(8,128)(2,1)S(1)}, u32[]{:S(2)}, u32[]{:S(2)}) collective-permute-start(bf16[384,4608]{1,0:T(8,128)(2,1)} %copy-done.8), channel_id=1, source_target_pairs={{0,1},{1,0},{2,3},{3,2},{4,5},{5,4},{6,7},{7,6},{8,9},{9,8},{10,11... | collective-permute-start | bytes 10616840 | tf_op jit(solution)/shard_map/ppermute | solution.py:23
  22.2 14.2 %collective-permute-start.7 = (bf16[512,512]{1,0:T(8,128)(2,1)S(1)}, bf16[512,512]{1,0:T(8,128)(2,1)S(1)}, u32[]{:S(2)}, u32[]{:S(2)}) collective-permute-start(bf16[512,512]{1,0:T(8,128)(2,1)S(1)} %shard_map.104.refs_0_), channel_id=1, source_target_pairs={{0,24},{8,0},{16,8},{24,16},{1,25},{9,1},{17,9},{25,17},{2,26},{10... | collective-permute-start | bytes 1572872 | tf_op jit(solution)/shard_map/ppermute | solution.py:23
  25.0 14.4 %collective-permute-start.6 = (bf16[512,512]{1,0:T(8,128)(2,1)S(1)}, bf16[512,512]{1,0:T(8,128)(2,1)S(1)}, u32[]{:S(2)}, u32[]{:S(2)}) collective-permute-start(bf16[512,512]{1,0:T(8,128)(2,1)S(1)} %shard_map.104.refs_0_), channel_id=1, source_target_pairs={{0,8},{8,16},{16,24},{24,0},{1,9},{9,17},{17,25},{25,1},{2,10},{10... | collective-permute-start | bytes 1572872 | tf_op jit(solution)/shard_map/ppermute | solution.py:23
  25.0 7.6 %collective-permute-start.5 = (bf16[1024,128]{1,0:T(8,128)(2,1)S(1)}, bf16[1024,128]{1,0:T(8,128)(2,1)S(1)}, u32[]{:S(2)}, u32[]{:S(2)}) collective-permute-start(bf16[1024,128]{1,0:T(8,128)(2,1)S(1)} %get-tuple-element.83), channel_id=1, source_target_pairs={{0,32},{32,0},{64,96},{96,64},{1,33},{33,1},{65,97},{97,65},{2,34}... | collective-permute-start | bytes 786440 | tf_op jit(solution)/shard_map/ppermute | solution.py:27
  28.9 23.9 %collective-permute-start.4 = (bf16[512,512]{1,0:T(8,128)(2,1)S(1)}, bf16[512,512]{1,0:T(8,128)(2,1)S(1)}, u32[]{:S(2)}, u32[]{:S(2)}) collective-permute-start(bf16[512,512]{1,0:T(8,128)(2,1)S(1)} %get-tuple-element.81), channel_id=1, source_target_pairs={{0,24},{8,0},{16,8},{24,16},{1,25},{9,1},{17,9},{25,17},{2,26},{10... | collective-permute-start | bytes 1572872 | tf_op jit(solution)/shard_map/ppermute | solution.py:23
  31.8 21.1 %collective-permute-start.3 = (bf16[512,512]{1,0:T(8,128)(2,1)S(1)}, bf16[512,512]{1,0:T(8,128)(2,1)S(1)}, u32[]{:S(2)}, u32[]{:S(2)}) collective-permute-start(bf16[512,512]{1,0:T(8,128)(2,1)S(1)} %get-tuple-element.80), channel_id=1, source_target_pairs={{0,8},{8,16},{16,24},{24,0},{1,9},{9,17},{17,25},{25,1},{2,10},{10... | collective-permute-start | bytes 1572872 | tf_op jit(solution)/shard_map/ppermute | solution.py:23
  41.2 20.7 %collective-permute-start.10 = (bf16[512,512]{1,0:T(8,128)(2,1)S(1)}, bf16[512,512]{1,0:T(8,128)(2,1)S(1)}, u32[]{:S(2)}, u32[]{:S(2)}) collective-permute-start(bf16[512,512]{1,0:T(8,128)(2,1)S(1)} %get-tuple-element.88), channel_id=1, source_target_pairs={{0,8},{8,16},{16,24},{24,0},{1,9},{9,17},{17,25},{25,1},{2,10},{10... | collective-permute-start | bytes 1572872 | tf_op jit(solution)/shard_map/ppermute | solution.py:23
  41.3 19.2 %collective-permute-start.9 = (bf16[512,512]{1,0:T(8,128)(2,1)S(1)}, bf16[512,512]{1,0:T(8,128)(2,1)S(1)}, u32[]{:S(2)}, u32[]{:S(2)}) collective-permute-start(bf16[512,512]{1,0:T(8,128)(2,1)S(1)} %get-tuple-element.93), channel_id=1, source_target_pairs={{0,24},{8,0},{16,8},{24,16},{1,25},{9,1},{17,9},{25,17},{2,26},{10... | collective-permute-start | bytes 1572872 | tf_op jit(solution)/shard_map/ppermute | solution.py:23
  44.0 4.2 %collective-permute-start.8 = (bf16[512,128]{1,0:T(8,128)(2,1)S(1)}, bf16[512,128]{1,0:T(8,128)(2,1)S(1)}, u32[]{:S(2)}, u32[]{:S(2)}) collective-permute-start(bf16[512,128]{1,0:T(8,128)(2,1)S(1)} %slice.37), channel_id=1, source_target_pairs={{0,96},{32,64},{64,32},{96,0},{1,97},{33,65},{65,33},{97,1},{2,98}... | collective-permute-start | bytes 393224 | tf_op jit(solution)/shard_map/ppermute | solution.py:27
  48.2 12.2 %collective-permute-start.11 = (bf16[256,512]{1,0:T(8,128)(2,1)}, bf16[256,512]{1,0:T(8,128)(2,1)S(1)}, u32[]{:S(2)}, u32[]{:S(2)}) collective-permute-start(bf16[256,512]{1,0:T(8,128)(2,1)} %bitcast.19.refs_0_), channel_id=1, source_target_pairs={{0,4},{2,6},{4,0},{6,2},{1,5},{3,7},{5,1},{7,3},{8,12},{10,14},{12... | collective-permute-start | bytes 786440 | tf_op jit(solution)/shard_map/ppermute | solution.py:23
  56.4 24.3 %copy-start.4 = (f32[1,262144]{1,0:T(1,128)S(1)}, f32[1,262144]{1,0:T(1,128)}, u32[]{:S(2)}) copy-start(f32[1,262144]{1,0:T(1,128)} %param.10) | copy-start | bytes 3145732
  56.4 24.3 %copy-start.7 = (f32[262144]{0:T(1024)S(1)}, f32[262144]{0:T(1024)}, u32[]{:S(2)}) copy-start(f32[262144]{0:T(1024)} %param.12) | copy-start | bytes 3145732
  56.5 9.2 %collective-permute-start.12 = (bf16[512,128]{1,0:T(8,128)(2,1)S(1)}, bf16[512,128]{1,0:T(8,128)(2,1)S(1)}, u32[]{:S(2)}, u32[]{:S(2)}) collective-permute-start(bf16[512,128]{1,0:T(8,128)(2,1)S(1)} %fusion.1), channel_id=1, source_target_pairs={{0,128},{128,0},{1,129},{129,1},{2,130},{130,2},{3,131},{131,3},{4... | collective-permute-start | bytes 393224 | tf_op jit(solution)/shard_map/ppermute | solution.py:23
  57.3 27.0 %collective-permute-start.15 = (bf16[512,512]{1,0:T(8,128)(2,1)S(1)}, bf16[512,512]{1,0:T(8,128)(2,1)S(1)}, u32[]{:S(2)}, u32[]{:S(2)}) collective-permute-start(bf16[512,512]{1,0:T(8,128)(2,1)S(1)} %collective-permute-done.6.refs_2_), channel_id=1, source_target_pairs={{0,8},{8,16},{16,24},{24,0},{1,9},{9,17},{17,25},{25,1},{2,10},{10... | collective-permute-start | bytes 1572872 | tf_op jit(solution)/shard_map/ppermute | solution.py:23
  65.9 18.4 %collective-permute-start.16 = (bf16[512,512]{1,0:T(8,128)(2,1)S(1)}, bf16[512,512]{1,0:T(8,128)(2,1)S(1)}, u32[]{:S(2)}, u32[]{:S(2)}) collective-permute-start(bf16[512,512]{1,0:T(8,128)(2,1)S(1)} %add_convert_fusion.1), channel_id=1, source_target_pairs={{0,8},{8,16},{16,24},{24,0},{1,9},{9,17},{17,25},{25,1},{2,10},{10... | collective-permute-start | bytes 1572872 | tf_op jit(solution)/shard_map/ppermute | solution.py:23
  66.1 18.2 %collective-permute-start.17 = (bf16[512,512]{1,0:T(8,128)(2,1)S(1)}, bf16[512,512]{1,0:T(8,128)(2,1)S(1)}, u32[]{:S(2)}, u32[]{:S(2)}) collective-permute-start(bf16[512,512]{1,0:T(8,128)(2,1)S(1)} %add_convert_fusion), channel_id=1, source_target_pairs={{0,24},{8,0},{16,8},{24,16},{1,25},{9,1},{17,9},{25,17},{2,26},{10... | collective-permute-start | bytes 1572872 | tf_op jit(solution)/shard_map/ppermute | solution.py:23
  68.9 4.2 %collective-permute-start.13 = (bf16[512,128]{1,0:T(8,128)(2,1)S(1)}, bf16[512,128]{1,0:T(8,128)(2,1)S(1)}, u32[]{:S(2)}, u32[]{:S(2)}) collective-permute-start(bf16[512,128]{1,0:T(8,128)(2,1)S(1)} %add_convert_fusion.5.refs_0_), channel_id=1, source_target_pairs={{0,96},{32,64},{64,32},{96,0},{1,97},{33,65},{65,33},{97,1},{2,98}... | collective-permute-start | bytes 393224 | tf_op jit(solution)/shard_map/ppermute | solution.py:27
  73.1 7.6 %collective-permute-start.14 = (bf16[1024,128]{1,0:T(8,128)(2,1)S(1)}, bf16[1024,128]{1,0:T(8,128)(2,1)S(1)}, u32[]{:S(2)}, u32[]{:S(2)}) collective-permute-start(bf16[1024,128]{1,0:T(8,128)(2,1)S(1)} %pad_maximum_fusion), channel_id=1, source_target_pairs={{0,32},{32,0},{64,96},{96,64},{1,33},{33,1},{65,97},{97,65},{2,34}... | collective-permute-start | bytes 786440 | tf_op jit(solution)/shard_map/ppermute | solution.py:27
  84.6 12.8 %collective-permute-start.21 = (bf16[256,512]{1,0:T(8,128)(2,1)S(1)}, bf16[256,512]{1,0:T(8,128)(2,1)S(1)}, u32[]{:S(2)}, u32[]{:S(2)}) collective-permute-start(bf16[256,512]{1,0:T(8,128)(2,1)S(1)} %get-tuple-element.127), channel_id=1, source_target_pairs={{0,6},{2,0},{4,2},{6,4},{1,7},{3,1},{5,3},{7,5},{8,14},{10,8},{12,... | collective-permute-start | bytes 786440 | tf_op jit(solution)/shard_map/ppermute | solution.py:23
  85.9 11.5 %collective-permute-start.19 = (bf16[512,512]{1,0:T(8,128)(2,1)S(1)}, bf16[512,512]{1,0:T(8,128)(2,1)S(1)}, u32[]{:S(2)}, u32[]{:S(2)}) collective-permute-start(bf16[512,512]{1,0:T(8,128)(2,1)S(1)} %shard_map.109.refs_1_), channel_id=1, source_target_pairs={{0,24},{8,0},{16,8},{24,16},{1,25},{9,1},{17,9},{25,17},{2,26},{10... | collective-permute-start | bytes 1572872 | tf_op jit(solution)/shard_map/ppermute | solution.py:23
  85.9 11.5 %collective-permute-start.18 = (bf16[512,512]{1,0:T(8,128)(2,1)S(1)}, bf16[512,512]{1,0:T(8,128)(2,1)S(1)}, u32[]{:S(2)}, u32[]{:S(2)}) collective-permute-start(bf16[512,512]{1,0:T(8,128)(2,1)S(1)} %shard_map.109.refs_1_), channel_id=1, source_target_pairs={{0,8},{8,16},{16,24},{24,0},{1,9},{9,17},{17,25},{25,1},{2,10},{10... | collective-permute-start | bytes 1572872 | tf_op jit(solution)/shard_map/ppermute | solution.py:23
  87.4 10.0 %collective-permute-start.20 = (bf16[256,512]{1,0:T(8,128)(2,1)S(1)}, bf16[256,512]{1,0:T(8,128)(2,1)S(1)}, u32[]{:S(2)}, u32[]{:S(2)}) collective-permute-start(bf16[256,512]{1,0:T(8,128)(2,1)S(1)} %get-tuple-element.119), channel_id=1, source_target_pairs={{0,2},{2,4},{4,6},{6,0},{1,3},{3,5},{5,7},{7,1},{8,10},{10,12},{12... | collective-permute-start | bytes 786440 | tf_op jit(solution)/shard_map/ppermute | solution.py:23
  97.5 12.9 %collective-permute-start.22 = (bf16[512,512]{1,0:T(8,128)(2,1)S(1)}, bf16[512,512]{1,0:T(8,128)(2,1)S(1)}, u32[]{:S(2)}, u32[]{:S(2)}) collective-permute-start(bf16[512,512]{1,0:T(8,128)(2,1)S(1)} %collective-permute-done.19.refs_1_), channel_id=1, source_target_pairs={{0,24},{8,0},{16,8},{24,16},{1,25},{9,1},{17,9},{25,17},{2,26},{10... | collective-permute-start | bytes 1572872 | tf_op jit(solution)/shard_map/ppermute | solution.py:23
  97.6 8.7 %collective-permute-start.24 = (bf16[128,512]{1,0:T(8,128)(2,1)S(1)}, bf16[128,512]{1,0:T(8,128)(2,1)S(1)}, u32[]{:S(2)}, u32[]{:S(2)}) collective-permute-start(bf16[128,512]{1,0:T(8,128)(2,1)S(1)} %add_convert_fusion.3), channel_id=1, source_target_pairs={{0,6},{2,0},{4,2},{6,4},{1,7},{3,1},{5,3},{7,5},{8,14},{10,8},{12,... | collective-permute-start | bytes 393224 | tf_op jit(solution)/shard_map/ppermute | solution.py:23
  101.2 9.1 %collective-permute-start.23 = (bf16[128,512]{1,0:T(8,128)(2,1)S(1)}, bf16[128,512]{1,0:T(8,128)(2,1)S(1)}, u32[]{:S(2)}, u32[]{:S(2)}) collective-permute-start(bf16[128,512]{1,0:T(8,128)(2,1)S(1)} %add_convert_fusion.4), channel_id=1, source_target_pairs={{0,2},{2,4},{4,6},{6,0},{1,3},{3,5},{5,7},{7,1},{8,10},{10,12},{12... | collective-permute-start | bytes 393224 | tf_op jit(solution)/shard_map/ppermute | solution.py:23
  110.9 7.4 %collective-permute-start.25 = (f32[384,512]{1,0:T(8,128)S(1)}, f32[384,512]{1,0:T(8,128)S(1)}, u32[]{:S(2)}, u32[]{:S(2)}) collective-permute-start(f32[384,512]{1,0:T(8,128)S(1)} %get-tuple-element.135), channel_id=1, source_target_pairs={{0,1},{1,0},{2,3},{3,2},{4,5},{5,4},{6,7},{7,6},{8,9},{9,8},{10,11... | collective-permute-start | bytes 2359304 | tf_op jit(solution)/shard_map/ppermute | solution.py:23
  (3 other events, 3.4 us)
